TPU v7x, 512 devices: a whole 4x4x16 slice. The times are simulated.
512 devices in a mesh: row: 16 (over z), col: 16 (over y_hi, x, core), rep: 2 (over y_lo).
Axes of the slice: x: 4, y: 4 (y_hi: 2, y_lo: 2; y = y_hi * 2 + y_lo), z: 16, core: 2. Of those that a mesh axis runs over, the one named last changes fastest.
Arguments:
- pair_rep: bfloat16 [1024, 1024, 128], P(('row', 'rep'), 'col'), may hold values from -6 to 6
- token_mask: int32 [1024], replicated, may hold values 0 or 1
- w_a: bfloat16 [128, 128], replicated, may hold values from -0.5 to 0.5
- w_a_gate: bfloat16 [128, 128], replicated, may hold values from -0.5 to 0.5
- w_b: bfloat16 [128, 128], replicated, may hold values from -0.5 to 0.5
- w_b_gate: bfloat16 [128, 128], replicated, may hold values from -0.5 to 0.5
- w_gate: bfloat16 [128, 128], replicated, may hold values from -0.5 to 0.5
- w_out: bfloat16 [128, 128], replicated, may hold values from -0.5 to 0.5
Outputs:
- update: bfloat16 [1024, 1024, 128], P(('row', 'rep'), 'col')
All inputs are finite; a program needn't handle non-finite values.
Results may differ from a plain program's by a relative error of at most 0.018.
Values may be sent and summed in bfloat16 or wider, within the bound.
No kernel may reach another device: no remote copies, remote signals or barrier semaphores. Data moves between devices by JAX's collectives and lax.ppermute only.
A program may use at most 64 MiB of HBM per device.

v0:
```python
import jax
import jax.numpy as jnp
from jax import lax
from jax.sharding import PartitionSpec as P

HID = 128
STEPS = 2


EPS = 1e-05


def passed_along(value, axis, steps):
    count = lax.axis_size(axis)
    pairs = [(source, (source + steps) % count) for source in range(count)]
    return lax.ppermute(value, axis, pairs)


def from_root(x, axis, root):
    mine = lax.axis_index(axis) == root
    return lax.psum(jnp.where(mine, x, jnp.zeros_like(x)), axis)


def layer_norm(values):
    mean = jnp.mean(values, axis=-1, keepdims=True)
    centred = values - mean
    var = jnp.mean(centred * centred, axis=-1, keepdims=True)
    return centred * lax.rsqrt(var + EPS)


def gated_tile(normed, w_value, w_sig, pair):
    value = jnp.einsum("ikd,dc->cik", normed, w_value, preferred_element_type=jnp.float32)
    sig = jnp.einsum("ikd,dc->cik", normed, w_sig, preferred_element_type=jnp.float32)
    return (pair[None] * jax.nn.sigmoid(sig) * value).astype(jnp.bfloat16)


def per_device(pair_rep, token_mask, w_a, w_a_gate, w_b, w_b_gate, w_gate, w_out):
    half_rows = pair_rep.shape[0]
    tile = pair_rep.shape[1]
    rep_count = lax.axis_size("rep")
    maskf = token_mask.astype(jnp.float32)
    row_index = lax.axis_index("row")
    col_index = lax.axis_index("col")
    rep_index = lax.axis_index("rep")
    mask_cols = lax.dynamic_slice_in_dim(maskf, col_index * tile, tile, 0)
    full = lax.all_gather(pair_rep, "rep", axis=0, tiled=True)
    normed = layer_norm(full.astype(jnp.float32)).astype(jnp.bfloat16)
    mask_rows = lax.dynamic_slice_in_dim(maskf, row_index * tile, tile, 0)
    pair = mask_rows[:, None] * mask_cols[None, :]
    share = w_a.shape[1] // rep_count
    first = rep_index * share
    left = gated_tile(
        normed,
        lax.dynamic_slice_in_dim(w_a, first, share, 1),
        lax.dynamic_slice_in_dim(w_a_gate, first, share, 1),
        pair,
    )
    right = gated_tile(
        normed,
        lax.dynamic_slice_in_dim(w_b, first, share, 1),
        lax.dynamic_slice_in_dim(w_b_gate, first, share, 1),
        pair,
    )
    own_normed = lax.dynamic_slice_in_dim(normed, rep_index * half_rows, half_rows, 0)
    total = jnp.zeros((share, tile, tile), jnp.float32)
    gate = jax.nn.sigmoid(
        jnp.einsum("ijd,de->ije", own_normed, w_gate, preferred_element_type=jnp.float32)
    )
    for step in range(STEPS):
        if step > 0:
            left, right = passed_along((left, right), "col", -1)
        partner = from_root(right, "row", col_index)
        total = total + jnp.einsum(
            "cik,cjk->cij", left, partner, preferred_element_type=jnp.float32
        )
    local_hidden = total.shape[0]
    sums, squares = (
        lax.psum(jnp.sum(total, axis=0).astype(jnp.bfloat16), "rep").astype(jnp.float32),
        lax.psum(jnp.sum(total * total, axis=0).astype(jnp.bfloat16), "rep").astype(jnp.float32),
    )
    mean = sums / HID
    var = squares / HID - mean * mean
    tri_normed = ((total - mean[None]) * lax.rsqrt(var[None] + EPS)).astype(jnp.bfloat16)
    w_rows = lax.dynamic_slice_in_dim(w_out, rep_index * local_hidden, local_hidden, 0)
    partial_out = jnp.einsum("cij,cd->ijd", tri_normed, w_rows, preferred_element_type=jnp.float32)
    projected = lax.psum_scatter(
        partial_out.astype(jnp.bfloat16), "rep", scatter_dimension=0, tiled=True
    ).astype(jnp.float32)
    return (gate * projected).astype(jnp.bfloat16)


def solution(mesh):
    placed = (P(("row", "rep"), "col", None), P(), P(), P(), P(), P(), P(), P())
    return jax.shard_map(
        per_device,
        mesh=mesh,
        in_specs=placed,
        out_specs=P(("row", "rep"), "col", None),
        check_vma=False,
    )
```

profile of v0, /device:TPU:1, one launch (start us, length us, event | category | flops | bytes accessed | tf_op | source)
XLA Modules:
  0.0 273.7 jit_solution(1140331308985976053)
XLA Ops:
  6.5 0.7 all-gather.2.cloned.1.call-update
  7.3 0.7 convert_element_type.41
  8.0 0.1 fusion.36
  8.2 38.1 %all-gather.2.cloned.1.call-done = bf16[64,64,128]{2,1,0:T(8,128)(2,1)} async-done(((bf16[32,64,128]{2,1,0:T(8,128)(2,1)}), bf16[64,64,128]{2,1,0:T(8,128)(2,1)}) %all-gather.2.cloned.1.call-update) | async-done | bytes 1048592 | tf_op jit(solution)/shard_map/all_gather | solution.py:46
  46.3 1.9 convert_reduce_fusion
  48.2 2.3 fusion.2
  50.6 1.3 fusion.3
  51.9 1.2 fusion.17
  53.1 2.2 broadcast_select_fusion.1
  55.3 2.7 collective-permute-start.1
  58.1 13.5 %collective-permute-done.1 = bf16[64,64,64]{2,0,1:T(8,128)(2,1)S(1)} collective-permute-done((bf16[64,64,64]{2,0,1:T(8,128)(2,1)S(1)}, bf16[64,64,64]{2,0,1:T(8,128)(2,1)S(1)}, u32[]{:S(2)}, u32[]{:S(2)}) %collective-permute-start.1) | collective-permute-done | bytes 524320 | tf_op jit(solution)/shard_map/ppermute | solution.py:16
  71.6 1.1 broadcast_select_fusion
  72.8 1.2 fusion.20
  74.0 1.2 multiply_convert_fusion.2
  75.2 4.9 %collective-permute-start = (bf16[64,64,64]{2,0,1:T(8,128)(2,1)S(1)}, bf16[64,64,64]{2,0,1:T(8,128)(2,1)S(1)}, u32[]{:S(2)}, u32[]{:S(2)}) collective-permute-start(bf16[64,64,64]{2,0,1:T(8,128)(2,1)S(1)} %multiply_convert_fusion.2), channel_id=1, source_target_pairs={{0,30},{2,0},{4,2},{6,4},{8,6},{10,8},{12,10},{14,12},{16,14},{18,... | collective-permute-start | bytes 1572872 | tf_op jit(solution)/shard_map/ppermute | solution.py:16
  80.2 132.1 %all-reduce.4.cloned.1.call-done = (bf16[64,64,64]{2,0,1:T(8,128)(2,1)}, bf16[64,64,64]{2,0,1:T(8,128)(2,1)}) async-done(((bf16[64,64,64]{2,0,1:T(8,128)(2,1)}, bf16[64,64,64]{2,0,1:T(8,128)(2,1)}), (bf16[64,64,64]{2,0,1:T(8,128)(2,1)}, bf16[64,64,64]{2,0,1:T(8,128)(2,1)})) %all-reduce.4.cloned.1.call-update) | async-done | bytes 1048592 | tf_op jit(solution)/shard_map/psum | solution.py:21
  212.2 2.6 fusion.12
  214.9 1.0 copy-done.3
  215.9 2.8 %fusion.35 = (bf16[64,64]{1,0:T(8,128)(2,1)S(1)}, bf16[64,64]{1,0:T(8,128)(2,1)S(1)}, f32[64,64,64]{2,1,0:T(8,128)S(1)}) fusion(f32[64,64,64]{2,1,0:T(8,128)S(1)} %fusion.12, bf16[64,64,64]{2,0,1:T(8,128)(2,1)S(1)} %copy-done.2, bf16[64,64,64]{2,0,1:T(8,128)(2,1)} %copy-done.3), kind=kOutput, calls=%fused_computation.51 | convolution fusion | flops 34594816 | bytes 3162112 | tf_op jit(solution)/shard_map/cik,cjk->cij/dot_general | solution.py:73
  218.8 6.3 %all-reduce.1 = (bf16[64,64]{1,0:T(8,128)(2,1)S(1)}, bf16[64,64]{1,0:T(8,128)(2,1)S(1)}) all-reduce(bf16[64,64]{1,0:T(8,128)(2,1)S(1)} %get-tuple-element.6, bf16[64,64]{1,0:T(8,128)(2,1)S(1)} %get-tuple-element.5), channel_id=1, replica_groups=mesh['row'=16,'col'=16,'rep'=2] {'rep'}, use_global_device_ids=true, to_apply=%region_7.8 | all-reduce | flops 8192 | bytes 32768 | tf_op jit(solution)/shard_map/psum | solution.py:79
  225.1 0.3 multiply_convert_fusion
  225.4 2.0 convolution_convert_fusion
  227.4 37.4 %reduce-scatter.2.cloned.1.call-done = bf16[32,64,128]{2,1,0:T(8,128)(2,1)} async-done(((bf16[64,64,128]{2,1,0:T(8,128)(2,1)}), bf16[32,64,128]{2,1,0:T(8,128)(2,1)}) %reduce-scatter.2.cloned.1.call-update) | async-done | bytes 524304 | tf_op jit(solution)/shard_map/reduce_scatter | solution.py:86
  264.9 2.3 fusion.8
  (27 shorter events, 0.3 us)
Async XLA Ops:
  6.5 46.6 %copy-start = (bf16[128,128]{1,0:T(8,128)(2,1)S(1)}, bf16[128,128]{1,0:T(8,128)(2,1)}, u32[]{:S(2)}) copy-start(bf16[128,128]{1,0:T(8,128)(2,1)} %param.12) | copy-start | bytes 98308
  6.5 39.8 %all-gather.2.cloned.1.call-start = ((), (), s32[]{:S(2)}) async-start(), calls=%async_computation.1 | async-start | bytes 1572864 | tf_op jit(solution)/shard_map/all_gather | solution.py:46
  7.3 205.0 %all-reduce.4.cloned.1.call-start = ((), (), s32[]{:S(2)}) async-start(), calls=%async_computation.3 | async-start | bytes 4194304 | tf_op jit(solution)/shard_map/psum | solution.py:21
  8.2 43.7 %copy-start.4 = (bf16[128,128]{1,0:T(8,128)(2,1)S(1)}, bf16[128,128]{1,0:T(8,128)(2,1)}, u32[]{:S(2)}) copy-start(bf16[128,128]{1,0:T(8,128)(2,1)} %param.13) | copy-start | bytes 98308
  46.3 4.3 %copy-start.1 = (bf16[64,64,128]{2,1,0:T(8,128)(2,1)S(1)}, bf16[64,64,128]{2,1,0:T(8,128)(2,1)}, u32[]{:S(2)}) copy-start(bf16[64,64,128]{2,1,0:T(8,128)(2,1)} %all-gather.2.cloned.1.call-done) | copy-start | bytes 3145732
  55.3 17.4 %copy-start.5 = (bf16[128,128]{1,0:T(8,128)(2,1)S(1)}, bf16[128,128]{1,0:T(8,128)(2,1)}, u32[]{:S(2)}) copy-start(bf16[128,128]{1,0:T(8,128)(2,1)} %param.11) | copy-start | bytes 98308
  55.3 16.3 %collective-permute-start.1 = (bf16[64,64,64]{2,0,1:T(8,128)(2,1)S(1)}, bf16[64,64,64]{2,0,1:T(8,128)(2,1)S(1)}, u32[]{:S(2)}, u32[]{:S(2)}) collective-permute-start(bf16[64,64,64]{2,0,1:T(8,128)(2,1)S(1)} %get-tuple-element.16), channel_id=1, source_target_pairs={{0,30},{2,0},{4,2},{6,4},{8,6},{10,8},{12,10},{14,12},{16,14},{18,... | collective-permute-start | bytes 1572872 | tf_op jit(solution)/shard_map/ppermute | solution.py:16
  72.7 1.3 copy-start.7
  72.7 192.2 %reduce-scatter.2.cloned.1.call-start = ((), (), s32[]{:S(2)}) async-start(), calls=%async_computation.2 | async-start | bytes 1572864 | tf_op jit(solution)/shard_map/reduce_scatter | solution.py:86
  75.2 139.7 %collective-permute-start = (bf16[64,64,64]{2,0,1:T(8,128)(2,1)S(1)}, bf16[64,64,64]{2,0,1:T(8,128)(2,1)S(1)}, u32[]{:S(2)}, u32[]{:S(2)}) collective-permute-start(bf16[64,64,64]{2,0,1:T(8,128)(2,1)S(1)} %multiply_convert_fusion.2), channel_id=1, source_target_pairs={{0,30},{2,0},{4,2},{6,4},{8,6},{10,8},{12,10},{14,12},{16,14},{18,... | collective-permute-start | bytes 1572872 | tf_op jit(solution)/shard_map/ppermute | solution.py:16
  212.2 3.7 %copy-start.2 = (bf16[64,64,64]{2,0,1:T(8,128)(2,1)S(1)}, bf16[64,64,64]{2,0,1:T(8,128)(2,1)}, u32[]{:S(2)}) copy-start(bf16[64,64,64]{2,0,1:T(8,128)(2,1)} %get-tuple-element.8) | copy-start | bytes 1572868
  214.9 1.0 copy-start.3
  218.7 6.7 %copy-start.6 = (bf16[128,128]{1,0:T(8,128)(2,1)S(1)}, bf16[128,128]{1,0:T(8,128)(2,1)}, u32[]{:S(2)}) copy-start(bf16[128,128]{1,0:T(8,128)(2,1)} %param.15) | copy-start | bytes 98308
  225.4 39.4 %copy-start.8 = (bf16[128,128]{1,0:T(8,128)(2,1)S(1)}, bf16[128,128]{1,0:T(8,128)(2,1)}, u32[]{:S(2)}) copy-start(bf16[128,128]{1,0:T(8,128)(2,1)} %param.14) | copy-start | bytes 98308
Sparse Core Ops, SparseCore 0:
  9.4 36.8 all-gather.1
  72.8 139.3 all-reduce.3
  227.5 37.2 reduce-scatter.1
where the time goes:
time: 274 us
  waiting for transfers between devices  222 us (81%)
  matrix products  15.5 us (6%)
  between operations  13.3 us (5%)
  starting transfers between devices  7.73 us (3%)
  other arithmetic  7.7 us (3%)
  blocking collectives  6.31 us (2%)
    psum x1, waiting for transfers between devices, from_root(): return lax.psum(jnp.where(mine, x, jnp.zeros_like(x)), axis)  132 us
    all_gather x1, waiting for transfers between devices, per_device(): full = lax.all_gather(pair_rep, 'rep', axis=0, tiled=True)  38.1 us
    reduce_scatter x1, waiting for transfers between devices, per_device(): lax.psum_scatter(partial_out.astype(jnp.bfloat16), 'rep', scatter_dimensi...  37.4 us
    ppermute x2, waiting for transfers between devices, passed_along(): return lax.ppermute(value, axis, pairs)  13.5 us
    ppermute x2, starting transfers between devices, passed_along(): return lax.ppermute(value, axis, pairs)  7.65 us
    psum x1, blocking collectives, per_device(): lax.psum(jnp.sum(total * total, axis=0).astype(jnp.bfloat16), 'rep')  6.31 us
  transfers between devices with their start and end apart: 5, of which 4 were waited for; matrix products, arithmetic and copies ran while one was open for 2% of the time, Pallas kernels for 0%

commit v1 on v0

v1 whole, which is shorter than its diff:
```python
import jax
import jax.numpy as jnp
from jax import lax
from jax.sharding import PartitionSpec as P

HID = 128
EPS = 1e-05


def layer_norm(values):
    mean = jnp.mean(values, axis=-1, keepdims=True)
    centred = values - mean
    var = jnp.mean(centred * centred, axis=-1, keepdims=True)
    return centred * lax.rsqrt(var + EPS)


def project(values, weights):
    return jnp.dot(values, weights, preferred_element_type=jnp.float32)


def gated(normed, w_value, w_sig, pair):
    return (pair * jax.nn.sigmoid(project(normed, w_sig)) * project(normed, w_value)).astype(jnp.bfloat16)


def tri_projected(left, right, w_out):
    tri = jnp.einsum("ikc,jkc->ijc", left, right, preferred_element_type=jnp.float32)
    mean = jnp.mean(tri, axis=-1, keepdims=True)
    var = jnp.mean(tri * tri, axis=-1, keepdims=True) - mean * mean
    normed = ((tri - mean) * lax.rsqrt(var + EPS)).astype(jnp.bfloat16)
    return project(normed, w_out)


def per_device(pair_rep, token_mask, w_a, w_a_gate, w_b, w_b_gate, w_gate, w_out):
    half, tile, chans = pair_rep.shape
    rows, cols, reps = lax.axis_size("row"), lax.axis_size("col"), lax.axis_size("rep")
    row, col, rep = lax.axis_index("row"), lax.axis_index("col"), lax.axis_index("rep")
    maskf = token_mask.astype(jnp.float32)
    mask_i = lax.dynamic_slice_in_dim(maskf, row * tile + rep * half, half, 0)
    mask_k = lax.dynamic_slice_in_dim(maskf, col * tile, tile, 0)
    pair = (mask_i[:, None] * mask_k[None, :]).reshape(-1, 1)
    normed = layer_norm(pair_rep.astype(jnp.float32)).astype(jnp.bfloat16).reshape(-1, chans)

    right = gated(normed, w_b, w_b_gate, pair)
    sends = rows // 2
    kept = right.shape[0] // rows * (rows - 1)
    piece = kept // sends
    rest = right[kept:]
    mine = None
    for s in range(sends):
        pairs = [(c * cols + c, 2 * s * cols + c) for c in range(cols)]
        pairs += [(c * cols + (c + 1) % cols, (2 * s + 1) * cols + c) for c in range(cols)]
        message = jnp.concatenate([right[s * piece : (s + 1) * piece], rest])
        got = lax.ppermute(message, ("row", "col"), pairs)
        mine = got if mine is None else mine + got

    left = gated(normed, w_a, w_a_gate, pair)
    swap = [(p, 1 - p) for p in range(reps)]
    back = [(c, (c - 1) % cols) for c in range(cols)]
    left_next = lax.ppermute(left, "col", back)
    other = lax.ppermute(left, "rep", swap)
    other_next = lax.ppermute(left_next, "rep", swap)

    rest_mine = mine[piece:]
    rest_other = lax.ppermute(rest_mine, "row", [(r, r ^ 1) for r in range(rows)])
    gathered = lax.all_gather(mine[:piece], "row", axis=0, tiled=True)
    gathered = gathered.reshape(sends, 2, piece, chans)
    even = row % 2 == 0
    rests = (jnp.where(even, rest_mine, rest_other), jnp.where(even, rest_other, rest_mine))
    right_all = jnp.concatenate(
        [
            jnp.concatenate([gathered[:, t].reshape(-1, chans), rests[t]]).reshape(half, tile, chans)
            for t in range(2)
        ],
        axis=1,
    )

    def both(first, second):
        return jnp.concatenate([first.reshape(half, tile, chans), second.reshape(half, tile, chans)], axis=1)

    theirs = tri_projected(both(other, other_next), right_all, w_out).astype(jnp.bfloat16)
    received = lax.ppermute(theirs, "rep", swap)
    ours = tri_projected(both(left, left_next), right_all, w_out)
    gate = jax.nn.sigmoid(project(normed, w_gate)).reshape(half, tile, chans)
    ours, received = ours.reshape(half, half, chans), received.reshape(half, half, chans).astype(jnp.float32)
    first = rep == 0
    projected = jnp.concatenate([jnp.where(first, ours, received), jnp.where(first, received, ours)], axis=1)
    return (gate * projected).astype(jnp.bfloat16)


def solution(mesh):
    placed = (P(("row", "rep"), "col", None), P(), P(), P(), P(), P(), P(), P())
    return jax.shard_map(
        per_device,
        mesh=mesh,
        in_specs=placed,
        out_specs=P(("row", "rep"), "col", None),
        check_vma=False,
    )
```

time: 274 us -> 123 us (0.45)
  the two profiles are of different devices: /device:TPU:1 before, /device:TPU:8 now
where the time goes in v1:
time: 123 us; the launch traced here: 122 us
  starting transfers between devices  38.7 us (31%)
  blocking collectives  35.5 us (29%)
  local copies, waits for them, and re-layouts  19.7 us (16%)
  matrix products  11.9 us (10%)
  other arithmetic  8.05 us (7%)
  waiting for transfers between devices  7.47 us (6%)
    all_gather x1, blocking collectives, per_device(): gathered = lax.all_gather(mine[:piece], 'row', axis=0, tiled=True)  35.5 us
    ppermute x8, starting transfers between devices, per_device(): got = lax.ppermute(message, ('row', 'col'), pairs)  22.3 us
    dot_general x2, matrix products, tri_projected(): jnp.einsum('ikc,jkc->ijc', left, right, preferred_element_type=jnp.float32)  6.74 us
    reshape x2, local copies, waits for them, and re-layouts, both(): second.reshape(half, tile, chans)  6.73 us
    reshape x2, local copies, waits for them, and re-layouts, both(): first.reshape(half, tile, chans)  5.79 us
    ppermute x1, starting transfers between devices, per_device(): left_next = lax.ppermute(left, 'col', back)  5.25 us
    dot_general x7, matrix products, project(): return jnp.dot(values, weights, preferred_element_type=jnp.float32)  5.18 us
    reshape x2, local copies, waits for them, and re-layouts, per_device(): jnp.concatenate([gathered[:, t].reshape(-1, chans), rests[t]])  4.08 us
  transfers between devices with their start and end apart: 13, of which 2 were waited for; matrix products, arithmetic and copies ran while one was open for 19% of the time, Pallas kernels for 0%

profile of v1, /device:TPU:8, one launch (start us, length us, event | category | flops | bytes accessed | tf_op | source)
XLA Modules:
  0.0 121.7 jit_solution(16395424192713836175)
XLA Ops:
  1.0 1.4 %convert_reduce_fusion = f32[32,64]{1,0:T(8,128)S(1)} fusion(bf16[32,64,128]{2,1,0:T(8,128)(2,1)} %param.8), kind=kLoop, calls=%fused_computation.31 | loop fusion | flops 522240 | bytes 532480 | tf_op jit(solution)/shard_map/reduce_sum | solution.py:11
  2.4 1.7 %fusion.21 = f32[32,64]{1,0:T(8,128)S(1)} fusion(bf16[32,64,128]{2,1,0:T(8,128)(2,1)} %param.8, f32[32,64]{1,0:T(8,128)S(1)} %broadcast_multiply_fusion.3), kind=kLoop, calls=%fused_computation.35 | loop fusion | flops 1046528 | bytes 540672 | tf_op jit(solution)/shard_map/reduce_sum | solution.py:13
  4.1 1.6 %fusion.22 = bf16[32,64,128]{2,1,0:T(8,128)(2,1)S(1)} fusion(bf16[32,64,128]{2,1,0:T(8,128)(2,1)} %param.8, f32[32,64]{1,0:T(8,128)S(1)} %add_rsqrt_fusion.2, f32[32,64]{1,0:T(8,128)S(1)} %broadcast_multiply_fusion.3), kind=kLoop, calls=%fused_computation.36 | loop fusion | flops 1048576 | bytes 1064960 | tf_op jit(solution)/shard_map/convert_element_type | solution.py:41
  7.6 5.2 %collective-permute-start.1 = (bf16[368,128]{1,0:T(8,128)(2,1)S(1)}, bf16[368,128]{1,0:T(8,128)(2,1)S(1)}, u32[]{:S(2)}, u32[]{:S(2)}) collective-permute-start(bf16[368,128]{1,0:T(8,128)(2,1)S(1)} %get-tuple-element.22), channel_id=1, source_target_pairs={{0,64},{34,66},{68,68},{102,70},{136,72},{170,74},{204,76},{238,78... | collective-permute-start | bytes 282632 | tf_op jit(solution)/shard_map/ppermute | solution.py:53
  12.8 4.6 %collective-permute-start.2 = (bf16[368,128]{1,0:T(8,128)(2,1)S(1)}, bf16[368,128]{1,0:T(8,128)(2,1)S(1)}, u32[]{:S(2)}, u32[]{:S(2)}) collective-permute-start(bf16[368,128]{1,0:T(8,128)(2,1)S(1)} %get-tuple-element.23), channel_id=1, source_target_pairs={{0,128},{34,130},{68,132},{102,134},{136,136},{170,138},{204,140},... | collective-permute-start | bytes 282632 | tf_op jit(solution)/shard_map/ppermute | solution.py:53
  17.4 3.4 %collective-permute-start.3 = (bf16[368,128]{1,0:T(8,128)(2,1)S(1)}, bf16[368,128]{1,0:T(8,128)(2,1)S(1)}, u32[]{:S(2)}, u32[]{:S(2)}) collective-permute-start(bf16[368,128]{1,0:T(8,128)(2,1)S(1)} %get-tuple-element.24), channel_id=1, source_target_pairs={{0,192},{34,194},{68,196},{102,198},{136,200},{170,202},{204,204},... | collective-permute-start | bytes 282632 | tf_op jit(solution)/shard_map/ppermute | solution.py:53
  20.8 4.6 %collective-permute-start.4 = (bf16[368,128]{1,0:T(8,128)(2,1)S(1)}, bf16[368,128]{1,0:T(8,128)(2,1)S(1)}, u32[]{:S(2)}, u32[]{:S(2)}) collective-permute-start(bf16[368,128]{1,0:T(8,128)(2,1)S(1)} %get-tuple-element.25), channel_id=1, source_target_pairs={{0,256},{34,258},{68,260},{102,262},{136,264},{170,266},{204,268},... | collective-permute-start | bytes 282632 | tf_op jit(solution)/shard_map/ppermute | solution.py:53
  31.1 1.4 %fusion.10 = f32[2048,128]{1,0:T(8,128)} fusion(bf16[2048,128]{1,0:T(8,128)(2,1)S(1)} %bitcast.54, bf16[128,128]{1,0:T(8,128)(2,1)S(1)} %copy-done.8), kind=kOutput, calls=%fused_computation.15 | convolution fusion | flops 67895296 | bytes 1605632 | tf_op jit(solution)/shard_map/dot_general | solution.py:18
  32.5 2.5 %copy.21 = bf16[32,64,128]{1,0,2:T(8,128)(2,1)S(1)} copy(bf16[32,64,128]{2,1,0:T(8,128)(2,1)} %bitcast.7) | data formatting | bytes 1048576 | tf_op jit(solution)/shard_map/reshape | solution.py:78
  35.0 5.3 %collective-permute-start.9 = (bf16[2048,128]{1,0:T(8,128)(2,1)}, bf16[2048,128]{1,0:T(8,128)(2,1)}, u32[]{:S(2)}, u32[]{:S(2)}) collective-permute-start(bf16[2048,128]{1,0:T(8,128)(2,1)} %fusion.12), channel_id=1, source_target_pairs={{0,30},{2,0},{4,2},{6,4},{8,6},{10,8},{12,10},{14,12},{16,14},{18,... | collective-permute-start | bytes 1572872 | tf_op jit(solution)/shard_map/ppermute | solution.py:59
  40.3 3.3 %collective-permute-start.10 = (bf16[2048,128]{1,0:T(8,128)(2,1)}, bf16[2048,128]{1,0:T(8,128)(2,1)}, u32[]{:S(2)}, u32[]{:S(2)}) collective-permute-start(bf16[2048,128]{1,0:T(8,128)(2,1)} %fusion.12), channel_id=1, source_target_pairs={{0,1},{1,0},{2,3},{3,2},{4,5},{5,4},{6,7},{7,6},{8,9},{9,8},{10,11... | collective-permute-start | bytes 1572872 | tf_op jit(solution)/shard_map/ppermute | solution.py:60
  43.6 35.5 %all_gather.3 = bf16[3840,128]{1,0:T(8,128)(2,1)S(1)} all-gather(bf16[240,128]{1,0:T(8,128)(2,1)S(1)} %slice.58), channel_id=1, replica_groups=mesh['row'=16,'col'=16,'rep'=2] {'row'}, dimensions={0}, use_global_device_ids=true | all-gather | bytes 1044480 | tf_op jit(solution)/shard_map/all_gather | solution.py:65
  79.1 1.9 %collective-permute-start.8 = (bf16[128,128]{1,0:T(8,128)(2,1)S(1)}, bf16[128,128]{1,0:T(8,128)(2,1)S(1)}, u32[]{:S(2)}, u32[]{:S(2)}) collective-permute-start(bf16[128,128]{1,0:T(8,128)(2,1)S(1)} %slice.60), channel_id=1, source_target_pairs={{0,32},{32,0},{64,96},{96,64},{128,160},{160,128},{192,224},{224,1... | collective-permute-start | bytes 98312 | tf_op jit(solution)/shard_map/ppermute | solution.py:64
  81.1 3.8 %collective-permute-done.8 = bf16[128,128]{1,0:T(8,128)(2,1)S(1)} collective-permute-done((bf16[128,128]{1,0:T(8,128)(2,1)S(1)}, bf16[128,128]{1,0:T(8,128)(2,1)S(1)}, u32[]{:S(2)}, u32[]{:S(2)}) %collective-permute-start.8) | collective-permute-done | bytes 32800 | tf_op jit(solution)/shard_map/ppermute | solution.py:64
  84.9 2.8 %collective-permute-start.11 = (bf16[2048,128]{1,0:T(8,128)(2,1)}, bf16[2048,128]{1,0:T(8,128)(2,1)}, u32[]{:S(2)}, u32[]{:S(2)}) collective-permute-start(bf16[2048,128]{1,0:T(8,128)(2,1)} %collective-permute-done.9), channel_id=1, source_target_pairs={{0,1},{1,0},{2,3},{3,2},{4,5},{5,4},{6,7},{7,6},{8,9},{9,8},{10,11... | collective-permute-start | bytes 1572872 | tf_op jit(solution)/shard_map/ppermute | solution.py:61
  88.6 1.6 %copy.19 = bf16[32,64,128]{1,0,2:T(8,128)(2,1)S(1)} copy(bf16[32,64,128]{2,1,0:T(8,128)(2,1)S(1)} %bitcast.57) | data formatting | bytes 1048576 | tf_op jit(solution)/shard_map/reshape | solution.py:71
  90.2 2.5 %copy.20 = bf16[32,64,128]{1,0,2:T(8,128)(2,1)S(1)} copy(bf16[32,64,128]{2,1,0:T(8,128)(2,1)} %bitcast.56) | data formatting | bytes 1048576 | tf_op jit(solution)/shard_map/reshape | solution.py:71
  92.7 3.3 %copy.22 = bf16[32,64,128]{1,0,2:T(8,128)(2,1)} copy(bf16[32,64,128]{2,1,0:T(8,128)(2,1)} %bitcast.8) | data formatting | bytes 1048576 | tf_op jit(solution)/shard_map/reshape | solution.py:78
  96.0 3.3 %copy.24 = bf16[32,64,128]{1,0,2:T(8,128)(2,1)} copy(bf16[32,64,128]{2,1,0:T(8,128)(2,1)} %bitcast.11) | data formatting | bytes 1048576 | tf_op jit(solution)/shard_map/reshape | solution.py:78
  99.3 4.0 %bitcast_reduce_fusion.1 = (f32[32,32]{0,1:T(8,128)S(1)}, f32[32,32]{0,1:T(8,128)S(1)}, f32[128,32,32]{2,1,0:T(8,128)}) fusion(bf16[32,64,128]{1,0,2:T(8,128)(2,1)} %copy.22, bf16[32,64,128]{1,0,2:T(8,128)(2,1)S(1)} %copy.21, bf16[32,64,128]{1,0,2:T(8,128)(2,1)S(1)} %copy.20, bf16[32,64,128]{1,0,2:T(8,128)(2,1)S(1)} %copy.19), kind=kOutput, calls=%fused_computation.26 | convolution fusion | flops 38139904 | bytes 2629632 | tf_op jit(solution)/shard_map/ikc,jkc->ijc/dot_general | solution.py:26
  103.4 3.4 %copy.25 = bf16[32,64,128]{1,0,2:T(8,128)(2,1)} copy(bf16[32,64,128]{2,1,0:T(8,128)(2,1)} %bitcast.12) | data formatting | bytes 1048576 | tf_op jit(solution)/shard_map/reshape | solution.py:78
  106.8 2.7 %bitcast_reduce_fusion = (f32[32,32]{0,1:T(8,128)S(1)}, f32[32,32]{0,1:T(8,128)S(1)}, f32[128,32,32]{2,1,0:T(8,128)S(1)}) fusion(bf16[32,64,128]{1,0,2:T(8,128)(2,1)} %copy.25, bf16[32,64,128]{1,0,2:T(8,128)(2,1)S(1)} %copy-done.2, bf16[32,64,128]{1,0,2:T(8,128)(2,1)S(1)} %copy.20, bf16[32,64,128]{1,0,2:T(8,128)(2,1)S(1)} %copy.19), kind=kOutput, calls=%fused_computation.20 | convolution fusion | flops 38139904 | bytes 2629632 | tf_op jit(solution)/shard_map/ikc,jkc->ijc/dot_general | solution.py:26
  112.1 3.2 %collective-permute-start.12 = (bf16[32,32,128]{2,1,0:T(8,128)(2,1)}, bf16[32,32,128]{2,1,0:T(8,128)(2,1)S(1)}, u32[]{:S(2)}, u32[]{:S(2)}) collective-permute-start(bf16[32,32,128]{2,1,0:T(8,128)(2,1)} %convolution_convert_fusion), channel_id=1, source_target_pairs={{0,1},{1,0},{2,3},{3,2},{4,5},{5,4},{6,7},{7,6},{8,9},{9,8},{10,11... | collective-permute-start | bytes 786440 | tf_op jit(solution)/shard_map/ppermute | solution.py:81
  116.9 3.6 %collective-permute-done.12 = bf16[32,32,128]{2,1,0:T(8,128)(2,1)S(1)} collective-permute-done((bf16[32,32,128]{2,1,0:T(8,128)(2,1)}, bf16[32,32,128]{2,1,0:T(8,128)(2,1)S(1)}, u32[]{:S(2)}, u32[]{:S(2)}) %collective-permute-start.12) | collective-permute-done | bytes 262176 | tf_op jit(solution)/shard_map/ppermute | solution.py:81
  (63 shorter events, 14.8 us)
Async XLA Ops:
  0.0 111.1 %copy-start = (bf16[128,128]{1,0:T(8,128)(2,1)S(1)}, bf16[128,128]{1,0:T(8,128)(2,1)}, u32[]{:S(2)}) copy-start(bf16[128,128]{1,0:T(8,128)(2,1)} %param.15) | copy-start | bytes 98308
  0.0 5.8 %copy-start.6 = (bf16[128,128]{1,0:T(8,128)(2,1)S(1)}, bf16[128,128]{1,0:T(8,128)(2,1)}, u32[]{:S(2)}) copy-start(bf16[128,128]{1,0:T(8,128)(2,1)} %param.13) | copy-start | bytes 98308
  5.8 0.8 copy-start.4
  6.5 18.9 %copy-start.7 = (bf16[128,128]{1,0:T(8,128)(2,1)S(1)}, bf16[128,128]{1,0:T(8,128)(2,1)}, u32[]{:S(2)}) copy-start(bf16[128,128]{1,0:T(8,128)(2,1)} %param.11) | copy-start | bytes 98308
  7.0 20.2 %collective-permute-start = (bf16[368,128]{1,0:T(8,128)(2,1)S(1)}, bf16[368,128]{1,0:T(8,128)(2,1)S(1)}, u32[]{:S(2)}, u32[]{:S(2)}) collective-permute-start(bf16[368,128]{1,0:T(8,128)(2,1)S(1)} %get-tuple-element.28), channel_id=1, source_target_pairs={{0,0},{34,2},{68,4},{102,6},{136,8},{170,10},{204,12},{238,14},{27... | collective-permute-start | bytes 282632 | tf_op jit(solution)/shard_map/ppermute | solution.py:53
  7.6 20.9 %collective-permute-start.1 = (bf16[368,128]{1,0:T(8,128)(2,1)S(1)}, bf16[368,128]{1,0:T(8,128)(2,1)S(1)}, u32[]{:S(2)}, u32[]{:S(2)}) collective-permute-start(bf16[368,128]{1,0:T(8,128)(2,1)S(1)} %get-tuple-element.22), channel_id=1, source_target_pairs={{0,64},{34,66},{68,68},{102,70},{136,72},{170,74},{204,76},{238,78... | collective-permute-start | bytes 282632 | tf_op jit(solution)/shard_map/ppermute | solution.py:53
  12.8 17.0 %collective-permute-start.2 = (bf16[368,128]{1,0:T(8,128)(2,1)S(1)}, bf16[368,128]{1,0:T(8,128)(2,1)S(1)}, u32[]{:S(2)}, u32[]{:S(2)}) collective-permute-start(bf16[368,128]{1,0:T(8,128)(2,1)S(1)} %get-tuple-element.23), channel_id=1, source_target_pairs={{0,128},{34,130},{68,132},{102,134},{136,136},{170,138},{204,140},... | collective-permute-start | bytes 282632 | tf_op jit(solution)/shard_map/ppermute | solution.py:53
  17.4 17.6 %collective-permute-start.3 = (bf16[368,128]{1,0:T(8,128)(2,1)S(1)}, bf16[368,128]{1,0:T(8,128)(2,1)S(1)}, u32[]{:S(2)}, u32[]{:S(2)}) collective-permute-start(bf16[368,128]{1,0:T(8,128)(2,1)S(1)} %get-tuple-element.24), channel_id=1, source_target_pairs={{0,192},{34,194},{68,196},{102,198},{136,200},{170,202},{204,204},... | collective-permute-start | bytes 282632 | tf_op jit(solution)/shard_map/ppermute | solution.py:53
  20.8 5.3 %copy-start.5 = (bf16[128,128]{1,0:T(8,128)(2,1)S(1)}, bf16[128,128]{1,0:T(8,128)(2,1)}, u32[]{:S(2)}) copy-start(bf16[128,128]{1,0:T(8,128)(2,1)} %param.10) | copy-start | bytes 98308
  20.8 19.4 %collective-permute-start.4 = (bf16[368,128]{1,0:T(8,128)(2,1)S(1)}, bf16[368,128]{1,0:T(8,128)(2,1)S(1)}, u32[]{:S(2)}, u32[]{:S(2)}) collective-permute-start(bf16[368,128]{1,0:T(8,128)(2,1)S(1)} %get-tuple-element.25), channel_id=1, source_target_pairs={{0,256},{34,258},{68,260},{102,262},{136,264},{170,266},{204,268},... | collective-permute-start | bytes 282632 | tf_op jit(solution)/shard_map/ppermute | solution.py:53
  26.1 5.0 %copy-start.8 = (bf16[128,128]{1,0:T(8,128)(2,1)S(1)}, bf16[128,128]{1,0:T(8,128)(2,1)}, u32[]{:S(2)}) copy-start(bf16[128,128]{1,0:T(8,128)(2,1)} %param.14) | copy-start | bytes 98308
  27.2 16.3 %collective-permute-start.5 = (bf16[368,128]{1,0:T(8,128)(2,1)S(1)}, bf16[368,128]{1,0:T(8,128)(2,1)S(1)}, u32[]{:S(2)}, u32[]{:S(2)}) collective-permute-start(bf16[368,128]{1,0:T(8,128)(2,1)S(1)} %get-tuple-element.26), channel_id=1, source_target_pairs={{0,320},{34,322},{68,324},{102,326},{136,328},{170,330},{204,332},... | collective-permute-start | bytes 282632 | tf_op jit(solution)/shard_map/ppermute | solution.py:53
  28.5 15.0 %collective-permute-start.6 = (bf16[368,128]{1,0:T(8,128)(2,1)S(1)}, bf16[368,128]{1,0:T(8,128)(2,1)S(1)}, u32[]{:S(2)}, u32[]{:S(2)}) collective-permute-start(bf16[368,128]{1,0:T(8,128)(2,1)S(1)} %get-tuple-element.27), channel_id=1, source_target_pairs={{0,384},{34,386},{68,388},{102,390},{136,392},{170,394},{204,396},... | collective-permute-start | bytes 282632 | tf_op jit(solution)/shard_map/ppermute | solution.py:53
  29.8 13.7 %collective-permute-start.7 = (bf16[368,128]{1,0:T(8,128)(2,1)S(1)}, bf16[368,128]{1,0:T(8,128)(2,1)S(1)}, u32[]{:S(2)}, u32[]{:S(2)}) collective-permute-start(bf16[368,128]{1,0:T(8,128)(2,1)S(1)} %concatenate.56), channel_id=1, source_target_pairs={{0,448},{34,450},{68,452},{102,454},{136,456},{170,458},{204,460},... | collective-permute-start | bytes 282632 | tf_op jit(solution)/shard_map/ppermute | solution.py:53
  35.0 49.9 %collective-permute-start.9 = (bf16[2048,128]{1,0:T(8,128)(2,1)}, bf16[2048,128]{1,0:T(8,128)(2,1)}, u32[]{:S(2)}, u32[]{:S(2)}) collective-permute-start(bf16[2048,128]{1,0:T(8,128)(2,1)} %fusion.12), channel_id=1, source_target_pairs={{0,30},{2,0},{4,2},{6,4},{8,6},{10,8},{12,10},{14,12},{16,14},{18,... | collective-permute-start | bytes 1572872 | tf_op jit(solution)/shard_map/ppermute | solution.py:59
  40.3 55.7 %collective-permute-start.10 = (bf16[2048,128]{1,0:T(8,128)(2,1)}, bf16[2048,128]{1,0:T(8,128)(2,1)}, u32[]{:S(2)}, u32[]{:S(2)}) collective-permute-start(bf16[2048,128]{1,0:T(8,128)(2,1)} %fusion.12), channel_id=1, source_target_pairs={{0,1},{1,0},{2,3},{3,2},{4,5},{5,4},{6,7},{7,6},{8,9},{9,8},{10,11... | collective-permute-start | bytes 1572872 | tf_op jit(solution)/shard_map/ppermute | solution.py:60
  79.1 5.8 %collective-permute-start.8 = (bf16[128,128]{1,0:T(8,128)(2,1)S(1)}, bf16[128,128]{1,0:T(8,128)(2,1)S(1)}, u32[]{:S(2)}, u32[]{:S(2)}) collective-permute-start(bf16[128,128]{1,0:T(8,128)(2,1)S(1)} %slice.60), channel_id=1, source_target_pairs={{0,32},{32,0},{64,96},{96,64},{128,160},{160,128},{192,224},{224,1... | collective-permute-start | bytes 98312 | tf_op jit(solution)/shard_map/ppermute | solution.py:64
  84.9 18.5 %collective-permute-start.11 = (bf16[2048,128]{1,0:T(8,128)(2,1)}, bf16[2048,128]{1,0:T(8,128)(2,1)}, u32[]{:S(2)}, u32[]{:S(2)}) collective-permute-start(bf16[2048,128]{1,0:T(8,128)(2,1)} %collective-permute-done.9), channel_id=1, source_target_pairs={{0,1},{1,0},{2,3},{3,2},{4,5},{5,4},{6,7},{7,6},{8,9},{9,8},{10,11... | collective-permute-start | bytes 1572872 | tf_op jit(solution)/shard_map/ppermute | solution.py:61
  103.4 3.4 %copy-start.2 = (bf16[32,64,128]{1,0,2:T(8,128)(2,1)S(1)}, bf16[32,64,128]{1,0,2:T(8,128)(2,1)}, u32[]{:S(2)}) copy-start(bf16[32,64,128]{1,0,2:T(8,128)(2,1)} %copy.24) | copy-start | bytes 1572868
  109.5 5.8 %copy-start.1 = (f32[128,32,32]{2,1,0:T(8,128)S(1)}, f32[128,32,32]{2,1,0:T(8,128)}, u32[]{:S(2)}) copy-start(f32[128,32,32]{2,1,0:T(8,128)} %get-tuple-element.33) | copy-start | bytes 1572868
  112.1 8.5 %collective-permute-start.12 = (bf16[32,32,128]{2,1,0:T(8,128)(2,1)}, bf16[32,32,128]{2,1,0:T(8,128)(2,1)S(1)}, u32[]{:S(2)}, u32[]{:S(2)}) collective-permute-start(bf16[32,32,128]{2,1,0:T(8,128)(2,1)} %convolution_convert_fusion), channel_id=1, source_target_pairs={{0,1},{1,0},{2,3},{3,2},{4,5},{5,4},{6,7},{7,6},{8,9},{9,8},{10,11... | collective-permute-start | bytes 786440 | tf_op jit(solution)/shard_map/ppermute | solution.py:81
  115.6 5.2 %copy-start.3 = (f32[2048,128]{1,0:T(8,128)S(1)}, f32[2048,128]{1,0:T(8,128)}, u32[]{:S(2)}) copy-start(f32[2048,128]{1,0:T(8,128)} %fusion.10) | copy-start | bytes 3145732

commit v2 on v1

v2 whole, which is shorter than its diff:
```python
import functools
import jax
import jax.numpy as jnp
from jax import lax
from jax.experimental import pallas as pl
from jax.experimental.pallas import tpu as pltpu
from jax.sharding import PartitionSpec as P

EPS = 1e-5
VMEM = pl.BlockSpec(memory_space=pltpu.VMEM)
SMEM = pl.BlockSpec(memory_space=pltpu.SMEM)
F32 = jnp.float32
BF16 = jnp.bfloat16

def row_sums(values, ones):
    return lax.dot_general(values, ones, (((1,), (0,)), ((), ())), preferred_element_type=F32)

def normalise(block, ones):
    chans = block.shape[1]
    centred = block.astype(F32) - row_sums(block, ones) * (1.0 / chans)
    squares = centred * centred
    high = squares.astype(BF16)
    low = (squares - high.astype(F32)).astype(BF16)
    var = (row_sums(high, ones) + row_sums(low, ones)) * (1.0 / chans)
    return (centred * lax.rsqrt(var + EPS)).astype(BF16)

def dot_t(a, b):
    return lax.dot_general(a, b, (((1,), (1,)), ((), ())), preferred_element_type=F32)

def transposed(w):
    return w[...].astype(F32).T.astype(BF16)

def gated(weights, normed, mask):
    both = dot_t(weights, normed)
    c = both.shape[0] // 2
    return both[:c] * mask * jax.nn.sigmoid(both[c:])

def left_kernel(flags, x, x_next, mask_k, w, w_gate, out, wt, held):
    half, tile, chans = x.shape
    hid = w.shape[1]
    wt[:hid] = transposed(w)
    wt[hid:] = transposed(w_gate)
    ones = jnp.ones((chans, chans), BF16)
    weights = wt[...]
    def step(i, carry):
        block = jnp.concatenate([x[i], x_next[i]], axis=0)
        got = gated(weights, normalise(block, ones), mask_k[...] * flags[i].astype(F32))
        held[pl.ds(i, hid, stride=half), :] = got
        return carry
    lax.fori_loop(0, half, step, 0, unroll=4)
    def cast(c, carry):
        out[pl.ds(c * 8, 8)] = held[pl.ds(pl.multiple_of(c * 8 * half, 8 * half), 8 * half), :].reshape(8, half, 2 * tile).astype(BF16)
        return carry
    lax.fori_loop(0, hid // 8, cast, 0)

def left_call(flags, x, x_next, mask_k, w, w_gate):
    half, tile, chans = x.shape
    hid = w.shape[1]
    return pl.pallas_call(
        left_kernel,
        out_shape=jax.ShapeDtypeStruct((hid, half, 2 * tile), BF16),
        in_specs=[SMEM] + [VMEM] * 5,
        out_specs=VMEM,
        scratch_shapes=[pltpu.VMEM((2 * hid, chans), BF16), pltpu.VMEM((hid * half, 2 * tile), F32)],
        compiler_params=pltpu.CompilerParams(vmem_limit_bytes=32 << 20),
        name="left",
        cost_estimate=pl.CostEstimate(flops=2*half*tile*2*chans*5*hid, bytes_accessed=4 << 20, transcendentals=half*tile*2*hid*2),
    )(flags, x, x_next, mask_k, w, w_gate)

def chunk_kernel(piece, *refs):
    *got, out, rest = refs
    chans = out.shape[1]
    total = got[0][...]
    for g in got[1:]:
        total = total + g[...]
    normed = normalise(total, jnp.ones((chans, chans), BF16))
    out[...] = normed[:piece]
    rest[...] = normed[piece:]

def chunk_call(got, piece):
    n, chans = got[0].shape
    return pl.pallas_call(
        functools.partial(chunk_kernel, piece),
        out_shape=(jax.ShapeDtypeStruct((piece, chans), BF16), jax.ShapeDtypeStruct((n - piece, chans), BF16)),
        in_specs=[VMEM] * len(got),
        out_specs=(VMEM, VMEM),
        compiler_params=pltpu.CompilerParams(vmem_limit_bytes=16 << 20),
        name="chunk",
        cost_estimate=pl.CostEstimate(flops=0, bytes_accessed=1 << 20, transcendentals=0),
    )(*got)

def tri_project(left, right, w_out, held, half):
    hid = left.shape[0]
    group = 8
    def channel(g, carry):
        for u in range(group):
            c = g * group + u
            held[pl.ds(c, half, stride=hid), :half] = dot_t(left[c], right[c])
        return carry
    lax.fori_loop(0, hid // group, channel, 0)
    weights = w_out[...]
    def projected(i):
        tri = held[pl.ds(pl.multiple_of(i * hid, hid), hid), :half]
        mean = jnp.sum(tri, axis=0, keepdims=True) * (1.0 / hid)
        var = jnp.sum(tri * tri, axis=0, keepdims=True) * (1.0 / hid) - mean * mean
        normed = ((tri - mean) * lax.rsqrt(var + EPS)).astype(BF16)
        return lax.dot_general(normed, weights, (((0,), (0,)), ((), ())), preferred_element_type=F32)
    return projected

def right_kernel(order, flags, gathered, rest_a, rest_b, mask_k, w, w_gate, left, w_out, out, right, wt, tiles, held, tri):
    shards, piece, chans = gathered.shape
    hid, half, width = left.shape
    tile = width // 2
    kept = shards // 2 * piece
    wt[:hid] = transposed(w)
    wt[hid:] = transposed(w_gate)
    for s in range(shards // 2):
        for t in range(2):
            tiles[t, pl.ds(s * piece, piece)] = gathered[order[2 * s + t]]
    tiles[0, kept:] = rest_a[...]
    tiles[1, kept:] = rest_b[...]
    weights = wt[...]
    def step(j, carry):
        at = pl.ds(pl.multiple_of(j * tile, tile), tile)
        block = jnp.concatenate([tiles[0, at], tiles[1, at]], axis=0)
        held[pl.ds(j, hid, stride=half), :] = gated(weights, block, mask_k[...] * flags[j].astype(F32))
        return carry
    lax.fori_loop(0, half, step, 0, unroll=4)
    def cast(c, carry):
        right[pl.ds(c * 8, 8)] = held[pl.ds(pl.multiple_of(c * 8 * half, 8 * half), 8 * half), :].reshape(8, half, width).astype(BF16)
        return carry
    lax.fori_loop(0, hid // 8, cast, 0)
    projected = tri_project(left, right, w_out, tri, half)
    def row(i, carry):
        out[i] = projected(i).astype(BF16)
        return carry
    lax.fori_loop(0, half, row, 0, unroll=4)

def right_call(order, flags, gathered, rest_a, rest_b, mask_k, w, w_gate, left, w_out):
    hid, half, width = left.shape
    chans = gathered.shape[-1]
    return pl.pallas_call(
        right_kernel,
        out_shape=(jax.ShapeDtypeStruct((half, half, chans), BF16), jax.ShapeDtypeStruct((hid, half, width), BF16)),
        in_specs=[SMEM] * 2 + [VMEM] * 8,
        out_specs=(VMEM, VMEM),
        scratch_shapes=[
            pltpu.VMEM((2 * hid, chans), BF16),
            pltpu.VMEM((2, half * width // 2, chans), BF16),
            pltpu.VMEM((hid * half, width), F32),
            pltpu.VMEM((hid * half, 128), F32),
        ],
        compiler_params=pltpu.CompilerParams(vmem_limit_bytes=40 << 20),
        name="right_tri",
        cost_estimate=pl.CostEstimate(flops=2*half*width*chans*2*hid, bytes_accessed=4 << 20, transcendentals=half*width*hid*2),
    )(order, flags, gathered, rest_a, rest_b, mask_k, w, w_gate, left, w_out)

def own_kernel(x, w_gate, left, right, w_out, out, gate, tri):
    half, tile, chans = x.shape
    projected = tri_project(left, right, w_out, tri, half)
    ones = jnp.ones((chans, chans), BF16)
    weights = w_gate[...]
    def row(i, carry):
        out[i] = projected(i)
        gate[i] = jax.nn.sigmoid(jnp.dot(normalise(x[i], ones), weights, preferred_element_type=F32))
        return carry
    lax.fori_loop(0, half, row, 0, unroll=4)

def own_call(x, w_gate, left, right, w_out):
    half, tile, chans = x.shape
    hid = left.shape[0]
    return pl.pallas_call(
        own_kernel,
        out_shape=(jax.ShapeDtypeStruct((half, half, chans), F32), jax.ShapeDtypeStruct((half, tile, chans), F32)),
        in_specs=[VMEM] * 5,
        out_specs=(VMEM, VMEM),
        scratch_shapes=[pltpu.VMEM((hid * half, 128), F32)],
        compiler_params=pltpu.CompilerParams(vmem_limit_bytes=32 << 20),
        name="own_tri",
        cost_estimate=pl.CostEstimate(flops=2*half*tile*chans*chans*4, bytes_accessed=4 << 20, transcendentals=half*tile*chans*2),
    )(x, w_gate, left, right, w_out)


def per_device(pair_rep, token_mask, w_a, w_a_gate, w_b, w_b_gate, w_gate, w_out):
    half, tile, chans = pair_rep.shape
    rows, cols, reps = lax.axis_size("row"), lax.axis_size("col"), lax.axis_size("rep")
    row, col, rep = lax.axis_index("row"), lax.axis_index("col"), lax.axis_index("rep")
    swap = [(p, 1 - p) for p in range(reps)]
    back = [(c, (c - 1) % cols) for c in range(cols)]
    flat = pair_rep.reshape(-1, chans)

    sends = rows // 2
    kept = flat.shape[0] // rows * (rows - 1)
    piece = kept // sends
    even = [0, 8, 6, -6, 4, -4, 2, -2]
    odd = [1, 7, -7, 5, -5, 3, -3, -1]
    got = []
    for s in range(sends):
        pairs = [(c * cols + c, (c + even[s]) % rows * cols + c) for c in range(cols)]
        pairs += [(c * cols + (c + 1) % cols, (c + odd[s]) % rows * cols + c) for c in range(cols)]
        message = jnp.concatenate([flat[s * piece : (s + 1) * piece], flat[kept:]])
        got.append(lax.ppermute(message, ("row", "col"), pairs))
    x_next = lax.ppermute(flat, "col", back)
    x_next, got = lax.optimization_barrier((x_next, got))
    order = jnp.array([o % rows for pair in zip(even, odd) for o in pair], jnp.int32)
    order = (order + col) % rows

    wrapped = jnp.concatenate([token_mask, token_mask[:tile]])
    mask_k = lax.dynamic_slice_in_dim(wrapped, col * tile, 2 * tile, 0).astype(F32).reshape(1, -1)
    mask_i = lax.dynamic_slice_in_dim(token_mask, row * tile + rep * half, half, 0)
    mask_j = lax.dynamic_slice_in_dim(token_mask, col * tile + rep * half, half, 0)

    left = left_call(mask_i, pair_rep, x_next.reshape(half, tile, chans), mask_k, w_a, w_a_gate)
    other = lax.ppermute(left, "rep", swap)

    chunk, rest = chunk_call(got, piece)
    rest_other = lax.ppermute(rest, "row", [(r, r ^ 1) for r in range(rows)])
    gathered = lax.all_gather(chunk, "row", axis=0, tiled=False)
    first = (row - col) % 2 == 0
    rests = (jnp.where(first, rest, rest_other), jnp.where(first, rest_other, rest))

    theirs, right = right_call(order, mask_j, gathered, *rests, mask_k, w_b, w_b_gate, other, w_out)
    received = lax.ppermute(theirs, "rep", swap)
    ours, gate = own_call(pair_rep, w_gate, left, right, w_out)
    received = received.astype(F32)
    low = rep == 0
    projected = jnp.concatenate([jnp.where(low, ours, received), jnp.where(low, received, ours)], axis=1)
    return (gate * projected).astype(BF16)


def solution(mesh):
    placed = (P(("row", "rep"), "col", None), P(), P(), P(), P(), P(), P(), P())
    return jax.shard_map(
        per_device,
        mesh=mesh,
        in_specs=placed,
        out_specs=P(("row", "rep"), "col", None),
        check_vma=False,
    )
```

time: 123 us -> 114 us (0.927)
  Pallas kernels: 0 us -> 30.8 us
  local copies, waits for them, and re-layouts: 19.7 us -> 5.56 us
  matrix products: 11.9 us -> 0 us
  other arithmetic: 8.05 us -> 1.3 us
  waiting for transfers between devices: 7.47 us -> 2.8 us
  blocking collectives: 35.5 us -> 33 us
    pallas_call x0 -> x4, Pallas kernels: none -> 30.8 us  [the longest x1 10.9 us: own_call(): pl.pallas_call(own_kernel, out_shape=(jax.ShapeDtypeStruct((half, half, c...]
    reshape x6 -> x0, local copies, waits for them, and re-layouts: 16.6 us -> none  [the longest x2 6.73 us: both(): second.reshape(half, tile, chans)]
    dot_general x9 -> x0, matrix products: 11.9 us -> none  [the longest x2 6.74 us: tri_projected(): jnp.einsum('ikc,jkc->ijc', left, right, preferred_element_type=jnp.float32)]
    ppermute x1, waiting for transfers between devices: 3.63 us -> 0.01 us  [per_device(): received = lax.ppermute(theirs, 'rep', swap)]
    unnamed x18 -> x22, local copies, waits for them, and re-layouts: 0.13 us -> 3.64 us
    reduce_sum x2 -> x0, other arithmetic: 3.07 us -> none  [the longest x1 1.68 us: layer_norm(): var = jnp.mean(centred * centred, axis=-1, keepdims=True)]
    convert_element_type x5 -> x1, other arithmetic: 3.85 us -> 0.98 us  [per_device(): return (gate * projected).astype(BF16)]
    convert_element_type x2 -> x0, local copies, waits for them, and re-layouts: 2.6 us -> none  [tri_projected(): normed = ((tri - mean) * lax.rsqrt(var + EPS)).astype(jnp.bfloat16)]
  transfers between devices with their start and end apart: 13 -> 12, of which waited for: 2 -> 2; matrix products, arithmetic and copies ran while one was open for 19% -> 2% of each run, Pallas kernels for 0% -> 10%
where the time goes in v2:
time: 114 us; the launch traced here: 113 us
  starting transfers between devices  39.5 us (35%)
  blocking collectives  33 us (29%)
  Pallas kernels  30.8 us (27%)
  local copies, waits for them, and re-layouts  5.56 us (5%)
  waiting for transfers between devices  2.8 us (2%)
  other arithmetic  1.3 us (1%)
    all_gather x1, blocking collectives, per_device(): gathered = lax.all_gather(chunk, 'row', axis=0, tiled=False)  33 us
    ppermute x8, starting transfers between devices, per_device(): got.append(lax.ppermute(message, ('row', 'col'), pairs))  23.6 us
    pallas_call x1, Pallas kernels, own_call(): pl.pallas_call(own_kernel, out_shape=(jax.ShapeDtypeStruct((half, half, c...  10.9 us
    pallas_call x1, Pallas kernels, left_call(): pl.pallas_call(left_kernel, out_shape=jax.ShapeDtypeStruct((hid, half, 2...  9.96 us
    pallas_call x1, Pallas kernels, right_call(): pl.pallas_call(right_kernel, out_shape=(jax.ShapeDtypeStruct((half, half,...  9.49 us
    ppermute x1, starting transfers between devices, per_device(): x_next = lax.ppermute(flat, 'col', back)  5.83 us
    ppermute x1, starting transfers between devices, per_device(): rest_other = lax.ppermute(rest, 'row', [(r, r ^ 1) for r in range(rows)])  4.13 us
    unnamed x22, local copies, waits for them, and re-layouts  3.64 us
  transfers between devices with their start and end apart: 12, of which 2 were waited for; matrix products, arithmetic and copies ran while one was open for 2% of the time, Pallas kernels for 10%

profile of v2, /device:TPU:8, one launch (start us, length us, event | category | flops | bytes accessed | tf_op | source)
XLA Modules:
  0.0 113.2 jit_solution(1400458516839635500)
XLA Ops:
  0.0 5.8 %collective-permute-start = (bf16[2048,128]{1,0:T(8,128)(2,1)}, bf16[2048,128]{1,0:T(8,128)(2,1)S(1)}, u32[]{:S(2)}, u32[]{:S(2)}) collective-permute-start(bf16[2048,128]{1,0:T(8,128)(2,1)} %bitcast.7), channel_id=1, source_target_pairs={{0,30},{2,0},{4,2},{6,4},{8,6},{10,8},{12,10},{14,12},{16,14},{18,... | collective-permute-start | bytes 1572872 | tf_op jit(solution)/shard_map/ppermute | solution.py:203
  5.8 0.8 slice.41
  6.6 1.1 fusion.3
  7.8 12.0 %collective-permute-start.8 = (bf16[368,128]{1,0:T(8,128)(2,1)S(1)}, bf16[368,128]{1,0:T(8,128)(2,1)S(1)}, u32[]{:S(2)}, u32[]{:S(2)}) collective-permute-start(bf16[368,128]{1,0:T(8,128)(2,1)S(1)} %get-tuple-element.47), channel_id=1, source_target_pairs={{0,448},{34,482},{68,4},{102,38},{136,72},{170,106},{204,140},{238... | collective-permute-start | bytes 282632 | tf_op jit(solution)/shard_map/ppermute | solution.py:202
  19.8 4.5 %collective-permute-start.2 = (bf16[368,128]{1,0:T(8,128)(2,1)S(1)}, bf16[368,128]{1,0:T(8,128)(2,1)S(1)}, u32[]{:S(2)}, u32[]{:S(2)}) collective-permute-start(bf16[368,128]{1,0:T(8,128)(2,1)S(1)} %get-tuple-element.48), channel_id=1, source_target_pairs={{0,256},{34,290},{68,324},{102,358},{136,392},{170,426},{204,460},... | collective-permute-start | bytes 282632 | tf_op jit(solution)/shard_map/ppermute | solution.py:202
  24.3 1.3 %collective-permute-start.3 = (bf16[368,128]{1,0:T(8,128)(2,1)S(1)}, bf16[368,128]{1,0:T(8,128)(2,1)S(1)}, u32[]{:S(2)}, u32[]{:S(2)}) collective-permute-start(bf16[368,128]{1,0:T(8,128)(2,1)S(1)} %get-tuple-element.49), channel_id=1, source_target_pairs={{0,192},{34,226},{68,260},{102,294},{136,328},{170,362},{204,396},... | collective-permute-start | bytes 282632 | tf_op jit(solution)/shard_map/ppermute | solution.py:202
  25.7 1.3 %collective-permute-start.4 = (bf16[368,128]{1,0:T(8,128)(2,1)S(1)}, bf16[368,128]{1,0:T(8,128)(2,1)S(1)}, u32[]{:S(2)}, u32[]{:S(2)}) collective-permute-start(bf16[368,128]{1,0:T(8,128)(2,1)S(1)} %get-tuple-element.50), channel_id=1, source_target_pairs={{0,320},{34,354},{68,388},{102,422},{136,456},{170,490},{204,12},{... | collective-permute-start | bytes 282632 | tf_op jit(solution)/shard_map/ppermute | solution.py:202
  27.1 1.3 %collective-permute-start.5 = (bf16[368,128]{1,0:T(8,128)(2,1)S(1)}, bf16[368,128]{1,0:T(8,128)(2,1)S(1)}, u32[]{:S(2)}, u32[]{:S(2)}) collective-permute-start(bf16[368,128]{1,0:T(8,128)(2,1)S(1)} %get-tuple-element.51), channel_id=1, source_target_pairs={{0,128},{34,162},{68,196},{102,230},{136,264},{170,298},{204,332},... | collective-permute-start | bytes 282632 | tf_op jit(solution)/shard_map/ppermute | solution.py:202
  28.4 1.3 %collective-permute-start.6 = (bf16[368,128]{1,0:T(8,128)(2,1)S(1)}, bf16[368,128]{1,0:T(8,128)(2,1)S(1)}, u32[]{:S(2)}, u32[]{:S(2)}) collective-permute-start(bf16[368,128]{1,0:T(8,128)(2,1)S(1)} %get-tuple-element.52), channel_id=1, source_target_pairs={{0,384},{34,418},{68,452},{102,486},{136,8},{170,42},{204,76},{238... | collective-permute-start | bytes 282632 | tf_op jit(solution)/shard_map/ppermute | solution.py:202
  29.7 1.3 %collective-permute-start.7 = (bf16[368,128]{1,0:T(8,128)(2,1)S(1)}, bf16[368,128]{1,0:T(8,128)(2,1)S(1)}, u32[]{:S(2)}, u32[]{:S(2)}) collective-permute-start(bf16[368,128]{1,0:T(8,128)(2,1)S(1)} %get-tuple-element.53), channel_id=1, source_target_pairs={{0,64},{34,98},{68,132},{102,166},{136,200},{170,234},{204,268},{2... | collective-permute-start | bytes 282632 | tf_op jit(solution)/shard_map/ppermute | solution.py:202
  31.0 0.7 collective-permute-start.1
  31.8 1.0 collective-permute-done.5.refs_4_
  32.8 1.8 %collective-permute-done.7.refs_6_ = bf16[368,128]{1,0:T(8,128)(2,1)S(1)} collective-permute-done((bf16[368,128]{1,0:T(8,128)(2,1)S(1)}, bf16[368,128]{1,0:T(8,128)(2,1)S(1)}, u32[]{:S(2)}, u32[]{:S(2)}) %collective-permute-start.7) | collective-permute-done | bytes 94240 | tf_op jit(solution)/shard_map/ppermute | solution.py:202
  34.6 10.0 %left.1 = bf16[128,32,128]{2,1,0:T(8,128)(2,1)S(1)} custom-call(s32[32]{0:T(128)S(1)} %get-tuple-element.56.flags, bf16[32,64,128]{2,1,0:T(8,128)(2,1)S(1)} %copy-done, bf16[32,64,128]{2,1,0:T(8,128)(2,1)S(1)} %bitcast.9, f32[1,128]{1,0:T(1,128)S(1)} %convert_bitcast_fusion.mask_k, bf16[128,128]{1,0:T(8,128)(2,1)S(1)} %copy-done.7, ...), custom_call_target="tpu_custom_call" | custom-call | flops 671088640 | bytes 4194304 | tf_op jit(solution)/shard_map/left/pallas_call | solution.py:59
  44.5 3.3 %collective-permute-start.10 = (bf16[128,32,128]{2,1,0:T(8,128)(2,1)S(1)}, bf16[128,32,128]{2,1,0:T(8,128)(2,1)S(1)}, u32[]{:S(2)}, u32[]{:S(2)}) collective-permute-start(bf16[128,32,128]{2,1,0:T(8,128)(2,1)S(1)} %left.1), channel_id=1, source_target_pairs={{0,1},{1,0},{2,3},{3,2},{4,5},{5,4},{6,7},{7,6},{8,9},{9,8},{10,11... | collective-permute-start | bytes 3145736 | tf_op jit(solution)/shard_map/ppermute | solution.py:214
  49.0 4.1 %collective-permute-start.9 = (bf16[128,128]{1,0:T(8,128)(2,1)S(1)}, bf16[128,128]{1,0:T(8,128)(2,1)S(1)}, u32[]{:S(2)}, u32[]{:S(2)}) collective-permute-start(bf16[128,128]{1,0:T(8,128)(2,1)S(1)} %get-tuple-element.30), channel_id=1, source_target_pairs={{0,32},{32,0},{64,96},{96,64},{128,160},{160,128},{192,224},{224,1... | collective-permute-start | bytes 98312 | tf_op jit(solution)/shard_map/ppermute | solution.py:217
  53.1 33.0 %all-gather = bf16[3840,128]{1,0:T(8,128)(2,1)S(1)} all-gather(bf16[240,128]{1,0:T(8,128)(2,1)S(1)} %get-tuple-element.29), channel_id=2, replica_groups=mesh['row'=16,'col'=16,'rep'=2] {'row'}, dimensions={0}, use_global_device_ids=true | all-gather | bytes 1044480 | tf_op jit(solution)/shard_map/all_gather | solution.py:218
  86.1 0.7 copy-done.3
  86.9 9.5 %right_tri.1 = (bf16[32,32,128]{2,1,0:T(8,128)(2,1)S(1)}, bf16[128,32,128]{2,1,0:T(8,128)(2,1)S(1)}) custom-call(s32[16]{0:T(128)S(1)} %and_select_fusion.order, s32[32]{0:T(128)S(1)} %get-tuple-element.55.flags, bf16[16,240,128]{2,1,0:T(8,128)(2,1)S(1)} %bitcast.6, bf16[128,128]{1,0:T(8,128)(2,1)S(1)} %get-tuple-element.46.rest_a, ...), custom_call_target="tpu_custom_call" | custom-call | flops 268435456 | bytes 4194304 | tf_op jit(solution)/shard_map/right_tri/pallas_call | solution.py:142
  96.4 1.0 copy-done.1
  97.3 2.6 %collective-permute-start.11 = (bf16[32,32,128]{2,1,0:T(8,128)(2,1)S(1)}, bf16[32,32,128]{2,1,0:T(8,128)(2,1)S(1)}, u32[]{:S(2)}, u32[]{:S(2)}) collective-permute-start(bf16[32,32,128]{2,1,0:T(8,128)(2,1)S(1)} %get-tuple-element.34), channel_id=1, source_target_pairs={{0,1},{1,0},{2,3},{3,2},{4,5},{5,4},{6,7},{7,6},{8,9},{9,8},{10,11... | collective-permute-start | bytes 786440 | tf_op jit(solution)/shard_map/ppermute | solution.py:223
  100.0 1.2 %copy-done.2 = bf16[128,32,128]{2,1,0:T(8,128)(2,1)S(1)} copy-done((bf16[128,32,128]{2,1,0:T(8,128)(2,1)S(1)}, bf16[128,32,128]{2,1,0:T(8,128)(2,1)}, u32[]{:S(2)}) %copy-start.2) | copy-done | bytes 1048600
  101.2 10.9 %own_tri.1 = (f32[32,32,128]{2,1,0:T(8,128)S(1)}, f32[32,64,128]{2,1,0:T(8,128)S(1)}) custom-call(bf16[32,64,128]{2,1,0:T(8,128)(2,1)S(1)} %copy-done, bf16[128,128]{1,0:T(8,128)(2,1)S(1)} %copy-done.6, bf16[128,32,128]{2,1,0:T(8,128)(2,1)S(1)} %left.1, bf16[128,32,128]{2,1,0:T(8,128)(2,1)S(1)} %copy-done.2, bf16[128,128]{1,0:T(8,128)(2,1)S(1)} %copy-done.3), custom_call_target="tpu_custom_call" | custom-call | flops 268435456 | bytes 4194304 | tf_op jit(solution)/shard_map/own_tri/pallas_call | solution.py:172
  112.3 1.0 fusion
  (38 shorter events, 1.7 us)
Async XLA Ops:
  0.0 34.5 %collective-permute-start = (bf16[2048,128]{1,0:T(8,128)(2,1)}, bf16[2048,128]{1,0:T(8,128)(2,1)S(1)}, u32[]{:S(2)}, u32[]{:S(2)}) collective-permute-start(bf16[2048,128]{1,0:T(8,128)(2,1)} %bitcast.7), channel_id=1, source_target_pairs={{0,30},{2,0},{4,2},{6,4},{8,6},{10,8},{12,10},{14,12},{16,14},{18,... | collective-permute-start | bytes 1572872 | tf_op jit(solution)/shard_map/ppermute | solution.py:203
  7.7 19.3 %copy-start.9 = (s32[1024]{0:T(1024)S(1)}, s32[1024]{0:T(1024)}, u32[]{:S(2)}) copy-start(s32[1024]{0:T(1024)} %param.10) | copy-start | bytes 12292
  7.7 24.0 %slice-start = ((s32[1024]{0:T(1024)}), s32[64]{0:T(128)S(1)}, s32[]{:S(2)}) async-start(s32[1024]{0:T(1024)} %param.10), calls=%async_computation | async-start | bytes 1024 | tf_op jit(solution)/shard_map/slice | solution.py:208
  7.7 26.8 %copy-start = (bf16[32,64,128]{2,1,0:T(8,128)(2,1)S(1)}, bf16[32,64,128]{2,1,0:T(8,128)(2,1)}, u32[]{:S(2)}) copy-start(bf16[32,64,128]{2,1,0:T(8,128)(2,1)} %x.3) | copy-start | bytes 1572868
  7.8 19.3 %collective-permute-start.8 = (bf16[368,128]{1,0:T(8,128)(2,1)S(1)}, bf16[368,128]{1,0:T(8,128)(2,1)S(1)}, u32[]{:S(2)}, u32[]{:S(2)}) collective-permute-start(bf16[368,128]{1,0:T(8,128)(2,1)S(1)} %get-tuple-element.47), channel_id=1, source_target_pairs={{0,448},{34,482},{68,4},{102,38},{136,72},{170,106},{204,140},{238... | collective-permute-start | bytes 282632 | tf_op jit(solution)/shard_map/ppermute | solution.py:202
  19.8 8.6 %collective-permute-start.2 = (bf16[368,128]{1,0:T(8,128)(2,1)S(1)}, bf16[368,128]{1,0:T(8,128)(2,1)S(1)}, u32[]{:S(2)}, u32[]{:S(2)}) collective-permute-start(bf16[368,128]{1,0:T(8,128)(2,1)S(1)} %get-tuple-element.48), channel_id=1, source_target_pairs={{0,256},{34,290},{68,324},{102,358},{136,392},{170,426},{204,460},... | collective-permute-start | bytes 282632 | tf_op jit(solution)/shard_map/ppermute | solution.py:202
  24.3 5.4 %collective-permute-start.3 = (bf16[368,128]{1,0:T(8,128)(2,1)S(1)}, bf16[368,128]{1,0:T(8,128)(2,1)S(1)}, u32[]{:S(2)}, u32[]{:S(2)}) collective-permute-start(bf16[368,128]{1,0:T(8,128)(2,1)S(1)} %get-tuple-element.49), channel_id=1, source_target_pairs={{0,192},{34,226},{68,260},{102,294},{136,328},{170,362},{204,396},... | collective-permute-start | bytes 282632 | tf_op jit(solution)/shard_map/ppermute | solution.py:202
  25.7 5.4 %collective-permute-start.4 = (bf16[368,128]{1,0:T(8,128)(2,1)S(1)}, bf16[368,128]{1,0:T(8,128)(2,1)S(1)}, u32[]{:S(2)}, u32[]{:S(2)}) collective-permute-start(bf16[368,128]{1,0:T(8,128)(2,1)S(1)} %get-tuple-element.50), channel_id=1, source_target_pairs={{0,320},{34,354},{68,388},{102,422},{136,456},{170,490},{204,12},{... | collective-permute-start | bytes 282632 | tf_op jit(solution)/shard_map/ppermute | solution.py:202
  27.0 7.6 %copy-start.8 = (bf16[128,128]{1,0:T(8,128)(2,1)S(1)}, bf16[128,128]{1,0:T(8,128)(2,1)}, u32[]{:S(2)}) copy-start(bf16[128,128]{1,0:T(8,128)(2,1)} %w_gate.3) | copy-start | bytes 98308
  27.0 7.6 %copy-start.7 = (bf16[128,128]{1,0:T(8,128)(2,1)S(1)}, bf16[128,128]{1,0:T(8,128)(2,1)}, u32[]{:S(2)}) copy-start(bf16[128,128]{1,0:T(8,128)(2,1)} %w.2) | copy-start | bytes 98308
  27.1 5.7 %collective-permute-start.5 = (bf16[368,128]{1,0:T(8,128)(2,1)S(1)}, bf16[368,128]{1,0:T(8,128)(2,1)S(1)}, u32[]{:S(2)}, u32[]{:S(2)}) collective-permute-start(bf16[368,128]{1,0:T(8,128)(2,1)S(1)} %get-tuple-element.51), channel_id=1, source_target_pairs={{0,128},{34,162},{68,196},{102,230},{136,264},{170,298},{204,332},... | collective-permute-start | bytes 282632 | tf_op jit(solution)/shard_map/ppermute | solution.py:202
  28.4 4.4 %collective-permute-start.6 = (bf16[368,128]{1,0:T(8,128)(2,1)S(1)}, bf16[368,128]{1,0:T(8,128)(2,1)S(1)}, u32[]{:S(2)}, u32[]{:S(2)}) collective-permute-start(bf16[368,128]{1,0:T(8,128)(2,1)S(1)} %get-tuple-element.52), channel_id=1, source_target_pairs={{0,384},{34,418},{68,452},{102,486},{136,8},{170,42},{204,76},{238... | collective-permute-start | bytes 282632 | tf_op jit(solution)/shard_map/ppermute | solution.py:202
  29.7 4.8 %collective-permute-start.7 = (bf16[368,128]{1,0:T(8,128)(2,1)S(1)}, bf16[368,128]{1,0:T(8,128)(2,1)S(1)}, u32[]{:S(2)}, u32[]{:S(2)}) collective-permute-start(bf16[368,128]{1,0:T(8,128)(2,1)S(1)} %get-tuple-element.53), channel_id=1, source_target_pairs={{0,64},{34,98},{68,132},{102,166},{136,200},{170,234},{204,268},{2... | collective-permute-start | bytes 282632 | tf_op jit(solution)/shard_map/ppermute | solution.py:202
  31.0 3.5 %collective-permute-start.1 = (bf16[368,128]{1,0:T(8,128)(2,1)S(1)}, bf16[368,128]{1,0:T(8,128)(2,1)S(1)}, u32[]{:S(2)}, u32[]{:S(2)}) collective-permute-start(bf16[368,128]{1,0:T(8,128)(2,1)S(1)} %get-tuple-element.54), channel_id=1, source_target_pairs={{0,0},{34,34},{68,68},{102,102},{136,136},{170,170},{204,204},{238... | collective-permute-start | bytes 282632 | tf_op jit(solution)/shard_map/ppermute | solution.py:202
  44.5 41.6 %collective-permute-start.10 = (bf16[128,32,128]{2,1,0:T(8,128)(2,1)S(1)}, bf16[128,32,128]{2,1,0:T(8,128)(2,1)S(1)}, u32[]{:S(2)}, u32[]{:S(2)}) collective-permute-start(bf16[128,32,128]{2,1,0:T(8,128)(2,1)S(1)} %left.1), channel_id=1, source_target_pairs={{0,1},{1,0},{2,3},{3,2},{4,5},{5,4},{6,7},{7,6},{8,9},{9,8},{10,11... | collective-permute-start | bytes 3145736 | tf_op jit(solution)/shard_map/ppermute | solution.py:214
  47.8 0.7 copy-start.10
  49.0 37.1 %collective-permute-start.9 = (bf16[128,128]{1,0:T(8,128)(2,1)S(1)}, bf16[128,128]{1,0:T(8,128)(2,1)S(1)}, u32[]{:S(2)}, u32[]{:S(2)}) collective-permute-start(bf16[128,128]{1,0:T(8,128)(2,1)S(1)} %get-tuple-element.30), channel_id=1, source_target_pairs={{0,32},{32,0},{64,96},{96,64},{128,160},{160,128},{192,224},{224,1... | collective-permute-start | bytes 98312 | tf_op jit(solution)/shard_map/ppermute | solution.py:217
  86.1 0.8 copy-start.3
  86.1 0.8 copy-start.4
  86.1 0.8 copy-start.5
  86.8 13.1 %copy-start.6 = (bf16[128,128]{1,0:T(8,128)(2,1)S(1)}, bf16[128,128]{1,0:T(8,128)(2,1)}, u32[]{:S(2)}) copy-start(bf16[128,128]{1,0:T(8,128)(2,1)} %w_gate.5) | copy-start | bytes 98308
  96.3 1.0 copy-start.1
  97.3 14.8 %collective-permute-start.11 = (bf16[32,32,128]{2,1,0:T(8,128)(2,1)S(1)}, bf16[32,32,128]{2,1,0:T(8,128)(2,1)S(1)}, u32[]{:S(2)}, u32[]{:S(2)}) collective-permute-start(bf16[32,32,128]{2,1,0:T(8,128)(2,1)S(1)} %get-tuple-element.34), channel_id=1, source_target_pairs={{0,1},{1,0},{2,3},{3,2},{4,5},{5,4},{6,7},{7,6},{8,9},{9,8},{10,11... | collective-permute-start | bytes 786440 | tf_op jit(solution)/shard_map/ppermute | solution.py:223
  100.0 1.2 %copy-start.2 = (bf16[128,32,128]{2,1,0:T(8,128)(2,1)S(1)}, bf16[128,32,128]{2,1,0:T(8,128)(2,1)}, u32[]{:S(2)}) copy-start(bf16[128,32,128]{2,1,0:T(8,128)(2,1)} %copy-done.1) | copy-start | bytes 3145732

commit v3 on v2

v3 whole, which is shorter than its diff:
```python
import functools

import jax
import jax.numpy as jnp
from jax import lax
from jax.experimental import pallas as pl
from jax.experimental.pallas import tpu as pltpu
from jax.sharding import PartitionSpec as P

EPS = 1e-5
VMEM = pl.BlockSpec(memory_space=pltpu.VMEM)
SMEM = pl.BlockSpec(memory_space=pltpu.SMEM)
F32 = jnp.float32
BF16 = jnp.bfloat16
GROUP = 16
LIMIT = 20 << 20


def dot(a, b, dims):
    return lax.dot_general(a, b, (dims, ((), ())), preferred_element_type=F32)


def normalise(block):
    chans = block.shape[1]
    ones = jnp.ones((chans, chans), BF16)
    centred = block.astype(F32) - dot(block, ones, ((1,), (0,))) * (1.0 / chans)
    var = dot((centred * centred).astype(BF16), ones, ((1,), (0,))) * (1.0 / chans)
    return (centred * lax.rsqrt(var + EPS)).astype(BF16)


def halved_transpose(w):
    return (w[...].astype(F32).T * 0.5).astype(BF16)


def gated(weights, normed, masks):
    hid = weights.shape[0] // 2
    both = dot(weights, normed, ((1,), (1,)))
    width = masks[0].shape[1]
    parts = []
    for n, mask in enumerate(masks):
        at = slice(n * width, (n + 1) * width)
        value = both[:hid, at] * mask
        parts.append(value + value * jnp.tanh(both[hid:, at]))
    return jnp.concatenate(parts, axis=1).reshape(hid, len(masks), width).astype(BF16)


def left_kernel(flags, x, x_next, mask_k, w, w_gate, v, v_gate, out, wt_right):
    half = x.shape[0]
    weights = jnp.concatenate([halved_transpose(w), halved_transpose(w_gate)])
    wt_right[...] = jnp.concatenate([halved_transpose(v), halved_transpose(v_gate)])
    for q in range(0, half, GROUP):
        blocks = [part[i] for i in range(q, q + GROUP) for part in (x, x_next)]
        masks = [mask_k[...] * flags[i].astype(F32) for i in range(q, q + GROUP)]
        out[:, q : q + GROUP, :] = gated(weights, normalise(jnp.concatenate(blocks)), masks)


def left_call(flags, x, x_next, mask_k, *ws):
    half, tile, chans = x.shape
    hid = ws[0].shape[1]
    return pl.pallas_call(
        left_kernel,
        out_shape=(
            jax.ShapeDtypeStruct((hid, half, 2 * tile), BF16),
            jax.ShapeDtypeStruct((2 * hid, chans), BF16),
        ),
        in_specs=[SMEM] + [VMEM] * 7,
        out_specs=(VMEM, VMEM),
        compiler_params=pltpu.CompilerParams(vmem_limit_bytes=LIMIT),
        name="left",
        cost_estimate=pl.CostEstimate(flops=10 * half * tile * 2 * chans * hid, bytes_accessed=2 << 20, transcendentals=4 * half * tile * hid),
    )(flags, x, x_next, mask_k, *ws)


def chunk_kernel(piece, *refs):
    *got, out, rest = refs
    total = got[0][...]
    for g in got[1:]:
        total = total + g[...]
    normed = normalise(total)
    out[...] = normed[:piece]
    rest[...] = normed[piece:]


def chunk_call(got, piece):
    n, chans = got[0].shape
    return pl.pallas_call(
        functools.partial(chunk_kernel, piece),
        out_shape=(jax.ShapeDtypeStruct((piece, chans), BF16), jax.ShapeDtypeStruct((n - piece, chans), BF16)),
        in_specs=[VMEM] * len(got),
        out_specs=(VMEM, VMEM),
        compiler_params=pltpu.CompilerParams(vmem_limit_bytes=LIMIT),
        name="chunk",
        cost_estimate=pl.CostEstimate(flops=4 * n * chans * chans, bytes_accessed=1 << 20, transcendentals=n * chans),
    )(*got)


def tri_projected(left, right, w_out, held, store):
    hid, half, _ = left.shape
    for c in range(0, hid, GROUP):
        parts = [dot(left[c + u], right[c + u], ((1,), (1,))) for u in range(GROUP)]
        held[:, c : c + GROUP, :] = jnp.swapaxes(jnp.stack(parts), 0, 1)
    pack = 128 // half
    for i in range(0, half, pack):
        tri = jnp.concatenate([held[i + u] for u in range(pack)], axis=1)
        mean = jnp.sum(tri, axis=0, keepdims=True) * (1.0 / hid)
        var = jnp.sum(tri * tri, axis=0, keepdims=True) * (1.0 / hid) - mean * mean
        normed = ((tri - mean) * lax.rsqrt(var + EPS)).astype(BF16)
        projected = dot(normed, w_out[...], ((0,), (0,)))
        for u in range(pack):
            store(i + u, projected[u * half : (u + 1) * half])


def right_kernel(order, flags, gathered, rest, rest_other, mask_k, weights, left, w_out, out, right, tiles, held):
    shards, piece, chans = gathered.shape
    hid, half, width = left.shape
    tile = width // 2
    kept = shards // 2 * piece
    for s in range(shards // 2):
        for t in range(2):
            tiles[t, s * piece : (s + 1) * piece] = gathered[order[2 * s + t]]
    tiles[order[shards], kept:] = rest[...]
    tiles[1 - order[shards], kept:] = rest_other[...]
    for q in range(0, half, GROUP):
        blocks = [tiles[t, j * tile : (j + 1) * tile] for j in range(q, q + GROUP) for t in range(2)]
        masks = [mask_k[...] * flags[j].astype(F32) for j in range(q, q + GROUP)]
        right[:, q : q + GROUP, :] = gated(weights[...], jnp.concatenate(blocks), masks)

    def store(i, rows):
        out[i] = rows.astype(BF16)

    tri_projected(left, right, w_out, held, store)


def right_call(order, flags, gathered, rest, rest_other, mask_k, weights, left, w_out):
    hid, half, width = left.shape
    chans = gathered.shape[-1]
    return pl.pallas_call(
        right_kernel,
        out_shape=(jax.ShapeDtypeStruct((half, half, chans), BF16), jax.ShapeDtypeStruct((hid, half, width), BF16)),
        in_specs=[SMEM] * 2 + [VMEM] * 7,
        out_specs=(VMEM, VMEM),
        scratch_shapes=[pltpu.VMEM((2, half * width // 2, chans), BF16), pltpu.VMEM((half, hid, half), F32)],
        compiler_params=pltpu.CompilerParams(vmem_limit_bytes=LIMIT),
        name="right_tri",
        cost_estimate=pl.CostEstimate(flops=8 * half * width * chans * hid, bytes_accessed=4 << 20, transcendentals=half * width * hid),
    )(order, flags, gathered, rest, rest_other, mask_k, weights, left, w_out)


def own_kernel(x, w_gate, left, right, w_out, out, gate, held):
    half, tile, chans = x.shape

    def store(i, rows):
        out[i] = rows

    tri_projected(left, right, w_out, held, store)
    for q in range(0, half, GROUP):
        normed = normalise(x[q : q + GROUP].reshape(GROUP * tile, chans))
        gate[q : q + GROUP] = jax.nn.sigmoid(dot(normed, w_gate[...], ((1,), (0,)))).reshape(GROUP, tile, chans)


def own_call(x, w_gate, left, right, w_out):
    half, tile, chans = x.shape
    hid = left.shape[0]
    return pl.pallas_call(
        own_kernel,
        out_shape=(jax.ShapeDtypeStruct((half, half, chans), F32), jax.ShapeDtypeStruct((half, tile, chans), F32)),
        in_specs=[VMEM] * 5,
        out_specs=(VMEM, VMEM),
        scratch_shapes=[pltpu.VMEM((half, hid, half), F32)],
        compiler_params=pltpu.CompilerParams(vmem_limit_bytes=LIMIT),
        name="own_tri",
        cost_estimate=pl.CostEstimate(flops=8 * half * tile * chans * chans, bytes_accessed=4 << 20, transcendentals=2 * half * tile * chans),
    )(x, w_gate, left, right, w_out)


def messages_kernel(kept, piece, flat, *outs):
    for s, out in enumerate(outs):
        out[:piece] = flat[s * piece : (s + 1) * piece]
        out[piece:] = flat[kept:]


def messages_call(flat, kept, sends):
    rows, chans = flat.shape
    piece = kept // sends
    shape = jax.ShapeDtypeStruct((piece + rows - kept, chans), flat.dtype)
    return pl.pallas_call(
        functools.partial(messages_kernel, kept, piece),
        out_shape=(shape,) * sends,
        in_specs=[VMEM],
        out_specs=(VMEM,) * sends,
        compiler_params=pltpu.CompilerParams(vmem_limit_bytes=LIMIT),
        name="messages",
        cost_estimate=pl.CostEstimate(flops=0, bytes_accessed=2 << 20, transcendentals=0),
    )(flat)


def per_device(pair_rep, token_mask, w_a, w_a_gate, w_b, w_b_gate, w_gate, w_out):
    half, tile, chans = pair_rep.shape
    rows, cols, reps = lax.axis_size("row"), lax.axis_size("col"), lax.axis_size("rep")
    row, col, rep = lax.axis_index("row"), lax.axis_index("col"), lax.axis_index("rep")
    swap = [(p, 1 - p) for p in range(reps)]
    flat = pair_rep.reshape(-1, chans)

    sends = rows // 2
    kept = flat.shape[0] // rows * (rows - 1)
    piece = kept // sends
    even = [8, 6, -6, 4, -4, 2, -2, 0]
    odd = [7, -7, 5, -5, 3, -3, 1, -1]
    got = []
    for s, message in enumerate(messages_call(flat, kept, sends)):
        pairs = [(c * cols + c, (c + even[s]) % rows * cols + c) for c in range(cols)]
        pairs += [(c * cols + (c + 1) % cols, (c + odd[s]) % rows * cols + c) for c in range(cols)]
        got.append(lax.ppermute(message, ("row", "col"), pairs))
    x_next = lax.ppermute(flat, "col", [(c, (c - 1) % cols) for c in range(cols)])
    x_next, got = lax.optimization_barrier((x_next, got))
    order = jnp.array([o % rows for pair in zip(even, odd) for o in pair], jnp.int32)
    order = jnp.concatenate([(order + col) % rows, (row + col).reshape(1) % 2])

    wrapped = jnp.concatenate([token_mask, token_mask[:tile]])
    mask_k = lax.dynamic_slice_in_dim(wrapped, col * tile, 2 * tile, 0).astype(F32).reshape(1, -1)
    mask_i = lax.dynamic_slice_in_dim(token_mask, row * tile + rep * half, half, 0)
    mask_j = lax.dynamic_slice_in_dim(token_mask, col * tile + rep * half, half, 0)

    left, wt_right = left_call(mask_i, pair_rep, x_next.reshape(half, tile, chans), mask_k, w_a, w_a_gate, w_b, w_b_gate)
    other = lax.ppermute(left, "rep", swap)

    chunk, rest = chunk_call(got, piece)
    rest_other = lax.ppermute(rest, "row", [(r, r ^ 1) for r in range(rows)])
    gathered = lax.all_gather(chunk, "row", axis=0, tiled=False)

    theirs, right = right_call(order, mask_j, gathered, rest, rest_other, mask_k, wt_right, other, w_out)
    received = lax.ppermute(theirs, "rep", swap)
    ours, gate = own_call(pair_rep, w_gate, left, right, w_out)
    received = received.astype(F32)
    low = rep == 0
    projected = jnp.concatenate([jnp.where(low, ours, received), jnp.where(low, received, ours)], axis=1)
    return (gate * projected).astype(BF16)


def solution(mesh):
    placed = (P(("row", "rep"), "col", None), P(), P(), P(), P(), P(), P(), P())
    return jax.shard_map(
        per_device,
        mesh=mesh,
        in_specs=placed,
        out_specs=P(("row", "rep"), "col", None),
        check_vma=False,
    )
```

time: 114 us -> 95 us (0.83)
  the two profiles are of different devices: /device:TPU:8 before, /device:TPU:36 now
where the time goes in v3:
time: 95 us; the launch traced here: 94.3 us
  blocking collectives  39 us (41%)
  waiting for transfers between devices  23.7 us (25%)
  starting transfers between devices  17.2 us (18%)
  Pallas kernels  7.3 us (8%)
  local copies, waits for them, and re-layouts  5.51 us (6%)
  other arithmetic  1.27 us (1%)
    all_gather x1, blocking collectives, per_device(): gathered = lax.all_gather(chunk, 'row', axis=0, tiled=False)  39 us
    ppermute x8, waiting for transfers between devices, per_device(): got.append(lax.ppermute(message, ('row', 'col'), pairs))  20.9 us
    ppermute x8, starting transfers between devices, per_device(): got.append(lax.ppermute(message, ('row', 'col'), pairs))  6.08 us
    unnamed x24, local copies, waits for them, and re-layouts  5.43 us
    ppermute x1, starting transfers between devices, per_device(): other = lax.ppermute(left, 'rep', swap)  3.49 us
    ppermute x1, starting transfers between devices, per_device(): rest_other = lax.ppermute(rest, 'row', [(r, r ^ 1) for r in range(rows)])  3.34 us
    pallas_call x1, Pallas kernels, right_call(): pl.pallas_call(right_kernel, out_shape=(jax.ShapeDtypeStruct((half, half,...  2.77 us
    ppermute x1, waiting for transfers between devices, per_device(): received = lax.ppermute(theirs, 'rep', swap)  2.74 us
  transfers between devices with their start and end apart: 12, of which 2 were waited for; matrix products, arithmetic and copies ran while one was open for 0% of the time, Pallas kernels for 2%

profile of v3, /device:TPU:36, one launch (start us, length us, event | category | flops | bytes accessed | tf_op | source)
XLA Modules:
  0.0 94.3 jit_solution(14635640439581560486)
XLA Ops:
  0.0 1.9 %collective-permute-start = (bf16[2048,128]{1,0:T(8,128)(2,1)}, bf16[2048,128]{1,0:T(8,128)(2,1)S(1)}, u32[]{:S(2)}, u32[]{:S(2)}) collective-permute-start(bf16[2048,128]{1,0:T(8,128)(2,1)} %bitcast.7), channel_id=1, source_target_pairs={{0,30},{2,0},{4,2},{6,4},{8,6},{10,8},{12,10},{14,12},{16,14},{18,... | collective-permute-start | bytes 1572872 | tf_op jit(solution)/shard_map/ppermute | solution.py:214
  1.9 1.0 %copy-done = bf16[32,64,128]{2,1,0:T(8,128)(2,1)S(1)} copy-done((bf16[32,64,128]{2,1,0:T(8,128)(2,1)S(1)}, bf16[32,64,128]{2,1,0:T(8,128)(2,1)}, u32[]{:S(2)}) %copy-start) | copy-done | bytes 524312
  3.0 0.8 collective-permute-start.1
  3.9 0.7 collective-permute-start.2
  4.5 0.7 collective-permute-start.3
  5.2 0.7 collective-permute-start.4
  6.0 0.7 collective-permute-start.5
  6.7 1.3 %collective-permute-start.6 = (bf16[368,128]{1,0:T(8,128)(2,1)S(1)}, bf16[368,128]{1,0:T(8,128)(2,1)S(1)}, u32[]{:S(2)}, u32[]{:S(2)}) collective-permute-start(bf16[368,128]{1,0:T(8,128)(2,1)S(1)} %get-tuple-element.35), channel_id=1, source_target_pairs={{0,64},{34,98},{68,132},{102,166},{136,200},{170,234},{204,268},{2... | collective-permute-start | bytes 282632 | tf_op jit(solution)/shard_map/ppermute | solution.py:213
  8.0 0.7 collective-permute-start.7
  8.7 0.7 collective-permute-start.8
  9.5 20.9 %collective-permute-done.6.refs_5_ = bf16[368,128]{1,0:T(8,128)(2,1)S(1)} collective-permute-done((bf16[368,128]{1,0:T(8,128)(2,1)S(1)}, bf16[368,128]{1,0:T(8,128)(2,1)S(1)}, u32[]{:S(2)}, u32[]{:S(2)}) %collective-permute-start.6) | collective-permute-done | bytes 94240 | tf_op jit(solution)/shard_map/ppermute | solution.py:213
  30.4 0.7 copy-done.8
  31.2 0.8 copy-done.9
  31.9 2.2 %left.1 = (bf16[128,32,128]{2,1,0:T(8,128)(2,1)S(1)}, bf16[256,128]{1,0:T(8,128)(2,1)S(1)}) custom-call(s32[32]{0:T(128)S(1)} %get-tuple-element.58.flags, bf16[32,64,128]{2,1,0:T(8,128)(2,1)S(1)} %copy-done.1, bf16[32,64,128]{2,1,0:T(8,128)(2,1)S(1)} %bitcast.9, f32[1,128]{1,0:T(1,128)S(1)} %convert_bitcast_fusion.mask_k, bf16[128,128]{1,0:T(8,128)(2,1)S(1)} %copy-done.6, ...), custom_call_target="tpu_custom_call" | custom-call | flops 671088640 | bytes 2097152 | tf_op jit(solution)/shard_map/left/pallas_call | solution.py:60
  34.1 3.5 %collective-permute-start.10 = (bf16[128,32,128]{2,1,0:T(8,128)(2,1)S(1)}, bf16[128,32,128]{2,1,0:T(8,128)(2,1)S(1)}, u32[]{:S(2)}, u32[]{:S(2)}) collective-permute-start(bf16[128,32,128]{2,1,0:T(8,128)(2,1)S(1)} %get-tuple-element.39.left), channel_id=1, source_target_pairs={{0,1},{1,0},{2,3},{3,2},{4,5},{5,4},{6,7},{7,6},{8,9},{9,8},{10,11... | collective-permute-start | bytes 3145736 | tf_op jit(solution)/shard_map/ppermute | solution.py:225
  38.7 3.3 %collective-permute-start.9 = (bf16[128,128]{1,0:T(8,128)(2,1)S(1)}, bf16[128,128]{1,0:T(8,128)(2,1)S(1)}, u32[]{:S(2)}, u32[]{:S(2)}) collective-permute-start(bf16[128,128]{1,0:T(8,128)(2,1)S(1)} %get-tuple-element.49.rest), channel_id=1, source_target_pairs={{0,32},{32,0},{64,96},{96,64},{128,160},{160,128},{192,224},{224,1... | collective-permute-start | bytes 98312 | tf_op jit(solution)/shard_map/ppermute | solution.py:228
  42.1 39.0 %all-gather = bf16[3840,128]{1,0:T(8,128)(2,1)S(1)} all-gather(bf16[240,128]{1,0:T(8,128)(2,1)S(1)} %get-tuple-element.48), channel_id=2, replica_groups=mesh['row'=16,'col'=16,'rep'=2] {'row'}, dimensions={0}, use_global_device_ids=true | all-gather | bytes 1044480 | tf_op jit(solution)/shard_map/all_gather | solution.py:229
  81.2 2.8 %right_tri.1 = (bf16[32,32,128]{2,1,0:T(8,128)(2,1)S(1)}, bf16[128,32,128]{2,1,0:T(8,128)(2,1)S(1)}) custom-call(s32[17]{0:T(128)S(1)} %pad_add_fusion.order, s32[32]{0:T(128)S(1)} %get-tuple-element.57.flags, bf16[16,240,128]{2,1,0:T(8,128)(2,1)S(1)} %bitcast.6, bf16[128,128]{1,0:T(8,128)(2,1)S(1)} %get-tuple-element.49.rest, ...), custom_call_target="tpu_custom_call" | custom-call | flops 536870912 | bytes 4194304 | tf_op jit(solution)/shard_map/right_tri/pallas_call | solution.py:137
  84.0 1.0 %copy-done.2 = bf16[128,32,128]{2,1,0:T(8,128)(2,1)} copy-done((bf16[128,32,128]{2,1,0:T(8,128)(2,1)}, bf16[128,32,128]{2,1,0:T(8,128)(2,1)S(1)}, u32[]{:S(2)}) %copy-start.2) | copy-done | bytes 1048600
  84.9 2.3 %collective-permute-start.11 = (bf16[32,32,128]{2,1,0:T(8,128)(2,1)S(1)}, bf16[32,32,128]{2,1,0:T(8,128)(2,1)S(1)}, u32[]{:S(2)}, u32[]{:S(2)}) collective-permute-start(bf16[32,32,128]{2,1,0:T(8,128)(2,1)S(1)} %get-tuple-element.54), channel_id=1, source_target_pairs={{0,1},{1,0},{2,3},{3,2},{4,5},{5,4},{6,7},{7,6},{8,9},{9,8},{10,11... | collective-permute-start | bytes 786440 | tf_op jit(solution)/shard_map/ppermute | solution.py:232
  87.3 1.2 %copy-done.3 = bf16[128,32,128]{2,1,0:T(8,128)(2,1)S(1)} copy-done((bf16[128,32,128]{2,1,0:T(8,128)(2,1)S(1)}, bf16[128,32,128]{2,1,0:T(8,128)(2,1)}, u32[]{:S(2)}) %copy-start.3) | copy-done | bytes 1048600
  88.5 1.9 %own_tri.1 = (f32[32,32,128]{2,1,0:T(8,128)S(1)}, f32[32,64,128]{2,1,0:T(8,128)S(1)}) custom-call(bf16[32,64,128]{2,1,0:T(8,128)(2,1)S(1)} %copy-done.1, bf16[128,128]{1,0:T(8,128)(2,1)S(1)} %copy-done.5, bf16[128,32,128]{2,1,0:T(8,128)(2,1)S(1)} %get-tuple-element.39.left, bf16[128,32,128]{2,1,0:T(8,128)(2,1)S(1)} %copy-done.3, bf16[128,128]{1,0:T(8,128)(2,1)S(1)} %copy-done.4), custom_call_target="tpu_custom_call" | custom-call | flops 268435456 | bytes 4194304 | tf_op jit(solution)/shard_map/own_tri/pallas_call | solution.py:164
  90.4 2.7 %collective-permute-done.11 = bf16[32,32,128]{2,1,0:T(8,128)(2,1)S(1)} collective-permute-done((bf16[32,32,128]{2,1,0:T(8,128)(2,1)S(1)}, bf16[32,32,128]{2,1,0:T(8,128)(2,1)S(1)}, u32[]{:S(2)}, u32[]{:S(2)}) %collective-permute-start.11) | collective-permute-done | bytes 262176 | tf_op jit(solution)/shard_map/ppermute | solution.py:232
  93.3 1.0 %fusion = bf16[32,64,128]{2,1,0:T(8,128)(2,1)} fusion(f32[32,64,128]{2,1,0:T(8,128)S(1)} %get-tuple-element.52, f32[32,32,128]{2,1,0:T(8,128)S(1)} %get-tuple-element.56, f32[32,32,128]{2,1,0:T(8,128)S(1)} %get-tuple-element.55), kind=kLoop, calls=%fused_computation.1 | loop fusion | flops 786432 | bytes 2621440 | tf_op jit(solution)/shard_map/convert_element_type | solution.py:237
  (38 shorter events, 1.5 us)
Async XLA Ops:
  0.0 30.4 %collective-permute-start = (bf16[2048,128]{1,0:T(8,128)(2,1)}, bf16[2048,128]{1,0:T(8,128)(2,1)S(1)}, u32[]{:S(2)}, u32[]{:S(2)}) collective-permute-start(bf16[2048,128]{1,0:T(8,128)(2,1)} %bitcast.7), channel_id=1, source_target_pairs={{0,30},{2,0},{4,2},{6,4},{8,6},{10,8},{12,10},{14,12},{16,14},{18,... | collective-permute-start | bytes 1572872 | tf_op jit(solution)/shard_map/ppermute | solution.py:214
  1.9 1.1 %copy-start = (bf16[32,64,128]{2,1,0:T(8,128)(2,1)S(1)}, bf16[32,64,128]{2,1,0:T(8,128)(2,1)}, u32[]{:S(2)}) copy-start(bf16[32,64,128]{2,1,0:T(8,128)(2,1)} %x.3) | copy-start | bytes 1572868
  3.0 27.4 %copy-start.1 = (bf16[32,64,128]{2,1,0:T(8,128)(2,1)S(1)}, bf16[32,64,128]{2,1,0:T(8,128)(2,1)}, u32[]{:S(2)}) copy-start(bf16[32,64,128]{2,1,0:T(8,128)(2,1)} %x.3) | copy-start | bytes 1572868
  3.0 3.0 %collective-permute-start.1 = (bf16[368,128]{1,0:T(8,128)(2,1)S(1)}, bf16[368,128]{1,0:T(8,128)(2,1)S(1)}, u32[]{:S(2)}, u32[]{:S(2)}) collective-permute-start(bf16[368,128]{1,0:T(8,128)(2,1)S(1)} %get-tuple-element.30), channel_id=1, source_target_pairs={{0,256},{34,290},{68,324},{102,358},{136,392},{170,426},{204,460},... | collective-permute-start | bytes 282632 | tf_op jit(solution)/shard_map/ppermute | solution.py:213
  3.8 2.1 %copy-start.10 = (s32[1024]{0:T(1024)S(1)}, s32[1024]{0:T(1024)}, u32[]{:S(2)}) copy-start(s32[1024]{0:T(1024)} %param.10) | copy-start | bytes 12292
  3.9 5.5 %slice-start = ((s32[1024]{0:T(1024)}), s32[64]{0:T(128)S(1)}, s32[]{:S(2)}) async-start(s32[1024]{0:T(1024)} %param.10), calls=%async_computation | async-start | bytes 1024 | tf_op jit(solution)/shard_map/slice | solution.py:219
  3.9 2.8 %collective-permute-start.2 = (bf16[368,128]{1,0:T(8,128)(2,1)S(1)}, bf16[368,128]{1,0:T(8,128)(2,1)S(1)}, u32[]{:S(2)}, u32[]{:S(2)}) collective-permute-start(bf16[368,128]{1,0:T(8,128)(2,1)S(1)} %get-tuple-element.31), channel_id=1, source_target_pairs={{0,192},{34,226},{68,260},{102,294},{136,328},{170,362},{204,396},... | collective-permute-start | bytes 282632 | tf_op jit(solution)/shard_map/ppermute | solution.py:213
  4.5 3.5 %collective-permute-start.3 = (bf16[368,128]{1,0:T(8,128)(2,1)S(1)}, bf16[368,128]{1,0:T(8,128)(2,1)S(1)}, u32[]{:S(2)}, u32[]{:S(2)}) collective-permute-start(bf16[368,128]{1,0:T(8,128)(2,1)S(1)} %get-tuple-element.32), channel_id=1, source_target_pairs={{0,320},{34,354},{68,388},{102,422},{136,456},{170,490},{204,12},{... | collective-permute-start | bytes 282632 | tf_op jit(solution)/shard_map/ppermute | solution.py:213
  5.2 3.5 %collective-permute-start.4 = (bf16[368,128]{1,0:T(8,128)(2,1)S(1)}, bf16[368,128]{1,0:T(8,128)(2,1)S(1)}, u32[]{:S(2)}, u32[]{:S(2)}) collective-permute-start(bf16[368,128]{1,0:T(8,128)(2,1)S(1)} %get-tuple-element.33), channel_id=1, source_target_pairs={{0,128},{34,162},{68,196},{102,230},{136,264},{170,298},{204,332},... | collective-permute-start | bytes 282632 | tf_op jit(solution)/shard_map/ppermute | solution.py:213
  5.9 24.5 %copy-start.7 = (bf16[128,128]{1,0:T(8,128)(2,1)S(1)}, bf16[128,128]{1,0:T(8,128)(2,1)}, u32[]{:S(2)}) copy-start(bf16[128,128]{1,0:T(8,128)(2,1)} %w_gate.2) | copy-start | bytes 98308
  5.9 24.5 %copy-start.6 = (bf16[128,128]{1,0:T(8,128)(2,1)S(1)}, bf16[128,128]{1,0:T(8,128)(2,1)}, u32[]{:S(2)}) copy-start(bf16[128,128]{1,0:T(8,128)(2,1)} %w.1) | copy-start | bytes 98308
  6.0 3.4 %collective-permute-start.5 = (bf16[368,128]{1,0:T(8,128)(2,1)S(1)}, bf16[368,128]{1,0:T(8,128)(2,1)S(1)}, u32[]{:S(2)}, u32[]{:S(2)}) collective-permute-start(bf16[368,128]{1,0:T(8,128)(2,1)S(1)} %get-tuple-element.34), channel_id=1, source_target_pairs={{0,384},{34,418},{68,452},{102,486},{136,8},{170,42},{204,76},{238... | collective-permute-start | bytes 282632 | tf_op jit(solution)/shard_map/ppermute | solution.py:213
  6.7 23.7 %collective-permute-start.6 = (bf16[368,128]{1,0:T(8,128)(2,1)S(1)}, bf16[368,128]{1,0:T(8,128)(2,1)S(1)}, u32[]{:S(2)}, u32[]{:S(2)}) collective-permute-start(bf16[368,128]{1,0:T(8,128)(2,1)S(1)} %get-tuple-element.35), channel_id=1, source_target_pairs={{0,64},{34,98},{68,132},{102,166},{136,200},{170,234},{204,268},{2... | collective-permute-start | bytes 282632 | tf_op jit(solution)/shard_map/ppermute | solution.py:213
  8.0 22.4 %collective-permute-start.7 = (bf16[368,128]{1,0:T(8,128)(2,1)S(1)}, bf16[368,128]{1,0:T(8,128)(2,1)S(1)}, u32[]{:S(2)}, u32[]{:S(2)}) collective-permute-start(bf16[368,128]{1,0:T(8,128)(2,1)S(1)} %get-tuple-element.36), channel_id=1, source_target_pairs={{0,448},{34,482},{68,4},{102,38},{136,72},{170,106},{204,140},{238... | collective-permute-start | bytes 282632 | tf_op jit(solution)/shard_map/ppermute | solution.py:213
  8.7 21.7 %collective-permute-start.8 = (bf16[368,128]{1,0:T(8,128)(2,1)S(1)}, bf16[368,128]{1,0:T(8,128)(2,1)S(1)}, u32[]{:S(2)}, u32[]{:S(2)}) collective-permute-start(bf16[368,128]{1,0:T(8,128)(2,1)S(1)} %get-tuple-element.37), channel_id=1, source_target_pairs={{0,0},{34,34},{68,68},{102,102},{136,136},{170,170},{204,204},{238... | collective-permute-start | bytes 282632 | tf_op jit(solution)/shard_map/ppermute | solution.py:213
  30.4 0.8 copy-start.8
  31.2 0.8 copy-start.9
  34.1 47.0 %collective-permute-start.10 = (bf16[128,32,128]{2,1,0:T(8,128)(2,1)S(1)}, bf16[128,32,128]{2,1,0:T(8,128)(2,1)S(1)}, u32[]{:S(2)}, u32[]{:S(2)}) collective-permute-start(bf16[128,32,128]{2,1,0:T(8,128)(2,1)S(1)} %get-tuple-element.39.left), channel_id=1, source_target_pairs={{0,1},{1,0},{2,3},{3,2},{4,5},{5,4},{6,7},{7,6},{8,9},{9,8},{10,11... | collective-permute-start | bytes 3145736 | tf_op jit(solution)/shard_map/ppermute | solution.py:225
  38.7 42.4 %collective-permute-start.9 = (bf16[128,128]{1,0:T(8,128)(2,1)S(1)}, bf16[128,128]{1,0:T(8,128)(2,1)S(1)}, u32[]{:S(2)}, u32[]{:S(2)}) collective-permute-start(bf16[128,128]{1,0:T(8,128)(2,1)S(1)} %get-tuple-element.49.rest), channel_id=1, source_target_pairs={{0,32},{32,0},{64,96},{96,64},{128,160},{160,128},{192,224},{224,1... | collective-permute-start | bytes 98312 | tf_op jit(solution)/shard_map/ppermute | solution.py:228
  42.1 39.1 %copy-start.4 = (bf16[128,128]{1,0:T(8,128)(2,1)S(1)}, bf16[128,128]{1,0:T(8,128)(2,1)}, u32[]{:S(2)}) copy-start(bf16[128,128]{1,0:T(8,128)(2,1)} %w_out.3) | copy-start | bytes 98308
  81.2 6.1 %copy-start.5 = (bf16[128,128]{1,0:T(8,128)(2,1)S(1)}, bf16[128,128]{1,0:T(8,128)(2,1)}, u32[]{:S(2)}) copy-start(bf16[128,128]{1,0:T(8,128)(2,1)} %w_gate.3) | copy-start | bytes 98308
  84.0 1.0 %copy-start.2 = (bf16[128,32,128]{2,1,0:T(8,128)(2,1)}, bf16[128,32,128]{2,1,0:T(8,128)(2,1)S(1)}, u32[]{:S(2)}) copy-start(bf16[128,32,128]{2,1,0:T(8,128)(2,1)S(1)} %get-tuple-element.51.right) | copy-start | bytes 3145732
  84.9 8.3 %collective-permute-start.11 = (bf16[32,32,128]{2,1,0:T(8,128)(2,1)S(1)}, bf16[32,32,128]{2,1,0:T(8,128)(2,1)S(1)}, u32[]{:S(2)}, u32[]{:S(2)}) collective-permute-start(bf16[32,32,128]{2,1,0:T(8,128)(2,1)S(1)} %get-tuple-element.54), channel_id=1, source_target_pairs={{0,1},{1,0},{2,3},{3,2},{4,5},{5,4},{6,7},{7,6},{8,9},{9,8},{10,11... | collective-permute-start | bytes 786440 | tf_op jit(solution)/shard_map/ppermute | solution.py:232
  87.3 1.2 %copy-start.3 = (bf16[128,32,128]{2,1,0:T(8,128)(2,1)S(1)}, bf16[128,32,128]{2,1,0:T(8,128)(2,1)}, u32[]{:S(2)}) copy-start(bf16[128,32,128]{2,1,0:T(8,128)(2,1)} %copy-done.2) | copy-start | bytes 3145732
  (1 other events, 0.7 us)

commit v4 on v3

--- a/solution.py
+++ b/solution.py
@@ -10,6 +10,7 @@
 EPS = 1e-5
 VMEM = pl.BlockSpec(memory_space=pltpu.VMEM)
 SMEM = pl.BlockSpec(memory_space=pltpu.SMEM)
+HBM = pl.BlockSpec(memory_space=pl.ANY)
 F32 = jnp.float32
 BF16 = jnp.bfloat16
 GROUP = 16
@@ -44,54 +45,50 @@
     return jnp.concatenate(parts, axis=1).reshape(hid, len(masks), width).astype(BF16)
 
 
-def left_kernel(flags, x, x_next, mask_k, w, w_gate, v, v_gate, out, wt_right):
+def left_kernel(flags, x, x_next, mask_k, weights, out):
     half = x.shape[0]
-    weights = jnp.concatenate([halved_transpose(w), halved_transpose(w_gate)])
-    wt_right[...] = jnp.concatenate([halved_transpose(v), halved_transpose(v_gate)])
     for q in range(0, half, GROUP):
         blocks = [part[i] for i in range(q, q + GROUP) for part in (x, x_next)]
         masks = [mask_k[...] * flags[i].astype(F32) for i in range(q, q + GROUP)]
-        out[:, q : q + GROUP, :] = gated(weights, normalise(jnp.concatenate(blocks)), masks)
-
-
-def left_call(flags, x, x_next, mask_k, *ws):
+        out[:, q : q + GROUP, :] = gated(weights[...], normalise(jnp.concatenate(blocks)), masks)
+
+
+def left_call(flags, x, x_next, mask_k, weights):
     half, tile, chans = x.shape
-    hid = ws[0].shape[1]
+    hid = weights.shape[0] // 2
     return pl.pallas_call(
         left_kernel,
-        out_shape=(
-            jax.ShapeDtypeStruct((hid, half, 2 * tile), BF16),
-            jax.ShapeDtypeStruct((2 * hid, chans), BF16),
-        ),
-        in_specs=[SMEM] + [VMEM] * 7,
-        out_specs=(VMEM, VMEM),
+        out_shape=jax.ShapeDtypeStruct((hid, half, 2 * tile), BF16),
+        in_specs=[SMEM] + [VMEM] * 4,
+        out_specs=VMEM,
         compiler_params=pltpu.CompilerParams(vmem_limit_bytes=LIMIT),
         name="left",
         cost_estimate=pl.CostEstimate(flops=10 * half * tile * 2 * chans * hid, bytes_accessed=2 << 20, transcendentals=4 * half * tile * hid),
-    )(flags, x, x_next, mask_k, *ws)
+    )(flags, x, x_next, mask_k, weights)
 
 
 def chunk_kernel(piece, *refs):
-    *got, out, rest = refs
+    *got, passed, out, rest = refs
     total = got[0][...]
     for g in got[1:]:
         total = total + g[...]
-    normed = normalise(total)
+    own = jnp.concatenate([total[:piece], total[2 * piece :]])
+    normed = normalise(own + passed[...])
     out[...] = normed[:piece]
     rest[...] = normed[piece:]
 
 
-def chunk_call(got, piece):
-    n, chans = got[0].shape
+def chunk_call(got, passed, piece):
+    n, chans = passed.shape
     return pl.pallas_call(
         functools.partial(chunk_kernel, piece),
         out_shape=(jax.ShapeDtypeStruct((piece, chans), BF16), jax.ShapeDtypeStruct((n - piece, chans), BF16)),
-        in_specs=[VMEM] * len(got),
+        in_specs=[VMEM] * (len(got) + 1),
         out_specs=(VMEM, VMEM),
         compiler_params=pltpu.CompilerParams(vmem_limit_bytes=LIMIT),
         name="chunk",
         cost_estimate=pl.CostEstimate(flops=4 * n * chans * chans, bytes_accessed=1 << 20, transcendentals=n * chans),
-    )(*got)
+    )(*got, passed)
 
 
 def tri_projected(left, right, w_out, held, store):
@@ -110,40 +107,49 @@
             store(i + u, projected[u * half : (u + 1) * half])
 
 
-def right_kernel(order, flags, gathered, rest, rest_other, mask_k, weights, left, w_out, out, right, tiles, held):
+def right_kernel(offsets, place, flags, gathered, rest, rest_other, mask_k, weights, left, w_out, out, right_out, tiles, right, held, sem):
     shards, piece, chans = gathered.shape
     hid, half, width = left.shape
     tile = width // 2
     kept = shards // 2 * piece
-    for s in range(shards // 2):
-        for t in range(2):
-            tiles[t, s * piece : (s + 1) * piece] = gathered[order[2 * s + t]]
-    tiles[order[shards], kept:] = rest[...]
-    tiles[1 - order[shards], kept:] = rest_other[...]
+    for t in range(2):
+        for s, offset in enumerate(offsets[t]):
+            shard = lax.rem(place[0] + offset % shards, shards)
+            tiles[t, s * piece : (s + 1) * piece] = gathered[shard]
+    tiles[place[1], kept:] = rest[...]
+    tiles[1 - place[1], kept:] = rest_other[...]
     for q in range(0, half, GROUP):
         blocks = [tiles[t, j * tile : (j + 1) * tile] for j in range(q, q + GROUP) for t in range(2)]
         masks = [mask_k[...] * flags[j].astype(F32) for j in range(q, q + GROUP)]
         right[:, q : q + GROUP, :] = gated(weights[...], jnp.concatenate(blocks), masks)
+    copy = pltpu.make_async_copy(right, right_out, sem)
+    copy.start()
 
     def store(i, rows):
         out[i] = rows.astype(BF16)
 
     tri_projected(left, right, w_out, held, store)
-
-
-def right_call(order, flags, gathered, rest, rest_other, mask_k, weights, left, w_out):
+    copy.wait()
+
+
+def right_call(offsets, place, flags, gathered, rest, rest_other, mask_k, weights, left, w_out):
     hid, half, width = left.shape
     chans = gathered.shape[-1]
     return pl.pallas_call(
-        right_kernel,
+        functools.partial(right_kernel, offsets),
         out_shape=(jax.ShapeDtypeStruct((half, half, chans), BF16), jax.ShapeDtypeStruct((hid, half, width), BF16)),
         in_specs=[SMEM] * 2 + [VMEM] * 7,
-        out_specs=(VMEM, VMEM),
-        scratch_shapes=[pltpu.VMEM((2, half * width // 2, chans), BF16), pltpu.VMEM((half, hid, half), F32)],
+        out_specs=(VMEM, pl.BlockSpec(memory_space=pltpu.HBM)),
+        scratch_shapes=[
+            pltpu.VMEM((2, half * width // 2, chans), BF16),
+            pltpu.VMEM((hid, half, width), BF16),
+            pltpu.VMEM((half, hid, half), F32),
+            pltpu.SemaphoreType.DMA,
+        ],
         compiler_params=pltpu.CompilerParams(vmem_limit_bytes=LIMIT),
         name="right_tri",
         cost_estimate=pl.CostEstimate(flops=8 * half * width * chans * hid, bytes_accessed=4 << 20, transcendentals=half * width * hid),
-    )(order, flags, gathered, rest, rest_other, mask_k, weights, left, w_out)
+    )(place, flags, gathered, rest, rest_other, mask_k, weights, left, w_out)
 
 
 def own_kernel(x, w_gate, left, right, w_out, out, gate, held):
@@ -173,25 +179,46 @@
     )(x, w_gate, left, right, w_out)
 
 
-def messages_kernel(kept, piece, flat, *outs):
+def first_kernel(sends, kept, *refs):
+    flat, *ws = refs[:7]
+    outs, (wt_left, wt_right, w_gate, w_out), held = refs[7 : 7 + sends], refs[7 + sends : 11 + sends], refs[11 + sends]
+    sems = refs[-1]
+    size = kept // sends
+    copies = []
+    for i, w in enumerate(ws):
+        dst = (held.at[0], held.at[1], held.at[2], held.at[3], w_gate, w_out)[i]
+        copies.append(pltpu.make_async_copy(w, dst, sems.at[i]))
     for s, out in enumerate(outs):
-        out[:piece] = flat[s * piece : (s + 1) * piece]
-        out[piece:] = flat[kept:]
-
-
-def messages_call(flat, kept, sends):
+        copies.append(pltpu.make_async_copy(flat.at[s * size : (s + 1) * size], out.at[:size], sems.at[6 + 2 * s]))
+        copies.append(pltpu.make_async_copy(flat.at[kept:], out.at[size:], sems.at[7 + 2 * s]))
+    for copy in copies:
+        copy.start()
+    for copy in copies[:6]:
+        copy.wait()
+    hid = held.shape[1]
+    for i, wt in enumerate((wt_left, wt_right)):
+        wt[:hid] = halved_transpose(held.at[2 * i])
+        wt[hid:] = halved_transpose(held.at[2 * i + 1])
+    for copy in copies[6:]:
+        copy.wait()
+
+
+def first_call(flat, sends, kept, *ws):
     rows, chans = flat.shape
-    piece = kept // sends
-    shape = jax.ShapeDtypeStruct((piece + rows - kept, chans), flat.dtype)
-    return pl.pallas_call(
-        functools.partial(messages_kernel, kept, piece),
-        out_shape=(shape,) * sends,
-        in_specs=[VMEM],
-        out_specs=(VMEM,) * sends,
-        compiler_params=pltpu.CompilerParams(vmem_limit_bytes=LIMIT),
-        name="messages",
+    hid = ws[0].shape[1]
+    message = jax.ShapeDtypeStruct((kept // sends + rows - kept, chans), flat.dtype)
+    weights = jax.ShapeDtypeStruct((2 * hid, chans), BF16)
+    square = jax.ShapeDtypeStruct((chans, hid), BF16)
+    return pl.pallas_call(
+        functools.partial(first_kernel, sends, kept),
+        out_shape=(message,) * sends + (weights, weights, square, square),
+        in_specs=[HBM] * 7,
+        out_specs=(VMEM,) * (sends + 4),
+        scratch_shapes=[pltpu.VMEM((4, chans, hid), BF16), pltpu.SemaphoreType.DMA((6 + 2 * sends,))],
+        compiler_params=pltpu.CompilerParams(vmem_limit_bytes=LIMIT),
+        name="first",
         cost_estimate=pl.CostEstimate(flops=0, bytes_accessed=2 << 20, transcendentals=0),
-    )(flat)
+    )(flat, *ws)
 
 
 def per_device(pair_rep, token_mask, w_a, w_a_gate, w_b, w_b_gate, w_gate, w_out):
@@ -201,34 +228,42 @@
     swap = [(p, 1 - p) for p in range(reps)]
     flat = pair_rep.reshape(-1, chans)
 
-    sends = rows // 2
     kept = flat.shape[0] // rows * (rows - 1)
-    piece = kept // sends
-    even = [8, 6, -6, 4, -4, 2, -2, 0]
-    odd = [7, -7, 5, -5, 3, -3, 1, -1]
+    piece = kept // 8
+    near = ((4, -2, 2, 0), (-3, 3, 1, -1))
+    far = ((8, -6, 6, -4), (-7, 7, 5, -5))
+    *messages, wt_left, wt_right, w_gate, w_out = first_call(flat, 4, kept, w_a, w_a_gate, w_b, w_b_gate, w_gate, w_out)
     got = []
-    for s, message in enumerate(messages_call(flat, kept, sends)):
-        pairs = [(c * cols + c, (c + even[s]) % rows * cols + c) for c in range(cols)]
-        pairs += [(c * cols + (c + 1) % cols, (c + odd[s]) % rows * cols + c) for c in range(cols)]
+    for s, message in enumerate(messages):
+        pairs = [(c * cols + c, (c + near[0][s]) % rows * cols + c) for c in range(cols)]
+        pairs += [(c * cols + (c + 1) % cols, (c + near[1][s]) % rows * cols + c) for c in range(cols)]
         got.append(lax.ppermute(message, ("row", "col"), pairs))
     x_next = lax.ppermute(flat, "col", [(c, (c - 1) % cols) for c in range(cols)])
-    x_next, got = lax.optimization_barrier((x_next, got))
-    order = jnp.array([o % rows for pair in zip(even, odd) for o in pair], jnp.int32)
-    order = jnp.concatenate([(order + col) % rows, (row + col).reshape(1) % 2])
+    onward = got[0][piece:] + got[1][piece:] + got[2][piece:] + got[3][piece:]
+    pairs = [
+        ((c + n) % rows * cols + c, (c + f) % rows * cols + c)
+        for c in range(cols)
+        for t in range(2)
+        for n, f in zip(near[t], far[t])
+    ]
+    passed = lax.ppermute(onward, ("row", "col"), pairs)
+    offsets = tuple(tuple(o for pair in zip(near[t], far[t]) for o in pair) for t in range(2))
+    place = jnp.stack([col, (row + col) % 2]).astype(jnp.int32)
 
     wrapped = jnp.concatenate([token_mask, token_mask[:tile]])
     mask_k = lax.dynamic_slice_in_dim(wrapped, col * tile, 2 * tile, 0).astype(F32).reshape(1, -1)
     mask_i = lax.dynamic_slice_in_dim(token_mask, row * tile + rep * half, half, 0)
     mask_j = lax.dynamic_slice_in_dim(token_mask, col * tile + rep * half, half, 0)
 
-    left, wt_right = left_call(mask_i, pair_rep, x_next.reshape(half, tile, chans), mask_k, w_a, w_a_gate, w_b, w_b_gate)
+    x_next, passed = lax.optimization_barrier((x_next, passed))
+    left = left_call(mask_i, pair_rep, x_next.reshape(half, tile, chans), mask_k, wt_left)
     other = lax.ppermute(left, "rep", swap)
 
-    chunk, rest = chunk_call(got, piece)
+    chunk, rest = chunk_call(got, passed, piece)
     rest_other = lax.ppermute(rest, "row", [(r, r ^ 1) for r in range(rows)])
     gathered = lax.all_gather(chunk, "row", axis=0, tiled=False)
 
-    theirs, right = right_call(order, mask_j, gathered, rest, rest_other, mask_k, wt_right, other, w_out)
+    theirs, right = right_call(offsets, place, mask_j, gathered, rest, rest_other, mask_k, wt_right, other, w_out)
     received = lax.ppermute(theirs, "rep", swap)
     ours, gate = own_call(pair_rep, w_gate, left, right, w_out)
     received = received.astype(F32)

time: 95 us -> 101 us (1.063)
  the two profiles are of different devices: /device:TPU:36 before, /device:TPU:6 now
where the time goes in v4:
time: 101 us; the launch traced here: 100 us
  blocking collectives  40.1 us (40%)
  waiting for transfers between devices  25.6 us (25%)
  starting transfers between devices  15.9 us (16%)
  Pallas kernels  8.74 us (9%)
  local copies, waits for them, and re-layouts  8.58 us (8%)
  other arithmetic  1.28 us (1%)
    all_gather x1, blocking collectives, per_device(): gathered = lax.all_gather(chunk, 'row', axis=0, tiled=False)  40.1 us
    ppermute x1, waiting for transfers between devices, per_device(): passed = lax.ppermute(onward, ('row', 'col'), pairs)  22.8 us
    unnamed x24, local copies, waits for them, and re-layouts  8.5 us
    ppermute x1, starting transfers between devices, per_device(): rest_other = lax.ppermute(rest, 'row', [(r, r ^ 1) for r in range(rows)])  3.84 us
    ppermute x1, starting transfers between devices, per_device(): other = lax.ppermute(left, 'rep', swap)  3.49 us
    pallas_call x1, Pallas kernels, right_call(): pl.pallas_call(functools.partial(right_kernel, offsets), out_shape=(jax.S...  2.95 us
    ppermute x1, waiting for transfers between devices, per_device(): received = lax.ppermute(theirs, 'rep', swap)  2.69 us
    ppermute x4, starting transfers between devices, per_device(): got.append(lax.ppermute(message, ('row', 'col'), pairs))  2.68 us
  transfers between devices with their start and end apart: 9, of which 2 were waited for; matrix products, arithmetic and copies ran while one was open for 0% of the time, Pallas kernels for 4%

profile of v4, /device:TPU:6, one launch (start us, length us, event | category | flops | bytes accessed | tf_op | source)
XLA Modules:
  0.0 100.4 jit_solution(1265514573854576737)
XLA Ops:
  0.0 2.2 %collective-permute-start = (bf16[2048,128]{1,0:T(8,128)(2,1)}, bf16[2048,128]{1,0:T(8,128)(2,1)S(1)}, u32[]{:S(2)}, u32[]{:S(2)}) collective-permute-start(bf16[2048,128]{1,0:T(8,128)(2,1)} %bitcast.8), channel_id=1, source_target_pairs={{0,30},{2,0},{4,2},{6,4},{8,6},{10,8},{12,10},{14,12},{16,14},{18,... | collective-permute-start | bytes 1572872 | tf_op jit(solution)/shard_map/ppermute | solution.py:241
  2.2 1.0 %copy-done = bf16[32,64,128]{2,1,0:T(8,128)(2,1)S(1)} copy-done((bf16[32,64,128]{2,1,0:T(8,128)(2,1)S(1)}, bf16[32,64,128]{2,1,0:T(8,128)(2,1)}, u32[]{:S(2)}) %copy-start) | copy-done | bytes 524312
  3.2 0.8 copy-done.4
  4.0 0.8 copy-done.5
  4.7 0.8 copy-done.6
  5.5 0.8 copy-done.7
  6.3 0.8 copy-done.8
  7.0 0.8 copy-done.9
  7.8 1.3 %first.1 = (bf16[608,128]{1,0:T(8,128)(2,1)S(1)}, bf16[608,128]{1,0:T(8,128)(2,1)S(1)}, bf16[608,128]{1,0:T(8,128)(2,1)S(1)}, bf16[608,128]{1,0:T(8,128)(2,1)S(1...) custom-call(bf16[2048,128]{1,0:T(8,128)(2,1)S(1)} %bitcast.9, ...), custom_call_target="tpu_custom_call" | custom-call | bytes 2097152 | tf_op jit(solution)/shard_map/first/pallas_call | solution.py:212
  9.1 0.7 collective-permute-start.1
  11.8 0.7 copy-done.10
  12.6 1.3 %collective-permute-start.5 = (bf16[368,128]{1,0:T(8,128)(2,1)S(1)}, bf16[368,128]{1,0:T(8,128)(2,1)S(1)}, u32[]{:S(2)}, u32[]{:S(2)}) collective-permute-start(bf16[368,128]{1,0:T(8,128)(2,1)S(1)} %slice_add_fusion), channel_id=1, source_target_pairs={{128,256},{448,320},{64,192},{0,384},{416,288},{96,224},{32,160},{... | collective-permute-start | bytes 282632 | tf_op jit(solution)/shard_map/ppermute | solution.py:249
  14.0 22.8 %collective-permute-done.5.refs_4_ = bf16[368,128]{1,0:T(8,128)(2,1)S(1)} collective-permute-done((bf16[368,128]{1,0:T(8,128)(2,1)S(1)}, bf16[368,128]{1,0:T(8,128)(2,1)S(1)}, u32[]{:S(2)}, u32[]{:S(2)}) %collective-permute-start.5) | collective-permute-done | bytes 94240 | tf_op jit(solution)/shard_map/ppermute | solution.py:249
  36.9 2.2 %left.1 = bf16[128,32,128]{2,1,0:T(8,128)(2,1)S(1)} custom-call(s32[32]{0:T(128)S(1)} %get-tuple-element.40.flags, bf16[32,64,128]{2,1,0:T(8,128)(2,1)S(1)} %copy-done.1, bf16[32,64,128]{2,1,0:T(8,128)(2,1)S(1)} %bitcast.10, f32[1,128]{1,0:T(1,128)S(1)} %convert_bitcast_fusion.mask_k, bf16[256,128]{1,0:T(8,128)(2,1)S(1)} %get-tuple-element.27.weights), custom_call_target="tpu_custom_call" | custom-call | flops 671088640 | bytes 2097152 | tf_op jit(solution)/shard_map/left/pallas_call | solution.py:59
  39.1 3.5 %collective-permute-start.7 = (bf16[128,32,128]{2,1,0:T(8,128)(2,1)S(1)}, bf16[128,32,128]{2,1,0:T(8,128)(2,1)S(1)}, u32[]{:S(2)}, u32[]{:S(2)}) collective-permute-start(bf16[128,32,128]{2,1,0:T(8,128)(2,1)S(1)} %left.1), channel_id=1, source_target_pairs={{0,1},{1,0},{2,3},{3,2},{4,5},{5,4},{6,7},{7,6},{8,9},{9,8},{10,11... | collective-permute-start | bytes 3145736 | tf_op jit(solution)/shard_map/ppermute | solution.py:260
  43.1 3.8 %collective-permute-start.6 = (bf16[128,128]{1,0:T(8,128)(2,1)S(1)}, bf16[128,128]{1,0:T(8,128)(2,1)S(1)}, u32[]{:S(2)}, u32[]{:S(2)}) collective-permute-start(bf16[128,128]{1,0:T(8,128)(2,1)S(1)} %get-tuple-element.30.rest), channel_id=1, source_target_pairs={{0,32},{32,0},{64,96},{96,64},{128,160},{160,128},{192,224},{224,1... | collective-permute-start | bytes 98312 | tf_op jit(solution)/shard_map/ppermute | solution.py:263
  46.9 40.1 %all-gather = bf16[3840,128]{1,0:T(8,128)(2,1)S(1)} all-gather(bf16[240,128]{1,0:T(8,128)(2,1)S(1)} %get-tuple-element.29), channel_id=2, replica_groups=mesh['row'=16,'col'=16,'rep'=2] {'row'}, dimensions={0}, use_global_device_ids=true | all-gather | bytes 1044480 | tf_op jit(solution)/shard_map/all_gather | solution.py:264
  87.1 3.0 %right_tri.1 = (bf16[32,32,128]{2,1,0:T(8,128)(2,1)S(1)}, bf16[128,32,128]{2,1,0:T(8,128)(2,1)S(1)}) custom-call(s32[2]{0:T(128)S(1)} %pad_add_fusion.place, s32[32]{0:T(128)S(1)} %get-tuple-element.39.flags, bf16[16,240,128]{2,1,0:T(8,128)(2,1)S(1)} %bitcast.7, bf16[128,128]{1,0:T(8,128)(2,1)S(1)} %get-tuple-element.30.rest, ...), custom_call_target="tpu_custom_call" | custom-call | flops 536870912 | bytes 4194304 | tf_op jit(solution)/shard_map/right_tri/pallas_call | solution.py:138
  90.0 1.0 copy-done.2
  91.0 2.4 %collective-permute-start.8 = (bf16[32,32,128]{2,1,0:T(8,128)(2,1)S(1)}, bf16[32,32,128]{2,1,0:T(8,128)(2,1)S(1)}, u32[]{:S(2)}, u32[]{:S(2)}) collective-permute-start(bf16[32,32,128]{2,1,0:T(8,128)(2,1)S(1)} %get-tuple-element.36), channel_id=1, source_target_pairs={{0,1},{1,0},{2,3},{3,2},{4,5},{5,4},{6,7},{7,6},{8,9},{9,8},{10,11... | collective-permute-start | bytes 786440 | tf_op jit(solution)/shard_map/ppermute | solution.py:267
  93.5 1.2 %copy-done.3 = bf16[128,32,128]{2,1,0:T(8,128)(2,1)S(1)} copy-done((bf16[128,32,128]{2,1,0:T(8,128)(2,1)S(1)}, bf16[128,32,128]{2,1,0:T(8,128)(2,1)}, u32[]{:S(2)}) %copy-start.3) | copy-done | bytes 1048600
  94.7 1.9 %own_tri.1 = (f32[32,32,128]{2,1,0:T(8,128)S(1)}, f32[32,64,128]{2,1,0:T(8,128)S(1)}) custom-call(bf16[32,64,128]{2,1,0:T(8,128)(2,1)S(1)} %copy-done.1, bf16[128,128]{1,0:T(8,128)(2,1)S(1)} %get-tuple-element.21.w_gate, bf16[128,32,128]{2,1,0:T(8,128)(2,1)S(1)} %left.1, bf16[128,32,128]{2,1,0:T(8,128)(2,1)S(1)} %copy-done.3, ...), custom_call_target="tpu_custom_call" | custom-call | flops 268435456 | bytes 4194304 | tf_op jit(solution)/shard_map/own_tri/pallas_call | solution.py:170
  96.6 2.7 %collective-permute-done.8 = bf16[32,32,128]{2,1,0:T(8,128)(2,1)S(1)} collective-permute-done((bf16[32,32,128]{2,1,0:T(8,128)(2,1)S(1)}, bf16[32,32,128]{2,1,0:T(8,128)(2,1)S(1)}, u32[]{:S(2)}, u32[]{:S(2)}) %collective-permute-start.8) | collective-permute-done | bytes 262176 | tf_op jit(solution)/shard_map/ppermute | solution.py:267
  99.4 1.0 fusion
  (32 shorter events, 2.8 us)
Async XLA Ops:
  0.0 36.9 %collective-permute-start = (bf16[2048,128]{1,0:T(8,128)(2,1)}, bf16[2048,128]{1,0:T(8,128)(2,1)S(1)}, u32[]{:S(2)}, u32[]{:S(2)}) collective-permute-start(bf16[2048,128]{1,0:T(8,128)(2,1)} %bitcast.8), channel_id=1, source_target_pairs={{0,30},{2,0},{4,2},{6,4},{8,6},{10,8},{12,10},{14,12},{16,14},{18,... | collective-permute-start | bytes 1572872 | tf_op jit(solution)/shard_map/ppermute | solution.py:241
  2.2 1.1 %copy-start = (bf16[32,64,128]{2,1,0:T(8,128)(2,1)S(1)}, bf16[32,64,128]{2,1,0:T(8,128)(2,1)}, u32[]{:S(2)}) copy-start(bf16[32,64,128]{2,1,0:T(8,128)(2,1)} %x.3) | copy-start | bytes 1572868
  3.2 0.8 copy-start.4
  4.0 0.8 copy-start.5
  4.7 0.8 copy-start.6
  5.5 0.8 copy-start.7
  6.3 0.8 copy-start.8
  7.0 0.8 copy-start.9
  7.8 29.1 %copy-start.1 = (bf16[32,64,128]{2,1,0:T(8,128)(2,1)S(1)}, bf16[32,64,128]{2,1,0:T(8,128)(2,1)}, u32[]{:S(2)}) copy-start(bf16[32,64,128]{2,1,0:T(8,128)(2,1)} %x.3) | copy-start | bytes 1572868
  9.1 3.5 %collective-permute-start.1 = (bf16[608,128]{1,0:T(8,128)(2,1)S(1)}, bf16[608,128]{1,0:T(8,128)(2,1)S(1)}, u32[]{:S(2)}, u32[]{:S(2)}) collective-permute-start(bf16[608,128]{1,0:T(8,128)(2,1)S(1)} %get-tuple-element.22), channel_id=1, source_target_pairs={{0,128},{34,162},{68,196},{102,230},{136,264},{170,298},{204,332},... | collective-permute-start | bytes 466952 | tf_op jit(solution)/shard_map/ppermute | solution.py:240
  9.7 2.8 %collective-permute-start.2 = (bf16[608,128]{1,0:T(8,128)(2,1)S(1)}, bf16[608,128]{1,0:T(8,128)(2,1)S(1)}, u32[]{:S(2)}, u32[]{:S(2)}) collective-permute-start(bf16[608,128]{1,0:T(8,128)(2,1)S(1)} %get-tuple-element.23), channel_id=1, source_target_pairs={{0,448},{34,482},{68,4},{102,38},{136,72},{170,106},{204,140},{238... | collective-permute-start | bytes 466952 | tf_op jit(solution)/shard_map/ppermute | solution.py:240
  10.4 2.2 %collective-permute-start.3 = (bf16[608,128]{1,0:T(8,128)(2,1)S(1)}, bf16[608,128]{1,0:T(8,128)(2,1)S(1)}, u32[]{:S(2)}, u32[]{:S(2)}) collective-permute-start(bf16[608,128]{1,0:T(8,128)(2,1)S(1)} %get-tuple-element.24), channel_id=1, source_target_pairs={{0,64},{34,98},{68,132},{102,166},{136,200},{170,234},{204,268},{2... | collective-permute-start | bytes 466952 | tf_op jit(solution)/shard_map/ppermute | solution.py:240
  11.1 1.5 %collective-permute-start.4 = (bf16[608,128]{1,0:T(8,128)(2,1)S(1)}, bf16[608,128]{1,0:T(8,128)(2,1)S(1)}, u32[]{:S(2)}, u32[]{:S(2)}) collective-permute-start(bf16[608,128]{1,0:T(8,128)(2,1)S(1)} %get-tuple-element.25), channel_id=1, source_target_pairs={{0,0},{34,34},{68,68},{102,102},{136,136},{170,170},{204,204},{238... | collective-permute-start | bytes 466952 | tf_op jit(solution)/shard_map/ppermute | solution.py:240
  11.8 0.7 copy-start.10
  12.6 1.4 %copy-start.11 = (s32[1024]{0:T(1024)S(1)}, s32[1024]{0:T(1024)}, u32[]{:S(2)}) copy-start(s32[1024]{0:T(1024)} %param.9) | copy-start | bytes 12292
  12.6 1.4 %slice-start = ((s32[1024]{0:T(1024)}), s32[64]{0:T(128)S(1)}, s32[]{:S(2)}) async-start(s32[1024]{0:T(1024)} %param.9), calls=%async_computation | async-start | bytes 1024 | tf_op jit(solution)/shard_map/slice | solution.py:253
  12.6 24.2 %collective-permute-start.5 = (bf16[368,128]{1,0:T(8,128)(2,1)S(1)}, bf16[368,128]{1,0:T(8,128)(2,1)S(1)}, u32[]{:S(2)}, u32[]{:S(2)}) collective-permute-start(bf16[368,128]{1,0:T(8,128)(2,1)S(1)} %slice_add_fusion), channel_id=1, source_target_pairs={{128,256},{448,320},{64,192},{0,384},{416,288},{96,224},{32,160},{... | collective-permute-start | bytes 282632 | tf_op jit(solution)/shard_map/ppermute | solution.py:249
  39.1 47.9 %collective-permute-start.7 = (bf16[128,32,128]{2,1,0:T(8,128)(2,1)S(1)}, bf16[128,32,128]{2,1,0:T(8,128)(2,1)S(1)}, u32[]{:S(2)}, u32[]{:S(2)}) collective-permute-start(bf16[128,32,128]{2,1,0:T(8,128)(2,1)S(1)} %left.1), channel_id=1, source_target_pairs={{0,1},{1,0},{2,3},{3,2},{4,5},{5,4},{6,7},{7,6},{8,9},{9,8},{10,11... | collective-permute-start | bytes 3145736 | tf_op jit(solution)/shard_map/ppermute | solution.py:260
  43.1 44.0 %collective-permute-start.6 = (bf16[128,128]{1,0:T(8,128)(2,1)S(1)}, bf16[128,128]{1,0:T(8,128)(2,1)S(1)}, u32[]{:S(2)}, u32[]{:S(2)}) collective-permute-start(bf16[128,128]{1,0:T(8,128)(2,1)S(1)} %get-tuple-element.30.rest), channel_id=1, source_target_pairs={{0,32},{32,0},{64,96},{96,64},{128,160},{160,128},{192,224},{224,1... | collective-permute-start | bytes 98312 | tf_op jit(solution)/shard_map/ppermute | solution.py:263
  90.0 1.0 %copy-start.2 = (bf16[128,32,128]{2,1,0:T(8,128)(2,1)}, bf16[128,32,128]{2,1,0:T(8,128)(2,1)S(1)}, u32[]{:S(2)}) copy-start(bf16[128,32,128]{2,1,0:T(8,128)(2,1)S(1)} %get-tuple-element.33.right) | copy-start | bytes 3145732
  91.0 8.3 %collective-permute-start.8 = (bf16[32,32,128]{2,1,0:T(8,128)(2,1)S(1)}, bf16[32,32,128]{2,1,0:T(8,128)(2,1)S(1)}, u32[]{:S(2)}, u32[]{:S(2)}) collective-permute-start(bf16[32,32,128]{2,1,0:T(8,128)(2,1)S(1)} %get-tuple-element.36), channel_id=1, source_target_pairs={{0,1},{1,0},{2,3},{3,2},{4,5},{5,4},{6,7},{7,6},{8,9},{9,8},{10,11... | collective-permute-start | bytes 786440 | tf_op jit(solution)/shard_map/ppermute | solution.py:267
  93.5 1.2 %copy-start.3 = (bf16[128,32,128]{2,1,0:T(8,128)(2,1)S(1)}, bf16[128,32,128]{2,1,0:T(8,128)(2,1)}, u32[]{:S(2)}) copy-start(bf16[128,32,128]{2,1,0:T(8,128)(2,1)} %copy-done.2) | copy-start | bytes 3145732

commit v5 on v4

--- a/solution.py
+++ b/solution.py
@@ -137,7 +137,7 @@
     chans = gathered.shape[-1]
     return pl.pallas_call(
         functools.partial(right_kernel, offsets),
-        out_shape=(jax.ShapeDtypeStruct((half, half, chans), BF16), jax.ShapeDtypeStruct((hid, half, width), BF16)),
+        out_shape=(jax.ShapeDtypeStruct((half, half, chans), BF16), pltpu.HBM((hid, half, width), BF16)),
         in_specs=[SMEM] * 2 + [VMEM] * 7,
         out_specs=(VMEM, pl.BlockSpec(memory_space=pltpu.HBM)),
         scratch_shapes=[
@@ -218,7 +218,7 @@
         compiler_params=pltpu.CompilerParams(vmem_limit_bytes=LIMIT),
         name="first",
         cost_estimate=pl.CostEstimate(flops=0, bytes_accessed=2 << 20, transcendentals=0),
-    )(flat, *ws)
+    )(*(pltpu.with_memory_space_constraint(a, pltpu.HBM) for a in (flat, *ws)))
 
 
 def per_device(pair_rep, token_mask, w_a, w_a_gate, w_b, w_b_gate, w_gate, w_out):

time: 101 us -> 94.2 us (0.933)
  local copies, waits for them, and re-layouts: 8.58 us -> 1.99 us
    unnamed x24 -> x8, local copies, waits for them, and re-layouts: 8.5 us -> 1.91 us
where the time goes in v5:
time: 94.2 us; the launch traced here: 93.8 us
  blocking collectives  40.1 us (43%)
  waiting for transfers between devices  25.6 us (27%)
  starting transfers between devices  16 us (17%)
  Pallas kernels  8.63 us (9%)
  local copies, waits for them, and re-layouts  1.99 us (2%)
  other arithmetic  1.28 us (1%)
    all_gather x1, blocking collectives, per_device(): gathered = lax.all_gather(chunk, 'row', axis=0, tiled=False)  40.1 us
    ppermute x1, waiting for transfers between devices, per_device(): passed = lax.ppermute(onward, ('row', 'col'), pairs)  22.9 us
    ppermute x1, starting transfers between devices, per_device(): rest_other = lax.ppermute(rest, 'row', [(r, r ^ 1) for r in range(rows)])  3.85 us
    ppermute x1, starting transfers between devices, per_device(): other = lax.ppermute(left, 'rep', swap)  3.48 us
    pallas_call x1, Pallas kernels, right_call(): pl.pallas_call(functools.partial(right_kernel, offsets), out_shape=(jax.S...  2.77 us
    ppermute x1, waiting for transfers between devices, per_device(): received = lax.ppermute(theirs, 'rep', swap)  2.76 us
    ppermute x4, starting transfers between devices, per_device(): got.append(lax.ppermute(message, ('row', 'col'), pairs))  2.68 us
    ppermute x1, starting transfers between devices, per_device(): received = lax.ppermute(theirs, 'rep', swap)  2.36 us
  transfers between devices with their start and end apart: 9, of which 2 were waited for; matrix products, arithmetic and copies ran while one was open for 0% of the time, Pallas kernels for 4%

profile of v5, /device:TPU:6, one launch (start us, length us, event | category | flops | bytes accessed | tf_op | source)
XLA Modules:
  0.0 93.8 jit_solution(16397189328493222583)
XLA Ops:
  0.0 2.3 %collective-permute-start = (bf16[2048,128]{1,0:T(8,128)(2,1)}, bf16[2048,128]{1,0:T(8,128)(2,1)S(1)}, u32[]{:S(2)}, u32[]{:S(2)}) collective-permute-start(bf16[2048,128]{1,0:T(8,128)(2,1)} %bitcast.8), channel_id=1, source_target_pairs={{0,30},{2,0},{4,2},{6,4},{8,6},{10,8},{12,10},{14,12},{16,14},{18,... | collective-permute-start | bytes 1572872 | tf_op jit(solution)/shard_map/ppermute | solution.py:241
  2.3 1.4 %first.1 = (bf16[608,128]{1,0:T(8,128)(2,1)S(1)}, bf16[608,128]{1,0:T(8,128)(2,1)S(1)}, bf16[608,128]{1,0:T(8,128)(2,1)S(1)}, bf16[608,128]{1,0:T(8,128)(2,1)S(1...) custom-call(bf16[2048,128]{1,0:T(8,128)(2,1)} %bitcast.9, ...), custom_call_target="tpu_custom_call" | custom-call | bytes 2097152 | tf_op jit(solution)/shard_map/first/pallas_call | solution.py:212
  3.7 0.7 collective-permute-start.1
  4.4 0.7 collective-permute-start.2
  5.0 0.7 collective-permute-start.3
  5.7 0.7 collective-permute-start.4
  6.4 0.7 copy-done.2
  7.1 0.1 fusion.2
  7.2 1.3 %collective-permute-start.5 = (bf16[368,128]{1,0:T(8,128)(2,1)S(1)}, bf16[368,128]{1,0:T(8,128)(2,1)S(1)}, u32[]{:S(2)}, u32[]{:S(2)}) collective-permute-start(bf16[368,128]{1,0:T(8,128)(2,1)S(1)} %slice_add_fusion), channel_id=1, source_target_pairs={{128,256},{448,320},{64,192},{0,384},{416,288},{96,224},{32,160},{... | collective-permute-start | bytes 282632 | tf_op jit(solution)/shard_map/ppermute | solution.py:249
  8.6 0.1 convert_bitcast_fusion.mask_k
  8.6 22.9 %collective-permute-done.5.refs_4_ = bf16[368,128]{1,0:T(8,128)(2,1)S(1)} collective-permute-done((bf16[368,128]{1,0:T(8,128)(2,1)S(1)}, bf16[368,128]{1,0:T(8,128)(2,1)S(1)}, u32[]{:S(2)}, u32[]{:S(2)}) %collective-permute-start.5) | collective-permute-done | bytes 94240 | tf_op jit(solution)/shard_map/ppermute | solution.py:249
  31.5 2.2 %left.1 = bf16[128,32,128]{2,1,0:T(8,128)(2,1)S(1)} custom-call(s32[32]{0:T(128)S(1)} %get-tuple-element.40.flags, bf16[32,64,128]{2,1,0:T(8,128)(2,1)S(1)} %copy-done, bf16[32,64,128]{2,1,0:T(8,128)(2,1)S(1)} %bitcast.10, f32[1,128]{1,0:T(1,128)S(1)} %convert_bitcast_fusion.mask_k, bf16[256,128]{1,0:T(8,128)(2,1)S(1)} %get-tuple-element.27.weights), custom_call_target="tpu_custom_call" | custom-call | flops 671088640 | bytes 2097152 | tf_op jit(solution)/shard_map/left/pallas_call | solution.py:59
  33.7 3.5 %collective-permute-start.7 = (bf16[128,32,128]{2,1,0:T(8,128)(2,1)S(1)}, bf16[128,32,128]{2,1,0:T(8,128)(2,1)S(1)}, u32[]{:S(2)}, u32[]{:S(2)}) collective-permute-start(bf16[128,32,128]{2,1,0:T(8,128)(2,1)S(1)} %left.1), channel_id=1, source_target_pairs={{0,1},{1,0},{2,3},{3,2},{4,5},{5,4},{6,7},{7,6},{8,9},{9,8},{10,11... | collective-permute-start | bytes 3145736 | tf_op jit(solution)/shard_map/ppermute | solution.py:260
  37.3 0.1 pad_add_fusion.place
  37.3 0.4 chunk.1
  37.7 3.8 %collective-permute-start.6 = (bf16[128,128]{1,0:T(8,128)(2,1)S(1)}, bf16[128,128]{1,0:T(8,128)(2,1)S(1)}, u32[]{:S(2)}, u32[]{:S(2)}) collective-permute-start(bf16[128,128]{1,0:T(8,128)(2,1)S(1)} %get-tuple-element.30.rest), channel_id=1, source_target_pairs={{0,32},{32,0},{64,96},{96,64},{128,160},{160,128},{192,224},{224,1... | collective-permute-start | bytes 98312 | tf_op jit(solution)/shard_map/ppermute | solution.py:263
  41.5 40.1 %all-gather = bf16[3840,128]{1,0:T(8,128)(2,1)S(1)} all-gather(bf16[240,128]{1,0:T(8,128)(2,1)S(1)} %get-tuple-element.29), channel_id=2, replica_groups=mesh['row'=16,'col'=16,'rep'=2] {'row'}, dimensions={0}, use_global_device_ids=true | all-gather | bytes 1044480 | tf_op jit(solution)/shard_map/all_gather | solution.py:264
  81.7 2.8 %right_tri.1 = (bf16[32,32,128]{2,1,0:T(8,128)(2,1)S(1)}, bf16[128,32,128]{2,1,0:T(8,128)(2,1)}) custom-call(s32[2]{0:T(128)S(1)} %pad_add_fusion.place, s32[32]{0:T(128)S(1)} %get-tuple-element.39.flags, bf16[16,240,128]{2,1,0:T(8,128)(2,1)S(1)} %bitcast.7, bf16[128,128]{1,0:T(8,128)(2,1)S(1)} %get-tuple-element.30.rest, ...), custom_call_target="tpu_custom_call" | custom-call | flops 536870912 | bytes 4194304 | tf_op jit(solution)/shard_map/right_tri/pallas_call | solution.py:138
  84.4 2.4 %collective-permute-start.8 = (bf16[32,32,128]{2,1,0:T(8,128)(2,1)S(1)}, bf16[32,32,128]{2,1,0:T(8,128)(2,1)S(1)}, u32[]{:S(2)}, u32[]{:S(2)}) collective-permute-start(bf16[32,32,128]{2,1,0:T(8,128)(2,1)S(1)} %get-tuple-element.36), channel_id=1, source_target_pairs={{0,1},{1,0},{2,3},{3,2},{4,5},{5,4},{6,7},{7,6},{8,9},{9,8},{10,11... | collective-permute-start | bytes 786440 | tf_op jit(solution)/shard_map/ppermute | solution.py:267
  86.8 1.2 %copy-done.1 = bf16[128,32,128]{2,1,0:T(8,128)(2,1)S(1)} copy-done((bf16[128,32,128]{2,1,0:T(8,128)(2,1)S(1)}, bf16[128,32,128]{2,1,0:T(8,128)(2,1)}, u32[]{:S(2)}) %copy-start.1) | copy-done | bytes 1048600
  88.0 1.9 %own_tri.1 = (f32[32,32,128]{2,1,0:T(8,128)S(1)}, f32[32,64,128]{2,1,0:T(8,128)S(1)}) custom-call(bf16[32,64,128]{2,1,0:T(8,128)(2,1)S(1)} %copy-done, bf16[128,128]{1,0:T(8,128)(2,1)S(1)} %get-tuple-element.21.w_gate, bf16[128,32,128]{2,1,0:T(8,128)(2,1)S(1)} %left.1, bf16[128,32,128]{2,1,0:T(8,128)(2,1)S(1)} %copy-done.1, ...), custom_call_target="tpu_custom_call" | custom-call | flops 268435456 | bytes 4194304 | tf_op jit(solution)/shard_map/own_tri/pallas_call | solution.py:170
  89.9 2.8 %collective-permute-done.8 = bf16[32,32,128]{2,1,0:T(8,128)(2,1)S(1)} collective-permute-done((bf16[32,32,128]{2,1,0:T(8,128)(2,1)S(1)}, bf16[32,32,128]{2,1,0:T(8,128)(2,1)S(1)}, u32[]{:S(2)}, u32[]{:S(2)}) %collective-permute-start.8) | collective-permute-done | bytes 262176 | tf_op jit(solution)/shard_map/ppermute | solution.py:267
  92.7 0.1 convert_select_fusion.1
  92.8 1.0 %fusion = bf16[32,64,128]{2,1,0:T(8,128)(2,1)} fusion(f32[32,64,128]{2,1,0:T(8,128)S(1)} %get-tuple-element.34, f32[32,32,128]{2,1,0:T(8,128)S(1)} %get-tuple-element.38, f32[32,32,128]{2,1,0:T(8,128)S(1)} %get-tuple-element.37), kind=kLoop, calls=%fused_computation.1 | loop fusion | flops 786432 | bytes 2621440 | tf_op jit(solution)/shard_map/convert_element_type | solution.py:272
  (16 shorter events, 0.1 us)
Async XLA Ops:
  0.0 31.5 %copy-start = (bf16[32,64,128]{2,1,0:T(8,128)(2,1)S(1)}, bf16[32,64,128]{2,1,0:T(8,128)(2,1)}, u32[]{:S(2)}) copy-start(bf16[32,64,128]{2,1,0:T(8,128)(2,1)} %x.3) | copy-start | bytes 1572868
  0.0 31.5 %collective-permute-start = (bf16[2048,128]{1,0:T(8,128)(2,1)}, bf16[2048,128]{1,0:T(8,128)(2,1)S(1)}, u32[]{:S(2)}, u32[]{:S(2)}) collective-permute-start(bf16[2048,128]{1,0:T(8,128)(2,1)} %bitcast.8), channel_id=1, source_target_pairs={{0,30},{2,0},{4,2},{6,4},{8,6},{10,8},{12,10},{14,12},{16,14},{18,... | collective-permute-start | bytes 1572872 | tf_op jit(solution)/shard_map/ppermute | solution.py:241
  3.7 3.5 %collective-permute-start.1 = (bf16[608,128]{1,0:T(8,128)(2,1)S(1)}, bf16[608,128]{1,0:T(8,128)(2,1)S(1)}, u32[]{:S(2)}, u32[]{:S(2)}) collective-permute-start(bf16[608,128]{1,0:T(8,128)(2,1)S(1)} %get-tuple-element.22), channel_id=1, source_target_pairs={{0,128},{34,162},{68,196},{102,230},{136,264},{170,298},{204,332},... | collective-permute-start | bytes 466952 | tf_op jit(solution)/shard_map/ppermute | solution.py:240
  4.4 2.8 %collective-permute-start.2 = (bf16[608,128]{1,0:T(8,128)(2,1)S(1)}, bf16[608,128]{1,0:T(8,128)(2,1)S(1)}, u32[]{:S(2)}, u32[]{:S(2)}) collective-permute-start(bf16[608,128]{1,0:T(8,128)(2,1)S(1)} %get-tuple-element.23), channel_id=1, source_target_pairs={{0,448},{34,482},{68,4},{102,38},{136,72},{170,106},{204,140},{238... | collective-permute-start | bytes 466952 | tf_op jit(solution)/shard_map/ppermute | solution.py:240
  5.0 2.2 %collective-permute-start.3 = (bf16[608,128]{1,0:T(8,128)(2,1)S(1)}, bf16[608,128]{1,0:T(8,128)(2,1)S(1)}, u32[]{:S(2)}, u32[]{:S(2)}) collective-permute-start(bf16[608,128]{1,0:T(8,128)(2,1)S(1)} %get-tuple-element.24), channel_id=1, source_target_pairs={{0,64},{34,98},{68,132},{102,166},{136,200},{170,234},{204,268},{2... | collective-permute-start | bytes 466952 | tf_op jit(solution)/shard_map/ppermute | solution.py:240
  5.7 1.5 %collective-permute-start.4 = (bf16[608,128]{1,0:T(8,128)(2,1)S(1)}, bf16[608,128]{1,0:T(8,128)(2,1)S(1)}, u32[]{:S(2)}, u32[]{:S(2)}) collective-permute-start(bf16[608,128]{1,0:T(8,128)(2,1)S(1)} %get-tuple-element.25), channel_id=1, source_target_pairs={{0,0},{34,34},{68,68},{102,102},{136,136},{170,170},{204,204},{238... | collective-permute-start | bytes 466952 | tf_op jit(solution)/shard_map/ppermute | solution.py:240
  6.4 0.7 copy-start.2
  7.2 1.4 %copy-start.3 = (s32[1024]{0:T(1024)S(1)}, s32[1024]{0:T(1024)}, u32[]{:S(2)}) copy-start(s32[1024]{0:T(1024)} %param.9) | copy-start | bytes 12292
  7.2 1.4 %slice-start = ((s32[1024]{0:T(1024)}), s32[64]{0:T(128)S(1)}, s32[]{:S(2)}) async-start(s32[1024]{0:T(1024)} %param.9), calls=%async_computation | async-start | bytes 1024 | tf_op jit(solution)/shard_map/slice | solution.py:253
  7.2 24.3 %collective-permute-start.5 = (bf16[368,128]{1,0:T(8,128)(2,1)S(1)}, bf16[368,128]{1,0:T(8,128)(2,1)S(1)}, u32[]{:S(2)}, u32[]{:S(2)}) collective-permute-start(bf16[368,128]{1,0:T(8,128)(2,1)S(1)} %slice_add_fusion), channel_id=1, source_target_pairs={{128,256},{448,320},{64,192},{0,384},{416,288},{96,224},{32,160},{... | collective-permute-start | bytes 282632 | tf_op jit(solution)/shard_map/ppermute | solution.py:249
  33.7 47.9 %collective-permute-start.7 = (bf16[128,32,128]{2,1,0:T(8,128)(2,1)S(1)}, bf16[128,32,128]{2,1,0:T(8,128)(2,1)S(1)}, u32[]{:S(2)}, u32[]{:S(2)}) collective-permute-start(bf16[128,32,128]{2,1,0:T(8,128)(2,1)S(1)} %left.1), channel_id=1, source_target_pairs={{0,1},{1,0},{2,3},{3,2},{4,5},{5,4},{6,7},{7,6},{8,9},{9,8},{10,11... | collective-permute-start | bytes 3145736 | tf_op jit(solution)/shard_map/ppermute | solution.py:260
  37.7 44.0 %collective-permute-start.6 = (bf16[128,128]{1,0:T(8,128)(2,1)S(1)}, bf16[128,128]{1,0:T(8,128)(2,1)S(1)}, u32[]{:S(2)}, u32[]{:S(2)}) collective-permute-start(bf16[128,128]{1,0:T(8,128)(2,1)S(1)} %get-tuple-element.30.rest), channel_id=1, source_target_pairs={{0,32},{32,0},{64,96},{96,64},{128,160},{160,128},{192,224},{224,1... | collective-permute-start | bytes 98312 | tf_op jit(solution)/shard_map/ppermute | solution.py:263
  84.4 8.3 %collective-permute-start.8 = (bf16[32,32,128]{2,1,0:T(8,128)(2,1)S(1)}, bf16[32,32,128]{2,1,0:T(8,128)(2,1)S(1)}, u32[]{:S(2)}, u32[]{:S(2)}) collective-permute-start(bf16[32,32,128]{2,1,0:T(8,128)(2,1)S(1)} %get-tuple-element.36), channel_id=1, source_target_pairs={{0,1},{1,0},{2,3},{3,2},{4,5},{5,4},{6,7},{7,6},{8,9},{9,8},{10,11... | collective-permute-start | bytes 786440 | tf_op jit(solution)/shard_map/ppermute | solution.py:267
  86.8 1.2 %copy-start.1 = (bf16[128,32,128]{2,1,0:T(8,128)(2,1)S(1)}, bf16[128,32,128]{2,1,0:T(8,128)(2,1)}, u32[]{:S(2)}) copy-start(bf16[128,32,128]{2,1,0:T(8,128)(2,1)} %get-tuple-element.33.right) | copy-start | bytes 3145732

commit v6 on v5

--- a/solution.py
+++ b/solution.py
@@ -14,6 +14,7 @@
 F32 = jnp.float32
 BF16 = jnp.bfloat16
 GROUP = 16
+REST = 16
 LIMIT = 20 << 20
 
 
@@ -67,22 +68,23 @@
     )(flags, x, x_next, mask_k, weights)
 
 
-def chunk_kernel(piece, *refs):
+def chunk_kernel(*refs):
     *got, passed, out, rest = refs
     total = got[0][...]
     for g in got[1:]:
         total = total + g[...]
-    own = jnp.concatenate([total[:piece], total[2 * piece :]])
+    size = (total.shape[0] - REST) // 2
+    own = jnp.concatenate([total[:size], total[2 * size :]])
     normed = normalise(own + passed[...])
-    out[...] = normed[:piece]
-    rest[...] = normed[piece:]
-
-
-def chunk_call(got, passed, piece):
+    out[...] = normed[: size - 1]
+    rest[...] = normed[size:]
+
+
+def chunk_call(got, passed):
     n, chans = passed.shape
     return pl.pallas_call(
-        functools.partial(chunk_kernel, piece),
-        out_shape=(jax.ShapeDtypeStruct((piece, chans), BF16), jax.ShapeDtypeStruct((n - piece, chans), BF16)),
+        chunk_kernel,
+        out_shape=(jax.ShapeDtypeStruct((n - REST - 1, chans), BF16), jax.ShapeDtypeStruct((REST, chans), BF16)),
         in_specs=[VMEM] * (len(got) + 1),
         out_specs=(VMEM, VMEM),
         compiler_params=pltpu.CompilerParams(vmem_limit_bytes=LIMIT),
@@ -107,17 +109,20 @@
             store(i + u, projected[u * half : (u + 1) * half])
 
 
-def right_kernel(offsets, place, flags, gathered, rest, rest_other, mask_k, weights, left, w_out, out, right_out, tiles, right, held, sem):
-    shards, piece, chans = gathered.shape
+def right_kernel(offsets, place, flags, gathered, rest, rest_other, mask_k, weights, left, w_out, out, right_out, tiles, rests, right, held, sem):
+    shards, piece, _ = gathered.shape
     hid, half, width = left.shape
     tile = width // 2
-    kept = shards // 2 * piece
+    rests[place[1]] = rest[...].astype(F32)
+    rests[1 - place[1]] = rest_other[...].astype(F32)
+    whole = piece + 1 - REST
     for t in range(2):
         for s, offset in enumerate(offsets[t]):
             shard = lax.rem(place[0] + offset % shards, shards)
-            tiles[t, s * piece : (s + 1) * piece] = gathered[shard]
-    tiles[place[1], kept:] = rest[...]
-    tiles[1 - place[1], kept:] = rest_other[...]
+            at = s * (piece + 1)
+            tiles[t, at : at + whole] = gathered[shard, :whole]
+            last = jnp.concatenate([gathered[shard, whole:].astype(F32), rests[t, s : s + 1]])
+            tiles[t, at + whole : at + whole + REST] = last.astype(BF16)
     for q in range(0, half, GROUP):
         blocks = [tiles[t, j * tile : (j + 1) * tile] for j in range(q, q + GROUP) for t in range(2)]
         masks = [mask_k[...] * flags[j].astype(F32) for j in range(q, q + GROUP)]
@@ -142,6 +147,7 @@
         out_specs=(VMEM, pl.BlockSpec(memory_space=pltpu.HBM)),
         scratch_shapes=[
             pltpu.VMEM((2, half * width // 2, chans), BF16),
+            pltpu.VMEM((2, REST, chans), F32),
             pltpu.VMEM((hid, half, width), BF16),
             pltpu.VMEM((half, hid, half), F32),
             pltpu.SemaphoreType.DMA,
@@ -179,46 +185,75 @@
     )(x, w_gate, left, right, w_out)
 
 
-def first_kernel(sends, kept, *refs):
-    flat, *ws = refs[:7]
-    outs, (wt_left, wt_right, w_gate, w_out), held = refs[7 : 7 + sends], refs[7 + sends : 11 + sends], refs[11 + sends]
-    sems = refs[-1]
-    size = kept // sends
+def first_kernel(flat, *refs):
+    *outs, tails, sems = refs
+    chunks = 2 * len(outs)
+    size = flat.shape[0] // chunks
+    copies = []
+    for s in range(chunks):
+        end = (s + 1) * size
+        copies.append(pltpu.make_async_copy(flat.at[end - REST : end], tails.at[s], sems.at[s]))
+    for s, out in enumerate(outs):
+        part = flat.at[2 * s * size : (2 * s + 2) * size]
+        copies.append(pltpu.make_async_copy(part, out.at[: 2 * size], sems.at[chunks + s]))
+    for copy in copies:
+        copy.start()
+    for copy in copies[:chunks]:
+        copy.wait()
+    rows = [tails[s].astype(F32)[REST - 1 :] for s in range(chunks)]
+    rest = jnp.concatenate(rows + [jnp.zeros((REST - chunks, flat.shape[1]), F32)]).astype(BF16)
+    for out in outs:
+        out[2 * size :] = rest
+    for copy in copies[chunks:]:
+        copy.wait()
+
+
+def first_call(flat, chunks):
+    rows, chans = flat.shape
+    sends = chunks // 2
+    message = jax.ShapeDtypeStruct((rows // sends + REST, chans), flat.dtype)
+    return pl.pallas_call(
+        first_kernel,
+        out_shape=(message,) * sends,
+        in_specs=[HBM],
+        out_specs=(VMEM,) * sends,
+        scratch_shapes=[pltpu.VMEM((chunks, REST, chans), BF16), pltpu.SemaphoreType.DMA((chunks + sends,))],
+        compiler_params=pltpu.CompilerParams(vmem_limit_bytes=LIMIT),
+        name="first",
+        cost_estimate=pl.CostEstimate(flops=0, bytes_accessed=2 << 20, transcendentals=0),
+    )(pltpu.with_memory_space_constraint(flat, pltpu.HBM))
+
+
+def weights_kernel(*refs):
+    ws, (wt_left, wt_right, w_gate, w_out), held, sems = refs[:6], refs[6:10], refs[10], refs[11]
     copies = []
     for i, w in enumerate(ws):
         dst = (held.at[0], held.at[1], held.at[2], held.at[3], w_gate, w_out)[i]
         copies.append(pltpu.make_async_copy(w, dst, sems.at[i]))
-    for s, out in enumerate(outs):
-        copies.append(pltpu.make_async_copy(flat.at[s * size : (s + 1) * size], out.at[:size], sems.at[6 + 2 * s]))
-        copies.append(pltpu.make_async_copy(flat.at[kept:], out.at[size:], sems.at[7 + 2 * s]))
     for copy in copies:
         copy.start()
-    for copy in copies[:6]:
+    for copy in copies:
         copy.wait()
-    hid = held.shape[1]
+    hid = held.shape[2]
     for i, wt in enumerate((wt_left, wt_right)):
         wt[:hid] = halved_transpose(held.at[2 * i])
         wt[hid:] = halved_transpose(held.at[2 * i + 1])
-    for copy in copies[6:]:
-        copy.wait()
-
-
-def first_call(flat, sends, kept, *ws):
-    rows, chans = flat.shape
-    hid = ws[0].shape[1]
-    message = jax.ShapeDtypeStruct((kept // sends + rows - kept, chans), flat.dtype)
+
+
+def weights_call(*ws):
+    chans, hid = ws[0].shape
     weights = jax.ShapeDtypeStruct((2 * hid, chans), BF16)
     square = jax.ShapeDtypeStruct((chans, hid), BF16)
     return pl.pallas_call(
-        functools.partial(first_kernel, sends, kept),
-        out_shape=(message,) * sends + (weights, weights, square, square),
-        in_specs=[HBM] * 7,
-        out_specs=(VMEM,) * (sends + 4),
-        scratch_shapes=[pltpu.VMEM((4, chans, hid), BF16), pltpu.SemaphoreType.DMA((6 + 2 * sends,))],
-        compiler_params=pltpu.CompilerParams(vmem_limit_bytes=LIMIT),
-        name="first",
-        cost_estimate=pl.CostEstimate(flops=0, bytes_accessed=2 << 20, transcendentals=0),
-    )(*(pltpu.with_memory_space_constraint(a, pltpu.HBM) for a in (flat, *ws)))
+        weights_kernel,
+        out_shape=(weights, weights, square, square),
+        in_specs=[HBM] * 6,
+        out_specs=(VMEM,) * 4,
+        scratch_shapes=[pltpu.VMEM((4, chans, hid), BF16), pltpu.SemaphoreType.DMA((6,))],
+        compiler_params=pltpu.CompilerParams(vmem_limit_bytes=LIMIT),
+        name="weights",
+        cost_estimate=pl.CostEstimate(flops=0, bytes_accessed=1 << 20, transcendentals=0),
+    )(*(pltpu.with_memory_space_constraint(w, pltpu.HBM) for w in ws))
 
 
 def per_device(pair_rep, token_mask, w_a, w_a_gate, w_b, w_b_gate, w_gate, w_out):
@@ -228,18 +263,18 @@
     swap = [(p, 1 - p) for p in range(reps)]
     flat = pair_rep.reshape(-1, chans)
 
-    kept = flat.shape[0] // rows * (rows - 1)
-    piece = kept // 8
-    near = ((4, -2, 2, 0), (-3, 3, 1, -1))
-    far = ((8, -6, 6, -4), (-7, 7, 5, -5))
-    *messages, wt_left, wt_right, w_gate, w_out = first_call(flat, 4, kept, w_a, w_a_gate, w_b, w_b_gate, w_gate, w_out)
+    near = ((0, 2, -2, 4), (1, -1, 3, -3))
+    far = ((-4, 6, -6, 8), (5, -5, 7, -7))
+    messages = first_call(flat, 8)
+    chunk_rows = flat.shape[0] // 8
     got = []
     for s, message in enumerate(messages):
         pairs = [(c * cols + c, (c + near[0][s]) % rows * cols + c) for c in range(cols)]
         pairs += [(c * cols + (c + 1) % cols, (c + near[1][s]) % rows * cols + c) for c in range(cols)]
         got.append(lax.ppermute(message, ("row", "col"), pairs))
+    wt_left, wt_right, w_gate, w_out = weights_call(w_a, w_a_gate, w_b, w_b_gate, w_gate, w_out)
     x_next = lax.ppermute(flat, "col", [(c, (c - 1) % cols) for c in range(cols)])
-    onward = got[0][piece:] + got[1][piece:] + got[2][piece:] + got[3][piece:]
+    onward = sum((g[chunk_rows:] for g in got[1:]), got[0][chunk_rows:])
     pairs = [
         ((c + n) % rows * cols + c, (c + f) % rows * cols + c)
         for c in range(cols)
@@ -255,11 +290,11 @@
     mask_i = lax.dynamic_slice_in_dim(token_mask, row * tile + rep * half, half, 0)
     mask_j = lax.dynamic_slice_in_dim(token_mask, col * tile + rep * half, half, 0)
 
-    x_next, passed = lax.optimization_barrier((x_next, passed))
     left = left_call(mask_i, pair_rep, x_next.reshape(half, tile, chans), mask_k, wt_left)
+    left, passed = lax.optimization_barrier((left, passed))
     other = lax.ppermute(left, "rep", swap)
 
-    chunk, rest = chunk_call(got, passed, piece)
+    chunk, rest = chunk_call(got, passed)
     rest_other = lax.ppermute(rest, "row", [(r, r ^ 1) for r in range(rows)])
     gathered = lax.all_gather(chunk, "row", axis=0, tiled=False)
 

time: 94.2 us -> 90 us (0.955)
  waiting for transfers between devices: 25.6 us -> 23.6 us
  blocking collectives: 40.1 us -> 38.5 us
  starting transfers between devices: 16 us -> 14.4 us
  Pallas kernels: 8.63 us -> 9.58 us
    ppermute x1, waiting for transfers between devices: 22.9 us -> 20.8 us  [per_device(): passed = lax.ppermute(onward, ('row', 'col'), pairs)]
    ppermute x1, starting transfers between devices: 3.85 us -> 2.27 us  [per_device(): rest_other = lax.ppermute(rest, 'row', [(r, r ^ 1) for r in range(rows)])]
    all_gather x1, blocking collectives: 40.1 us -> 38.5 us  [per_device(): gathered = lax.all_gather(chunk, 'row', axis=0, tiled=False)]
    pallas_call x2 -> x3, Pallas kernels: 1.72 us -> 2.67 us  [the longest x1 1.33 us: first_call(): pl.pallas_call(first_kernel, out_shape=(message,) * sends, in_specs=[HBM]...]
  transfers between devices with their start and end apart: 9 -> 9, of which waited for: 2 -> 2; matrix products, arithmetic and copies ran while one was open for 0% -> 0% of each run, Pallas kernels for 4% -> 8%
where the time goes in v6:
time: 90 us; the launch traced here: 89.6 us
  blocking collectives  38.5 us (43%)
  waiting for transfers between devices  23.6 us (26%)
  starting transfers between devices  14.4 us (16%)
  Pallas kernels  9.58 us (11%)
  local copies, waits for them, and re-layouts  1.99 us (2%)
  other arithmetic  1.28 us (1%)
    all_gather x1, blocking collectives, per_device(): gathered = lax.all_gather(chunk, 'row', axis=0, tiled=False)  38.5 us
    ppermute x1, waiting for transfers between devices, per_device(): passed = lax.ppermute(onward, ('row', 'col'), pairs)  20.8 us
    ppermute x1, starting transfers between devices, per_device(): other = lax.ppermute(left, 'rep', swap)  3.47 us
    pallas_call x1, Pallas kernels, right_call(): pl.pallas_call(functools.partial(right_kernel, offsets), out_shape=(jax.S...  2.78 us
    ppermute x1, waiting for transfers between devices, per_device(): received = lax.ppermute(theirs, 'rep', swap)  2.75 us
    ppermute x4, starting transfers between devices, per_device(): got.append(lax.ppermute(message, ('row', 'col'), pairs))  2.68 us
    ppermute x1, starting transfers between devices, per_device(): received = lax.ppermute(theirs, 'rep', swap)  2.37 us
    ppermute x1, starting transfers between devices, per_device(): lax.ppermute(flat, 'col', [(c, (c - 1) % cols) for c in range(cols)])  2.3 us
  transfers between devices with their start and end apart: 9, of which 2 were waited for; matrix products, arithmetic and copies ran while one was open for 0% of the time, Pallas kernels for 8%

profile of v6, /device:TPU:6, one launch (start us, length us, event | category | flops | bytes accessed | tf_op | source)
XLA Modules:
  0.0 89.6 jit_solution(9312629806229240551)
XLA Ops:
  0.0 2.3 %collective-permute-start = (bf16[2048,128]{1,0:T(8,128)(2,1)}, bf16[2048,128]{1,0:T(8,128)(2,1)S(1)}, u32[]{:S(2)}, u32[]{:S(2)}) collective-permute-start(bf16[2048,128]{1,0:T(8,128)(2,1)} %bitcast.7), channel_id=1, source_target_pairs={{0,30},{2,0},{4,2},{6,4},{8,6},{10,8},{12,10},{14,12},{16,14},{18,... | collective-permute-start | bytes 1572872 | tf_op jit(solution)/shard_map/ppermute | solution.py:276
  2.3 1.3 %first.1 = (bf16[528,128]{1,0:T(8,128)(2,1)S(1)}, bf16[528,128]{1,0:T(8,128)(2,1)S(1)}, bf16[528,128]{1,0:T(8,128)(2,1)S(1)}, bf16[528,128]{1,0:T(8,128)(2,1)S(1)}) custom-call(bf16[2048,128]{1,0:T(8,128)(2,1)} %bitcast.8), custom_call_target="tpu_custom_call" | custom-call | bytes 2097152 | tf_op jit(solution)/shard_map/first/pallas_call | solution.py:215
  3.6 0.7 collective-permute-start.1
  4.3 0.7 collective-permute-start.2
  5.0 0.7 collective-permute-start.3
  5.7 0.7 collective-permute-start.4
  6.4 0.7 copy-done.2
  7.2 1.3 %collective-permute-start.5 = (bf16[272,128]{1,0:T(8,128)(2,1)S(1)}, bf16[272,128]{1,0:T(8,128)(2,1)S(1)}, u32[]{:S(2)}, u32[]{:S(2)}) collective-permute-start(bf16[272,128]{1,0:T(8,128)(2,1)S(1)} %slice_add_fusion), channel_id=1, source_target_pairs={{0,384},{64,192},{448,320},{128,256},{32,160},{480,352},{96,224},{... | collective-permute-start | bytes 208904 | tf_op jit(solution)/shard_map/ppermute | solution.py:284
  8.5 0.1 convert_bitcast_fusion.mask_k
  8.6 1.0 %weights.1 = (bf16[256,128]{1,0:T(8,128)(2,1)S(1)}, bf16[256,128]{1,0:T(8,128)(2,1)S(1)}, bf16[128,128]{1,0:T(8,128)(2,1)S(1)}, bf16[128,128]{1,0:T(8,128)(2,1)S(1)}) custom-call(bf16[128,128]{1,0:T(8,128)(2,1)} %refs_0_.1, bf16[128,128]{1,0:T(8,128)(2,1)} %refs_1_.1, bf16[128,128]{1,0:T(8,128)(2,1)} %refs_2_.1, bf16[128,128]{1,0:T(8,128)(2,1)} %refs_3_.1, ...), custom_call_target="tpu_custom_call" | custom-call | bytes 1048576 | tf_op jit(solution)/shard_map/weights/pallas_call | solution.py:247
  9.6 2.2 %left.1 = bf16[128,32,128]{2,1,0:T(8,128)(2,1)S(1)} custom-call(s32[32]{0:T(128)S(1)} %get-tuple-element.40.flags, bf16[32,64,128]{2,1,0:T(8,128)(2,1)S(1)} %copy-done, bf16[32,64,128]{2,1,0:T(8,128)(2,1)S(1)} %bitcast.10, f32[1,128]{1,0:T(1,128)S(1)} %convert_bitcast_fusion.mask_k, bf16[256,128]{1,0:T(8,128)(2,1)S(1)} %get-tuple-element.22.weights), custom_call_target="tpu_custom_call" | custom-call | flops 671088640 | bytes 2097152 | tf_op jit(solution)/shard_map/left/pallas_call | solution.py:60
  11.9 20.8 %collective-permute-done.5.refs_4_ = bf16[272,128]{1,0:T(8,128)(2,1)S(1)} collective-permute-done((bf16[272,128]{1,0:T(8,128)(2,1)S(1)}, bf16[272,128]{1,0:T(8,128)(2,1)S(1)}, u32[]{:S(2)}, u32[]{:S(2)}) %collective-permute-start.5) | collective-permute-done | bytes 69664 | tf_op jit(solution)/shard_map/ppermute | solution.py:284
  32.7 3.5 %collective-permute-start.7 = (bf16[128,32,128]{2,1,0:T(8,128)(2,1)S(1)}, bf16[128,32,128]{2,1,0:T(8,128)(2,1)S(1)}, u32[]{:S(2)}, u32[]{:S(2)}) collective-permute-start(bf16[128,32,128]{2,1,0:T(8,128)(2,1)S(1)} %left.1), channel_id=1, source_target_pairs={{0,1},{1,0},{2,3},{3,2},{4,5},{5,4},{6,7},{7,6},{8,9},{9,8},{10,11... | collective-permute-start | bytes 3145736 | tf_op jit(solution)/shard_map/ppermute | solution.py:295
  36.2 0.1 pad_add_fusion.place
  36.3 0.3 chunk.1
  36.6 2.3 %collective-permute-start.6 = (bf16[16,128]{1,0:T(8,128)(2,1)S(1)}, bf16[16,128]{1,0:T(8,128)(2,1)S(1)}, u32[]{:S(2)}, u32[]{:S(2)}) collective-permute-start(bf16[16,128]{1,0:T(8,128)(2,1)S(1)} %get-tuple-element.30.rest), channel_id=1, source_target_pairs={{0,32},{32,0},{64,96},{96,64},{128,160},{160,128},{192,224},{224,1... | collective-permute-start | bytes 12296 | tf_op jit(solution)/shard_map/ppermute | solution.py:298
  38.9 38.5 %all-gather.1.gathered = bf16[16,255,128]{2,1,0:T(8,128)(2,1)S(1)} all-gather(bf16[1,255,128]{2,1,0:T(8,128)(2,1)S(1)} %bitcast.9), channel_id=2, replica_groups=mesh['row'=16,'col'=16,'rep'=2] {'row'}, dimensions={0}, use_global_device_ids=true | all-gather | bytes 1109760 | tf_op jit(solution)/shard_map/all_gather | solution.py:299
  77.4 2.8 %right_tri.1 = (bf16[32,32,128]{2,1,0:T(8,128)(2,1)S(1)}, bf16[128,32,128]{2,1,0:T(8,128)(2,1)}) custom-call(s32[2]{0:T(128)S(1)} %pad_add_fusion.place, s32[32]{0:T(128)S(1)} %get-tuple-element.39.flags, bf16[16,255,128]{2,1,0:T(8,128)(2,1)S(1)} %all-gather.1.gathered, bf16[16,128]{1,0:T(8,128)(2,1)S(1)} %get-tuple-element.30.rest, ...), custom_call_target="tpu_custom_call" | custom-call | flops 536870912 | bytes 4194304 | tf_op jit(solution)/shard_map/right_tri/pallas_call | solution.py:143
  80.2 2.4 %collective-permute-start.8 = (bf16[32,32,128]{2,1,0:T(8,128)(2,1)S(1)}, bf16[32,32,128]{2,1,0:T(8,128)(2,1)S(1)}, u32[]{:S(2)}, u32[]{:S(2)}) collective-permute-start(bf16[32,32,128]{2,1,0:T(8,128)(2,1)S(1)} %get-tuple-element.36), channel_id=1, source_target_pairs={{0,1},{1,0},{2,3},{3,2},{4,5},{5,4},{6,7},{7,6},{8,9},{9,8},{10,11... | collective-permute-start | bytes 786440 | tf_op jit(solution)/shard_map/ppermute | solution.py:302
  82.6 1.2 %copy-done.1 = bf16[128,32,128]{2,1,0:T(8,128)(2,1)S(1)} copy-done((bf16[128,32,128]{2,1,0:T(8,128)(2,1)S(1)}, bf16[128,32,128]{2,1,0:T(8,128)(2,1)}, u32[]{:S(2)}) %copy-start.1) | copy-done | bytes 1048600
  83.8 1.9 %own_tri.1 = (f32[32,32,128]{2,1,0:T(8,128)S(1)}, f32[32,64,128]{2,1,0:T(8,128)S(1)}) custom-call(bf16[32,64,128]{2,1,0:T(8,128)(2,1)S(1)} %copy-done, bf16[128,128]{1,0:T(8,128)(2,1)S(1)} %get-tuple-element.21.w_gate, bf16[128,32,128]{2,1,0:T(8,128)(2,1)S(1)} %left.1, bf16[128,32,128]{2,1,0:T(8,128)(2,1)S(1)} %copy-done.1, ...), custom_call_target="tpu_custom_call" | custom-call | flops 268435456 | bytes 4194304 | tf_op jit(solution)/shard_map/own_tri/pallas_call | solution.py:176
  85.7 2.8 %collective-permute-done.8 = bf16[32,32,128]{2,1,0:T(8,128)(2,1)S(1)} collective-permute-done((bf16[32,32,128]{2,1,0:T(8,128)(2,1)S(1)}, bf16[32,32,128]{2,1,0:T(8,128)(2,1)S(1)}, u32[]{:S(2)}, u32[]{:S(2)}) %collective-permute-start.8) | collective-permute-done | bytes 262176 | tf_op jit(solution)/shard_map/ppermute | solution.py:302
  88.5 0.1 convert_select_fusion.1
  88.6 1.0 %fusion = bf16[32,64,128]{2,1,0:T(8,128)(2,1)} fusion(f32[32,64,128]{2,1,0:T(8,128)S(1)} %get-tuple-element.34, f32[32,32,128]{2,1,0:T(8,128)S(1)} %get-tuple-element.38, f32[32,32,128]{2,1,0:T(8,128)S(1)} %get-tuple-element.37), kind=kLoop, calls=%fused_computation.1 | loop fusion | flops 786432 | bytes 2621440 | tf_op jit(solution)/shard_map/convert_element_type | solution.py:307
  (17 shorter events, 0.1 us)
Async XLA Ops:
  0.0 9.6 %copy-start = (bf16[32,64,128]{2,1,0:T(8,128)(2,1)S(1)}, bf16[32,64,128]{2,1,0:T(8,128)(2,1)}, u32[]{:S(2)}) copy-start(bf16[32,64,128]{2,1,0:T(8,128)(2,1)} %x.3) | copy-start | bytes 1572868
  0.0 9.6 %collective-permute-start = (bf16[2048,128]{1,0:T(8,128)(2,1)}, bf16[2048,128]{1,0:T(8,128)(2,1)S(1)}, u32[]{:S(2)}, u32[]{:S(2)}) collective-permute-start(bf16[2048,128]{1,0:T(8,128)(2,1)} %bitcast.7), channel_id=1, source_target_pairs={{0,30},{2,0},{4,2},{6,4},{8,6},{10,8},{12,10},{14,12},{16,14},{18,... | collective-permute-start | bytes 1572872 | tf_op jit(solution)/shard_map/ppermute | solution.py:276
  3.6 3.5 %collective-permute-start.1 = (bf16[528,128]{1,0:T(8,128)(2,1)S(1)}, bf16[528,128]{1,0:T(8,128)(2,1)S(1)}, u32[]{:S(2)}, u32[]{:S(2)}) collective-permute-start(bf16[528,128]{1,0:T(8,128)(2,1)S(1)} %get-tuple-element.23), channel_id=1, source_target_pairs={{0,0},{34,34},{68,68},{102,102},{136,136},{170,170},{204,204},{238... | collective-permute-start | bytes 405512 | tf_op jit(solution)/shard_map/ppermute | solution.py:274
  4.3 2.8 %collective-permute-start.2 = (bf16[528,128]{1,0:T(8,128)(2,1)S(1)}, bf16[528,128]{1,0:T(8,128)(2,1)S(1)}, u32[]{:S(2)}, u32[]{:S(2)}) collective-permute-start(bf16[528,128]{1,0:T(8,128)(2,1)S(1)} %get-tuple-element.24), channel_id=1, source_target_pairs={{0,64},{34,98},{68,132},{102,166},{136,200},{170,234},{204,268},{2... | collective-permute-start | bytes 405512 | tf_op jit(solution)/shard_map/ppermute | solution.py:274
  5.0 2.1 %collective-permute-start.3 = (bf16[528,128]{1,0:T(8,128)(2,1)S(1)}, bf16[528,128]{1,0:T(8,128)(2,1)S(1)}, u32[]{:S(2)}, u32[]{:S(2)}) collective-permute-start(bf16[528,128]{1,0:T(8,128)(2,1)S(1)} %get-tuple-element.25), channel_id=1, source_target_pairs={{0,448},{34,482},{68,4},{102,38},{136,72},{170,106},{204,140},{238... | collective-permute-start | bytes 405512 | tf_op jit(solution)/shard_map/ppermute | solution.py:274
  5.7 1.5 %collective-permute-start.4 = (bf16[528,128]{1,0:T(8,128)(2,1)S(1)}, bf16[528,128]{1,0:T(8,128)(2,1)S(1)}, u32[]{:S(2)}, u32[]{:S(2)}) collective-permute-start(bf16[528,128]{1,0:T(8,128)(2,1)S(1)} %get-tuple-element.26), channel_id=1, source_target_pairs={{0,128},{34,162},{68,196},{102,230},{136,264},{170,298},{204,332},... | collective-permute-start | bytes 405512 | tf_op jit(solution)/shard_map/ppermute | solution.py:274
  6.4 0.7 copy-start.2
  7.1 1.4 %copy-start.3 = (s32[1024]{0:T(1024)S(1)}, s32[1024]{0:T(1024)}, u32[]{:S(2)}) copy-start(s32[1024]{0:T(1024)} %param.9) | copy-start | bytes 12292
  7.1 1.4 %slice-start = ((s32[1024]{0:T(1024)}), s32[64]{0:T(128)S(1)}, s32[]{:S(2)}) async-start(s32[1024]{0:T(1024)} %param.9), calls=%async_computation | async-start | bytes 1024 | tf_op jit(solution)/shard_map/slice | solution.py:288
  7.2 25.5 %collective-permute-start.5 = (bf16[272,128]{1,0:T(8,128)(2,1)S(1)}, bf16[272,128]{1,0:T(8,128)(2,1)S(1)}, u32[]{:S(2)}, u32[]{:S(2)}) collective-permute-start(bf16[272,128]{1,0:T(8,128)(2,1)S(1)} %slice_add_fusion), channel_id=1, source_target_pairs={{0,384},{64,192},{448,320},{128,256},{32,160},{480,352},{96,224},{... | collective-permute-start | bytes 208904 | tf_op jit(solution)/shard_map/ppermute | solution.py:284
  32.7 44.7 %collective-permute-start.7 = (bf16[128,32,128]{2,1,0:T(8,128)(2,1)S(1)}, bf16[128,32,128]{2,1,0:T(8,128)(2,1)S(1)}, u32[]{:S(2)}, u32[]{:S(2)}) collective-permute-start(bf16[128,32,128]{2,1,0:T(8,128)(2,1)S(1)} %left.1), channel_id=1, source_target_pairs={{0,1},{1,0},{2,3},{3,2},{4,5},{5,4},{6,7},{7,6},{8,9},{9,8},{10,11... | collective-permute-start | bytes 3145736 | tf_op jit(solution)/shard_map/ppermute | solution.py:295
  36.6 40.8 %collective-permute-start.6 = (bf16[16,128]{1,0:T(8,128)(2,1)S(1)}, bf16[16,128]{1,0:T(8,128)(2,1)S(1)}, u32[]{:S(2)}, u32[]{:S(2)}) collective-permute-start(bf16[16,128]{1,0:T(8,128)(2,1)S(1)} %get-tuple-element.30.rest), channel_id=1, source_target_pairs={{0,32},{32,0},{64,96},{96,64},{128,160},{160,128},{192,224},{224,1... | collective-permute-start | bytes 12296 | tf_op jit(solution)/shard_map/ppermute | solution.py:298
  80.2 8.3 %collective-permute-start.8 = (bf16[32,32,128]{2,1,0:T(8,128)(2,1)S(1)}, bf16[32,32,128]{2,1,0:T(8,128)(2,1)S(1)}, u32[]{:S(2)}, u32[]{:S(2)}) collective-permute-start(bf16[32,32,128]{2,1,0:T(8,128)(2,1)S(1)} %get-tuple-element.36), channel_id=1, source_target_pairs={{0,1},{1,0},{2,3},{3,2},{4,5},{5,4},{6,7},{7,6},{8,9},{9,8},{10,11... | collective-permute-start | bytes 786440 | tf_op jit(solution)/shard_map/ppermute | solution.py:302
  82.6 1.2 %copy-start.1 = (bf16[128,32,128]{2,1,0:T(8,128)(2,1)S(1)}, bf16[128,32,128]{2,1,0:T(8,128)(2,1)}, u32[]{:S(2)}) copy-start(bf16[128,32,128]{2,1,0:T(8,128)(2,1)} %get-tuple-element.33.right) | copy-start | bytes 3145732

commit v7 on v6

--- a/solution.py
+++ b/solution.py
@@ -109,9 +109,9 @@
             store(i + u, projected[u * half : (u + 1) * half])
 
 
-def right_kernel(offsets, place, flags, gathered, rest, rest_other, mask_k, weights, left, w_out, out, right_out, tiles, rests, right, held, sem):
+def right_kernel(offsets, place, flags, gathered, rest, rest_other, mask_k, weights, right, tiles, rests):
     shards, piece, _ = gathered.shape
-    hid, half, width = left.shape
+    hid, half, width = right.shape
     tile = width // 2
     rests[place[1]] = rest[...].astype(F32)
     rests[1 - place[1]] = rest_other[...].astype(F32)
@@ -127,35 +127,43 @@
         blocks = [tiles[t, j * tile : (j + 1) * tile] for j in range(q, q + GROUP) for t in range(2)]
         masks = [mask_k[...] * flags[j].astype(F32) for j in range(q, q + GROUP)]
         right[:, q : q + GROUP, :] = gated(weights[...], jnp.concatenate(blocks), masks)
-    copy = pltpu.make_async_copy(right, right_out, sem)
-    copy.start()
-
+
+
+def right_call(offsets, place, flags, gathered, rest, rest_other, mask_k, weights):
+    half, chans = flags.shape[0], gathered.shape[-1]
+    hid, width = weights.shape[0] // 2, mask_k.shape[1]
+    return pl.pallas_call(
+        functools.partial(right_kernel, offsets),
+        out_shape=jax.ShapeDtypeStruct((hid, half, width), BF16),
+        in_specs=[SMEM] * 2 + [VMEM] * 5,
+        out_specs=VMEM,
+        scratch_shapes=[pltpu.VMEM((2, half * width // 2, chans), BF16), pltpu.VMEM((2, REST, chans), F32)],
+        compiler_params=pltpu.CompilerParams(vmem_limit_bytes=LIMIT),
+        name="right",
+        cost_estimate=pl.CostEstimate(flops=5 * 10**9, bytes_accessed=4 << 20, transcendentals=half * width * hid),
+    )(place, flags, gathered, rest, rest_other, mask_k, weights)
+
+
+def theirs_kernel(left, right, w_out, out, held):
     def store(i, rows):
         out[i] = rows.astype(BF16)
 
     tri_projected(left, right, w_out, held, store)
-    copy.wait()
-
-
-def right_call(offsets, place, flags, gathered, rest, rest_other, mask_k, weights, left, w_out):
-    hid, half, width = left.shape
-    chans = gathered.shape[-1]
-    return pl.pallas_call(
-        functools.partial(right_kernel, offsets),
-        out_shape=(jax.ShapeDtypeStruct((half, half, chans), BF16), pltpu.HBM((hid, half, width), BF16)),
-        in_specs=[SMEM] * 2 + [VMEM] * 7,
-        out_specs=(VMEM, pl.BlockSpec(memory_space=pltpu.HBM)),
-        scratch_shapes=[
-            pltpu.VMEM((2, half * width // 2, chans), BF16),
-            pltpu.VMEM((2, REST, chans), F32),
-            pltpu.VMEM((hid, half, width), BF16),
-            pltpu.VMEM((half, hid, half), F32),
-            pltpu.SemaphoreType.DMA,
-        ],
-        compiler_params=pltpu.CompilerParams(vmem_limit_bytes=LIMIT),
-        name="right_tri",
-        cost_estimate=pl.CostEstimate(flops=8 * half * width * chans * hid, bytes_accessed=4 << 20, transcendentals=half * width * hid),
-    )(place, flags, gathered, rest, rest_other, mask_k, weights, left, w_out)
+
+
+def theirs_call(left, right, w_out):
+    hid, half, _ = left.shape
+    chans = w_out.shape[1]
+    return pl.pallas_call(
+        theirs_kernel,
+        out_shape=jax.ShapeDtypeStruct((half, half, chans), BF16),
+        in_specs=[VMEM] * 3,
+        out_specs=VMEM,
+        scratch_shapes=[pltpu.VMEM((half, hid, half), F32)],
+        compiler_params=pltpu.CompilerParams(vmem_limit_bytes=LIMIT),
+        name="theirs",
+        cost_estimate=pl.CostEstimate(flops=8 * half * half * chans * hid, bytes_accessed=2 << 20, transcendentals=0),
+    )(left, right, w_out)
 
 
 def own_kernel(x, w_gate, left, right, w_out, out, gate, held):
@@ -252,7 +260,7 @@
         scratch_shapes=[pltpu.VMEM((4, chans, hid), BF16), pltpu.SemaphoreType.DMA((6,))],
         compiler_params=pltpu.CompilerParams(vmem_limit_bytes=LIMIT),
         name="weights",
-        cost_estimate=pl.CostEstimate(flops=0, bytes_accessed=1 << 20, transcendentals=0),
+        cost_estimate=pl.CostEstimate(flops=10**10, bytes_accessed=1 << 20, transcendentals=0),
     )(*(pltpu.with_memory_space_constraint(w, pltpu.HBM) for w in ws))
 
 
@@ -273,6 +281,7 @@
         pairs += [(c * cols + (c + 1) % cols, (c + near[1][s]) % rows * cols + c) for c in range(cols)]
         got.append(lax.ppermute(message, ("row", "col"), pairs))
     wt_left, wt_right, w_gate, w_out = weights_call(w_a, w_a_gate, w_b, w_b_gate, w_gate, w_out)
+    flat, messages = lax.optimization_barrier((flat, messages))
     x_next = lax.ppermute(flat, "col", [(c, (c - 1) % cols) for c in range(cols)])
     onward = sum((g[chunk_rows:] for g in got[1:]), got[0][chunk_rows:])
     pairs = [
@@ -291,14 +300,14 @@
     mask_j = lax.dynamic_slice_in_dim(token_mask, col * tile + rep * half, half, 0)
 
     left = left_call(mask_i, pair_rep, x_next.reshape(half, tile, chans), mask_k, wt_left)
-    left, passed = lax.optimization_barrier((left, passed))
     other = lax.ppermute(left, "rep", swap)
 
     chunk, rest = chunk_call(got, passed)
     rest_other = lax.ppermute(rest, "row", [(r, r ^ 1) for r in range(rows)])
     gathered = lax.all_gather(chunk, "row", axis=0, tiled=False)
 
-    theirs, right = right_call(offsets, place, mask_j, gathered, rest, rest_other, mask_k, wt_right, other, w_out)
+    right = right_call(offsets, place, mask_j, gathered, rest, rest_other, mask_k, wt_right)
+    theirs = theirs_call(other, right, w_out)
     received = lax.ppermute(theirs, "rep", swap)
     ours, gate = own_call(pair_rep, w_gate, left, right, w_out)
     received = received.astype(F32)

time: 90 us -> 85.5 us (0.950)
  the two profiles are of different devices: /device:TPU:6 before, /device:TPU:8 now
where the time goes in v7:
time: 85.5 us; the launch traced here: 85.1 us
  blocking collectives  39.7 us (46%)
  starting transfers between devices  29.6 us (35%)
  Pallas kernels  9.7 us (11%)
  waiting for transfers between devices  3.77 us (4%)
  other arithmetic  1.27 us (1%)
    all_gather x1, blocking collectives, per_device(): gathered = lax.all_gather(chunk, 'row', axis=0, tiled=False)  39.7 us
    ppermute x4, starting transfers between devices, per_device(): got.append(lax.ppermute(message, ('row', 'col'), pairs))  14.5 us
    ppermute x1, starting transfers between devices, per_device(): passed = lax.ppermute(onward, ('row', 'col'), pairs)  5.47 us
    ppermute x1, waiting for transfers between devices, per_device(): received = lax.ppermute(theirs, 'rep', swap)  3.75 us
    ppermute x1, starting transfers between devices, per_device(): other = lax.ppermute(left, 'rep', swap)  3.26 us
    ppermute x1, starting transfers between devices, per_device(): received = lax.ppermute(theirs, 'rep', swap)  2.59 us
    pallas_call x1, Pallas kernels, left_call(): pl.pallas_call(left_kernel, out_shape=jax.ShapeDtypeStruct((hid, half, 2...  2.24 us
    ppermute x1, starting transfers between devices, per_device(): rest_other = lax.ppermute(rest, 'row', [(r, r ^ 1) for r in range(rows)])  1.92 us
  transfers between devices with their start and end apart: 9, of which 1 were waited for; matrix products, arithmetic and copies ran while one was open for 0% of the time, Pallas kernels for 8%

profile of v7, /device:TPU:8, one launch (start us, length us, event | category | flops | bytes accessed | tf_op | source)
XLA Modules:
  0.0 85.1 jit_solution(13986249771188763534)
XLA Ops:
  0.0 1.4 %first.1 = (bf16[528,128]{1,0:T(8,128)(2,1)S(1)}, bf16[528,128]{1,0:T(8,128)(2,1)S(1)}, bf16[528,128]{1,0:T(8,128)(2,1)S(1)}, bf16[528,128]{1,0:T(8,128)(2,1)S(1)}) custom-call(bf16[2048,128]{1,0:T(8,128)(2,1)} %bitcast.7), custom_call_target="tpu_custom_call" | custom-call | bytes 2097152 | tf_op jit(solution)/shard_map/first/pallas_call | solution.py:223
  1.4 0.7 collective-permute-start.1
  2.1 5.2 %collective-permute-start.2 = (bf16[528,128]{1,0:T(8,128)(2,1)S(1)}, bf16[528,128]{1,0:T(8,128)(2,1)S(1)}, u32[]{:S(2)}, u32[]{:S(2)}) collective-permute-start(bf16[528,128]{1,0:T(8,128)(2,1)S(1)} %get-tuple-element.20), channel_id=1, source_target_pairs={{0,64},{34,98},{68,132},{102,166},{136,200},{170,234},{204,268},{2... | collective-permute-start | bytes 405512 | tf_op jit(solution)/shard_map/ppermute | solution.py:282
  7.3 7.3 %collective-permute-start.3 = (bf16[528,128]{1,0:T(8,128)(2,1)S(1)}, bf16[528,128]{1,0:T(8,128)(2,1)S(1)}, u32[]{:S(2)}, u32[]{:S(2)}) collective-permute-start(bf16[528,128]{1,0:T(8,128)(2,1)S(1)} %get-tuple-element.21), channel_id=1, source_target_pairs={{0,448},{34,482},{68,4},{102,38},{136,72},{170,106},{204,140},{238... | collective-permute-start | bytes 405512 | tf_op jit(solution)/shard_map/ppermute | solution.py:282
  14.6 1.3 %collective-permute-start.4 = (bf16[528,128]{1,0:T(8,128)(2,1)S(1)}, bf16[528,128]{1,0:T(8,128)(2,1)S(1)}, u32[]{:S(2)}, u32[]{:S(2)}) collective-permute-start(bf16[528,128]{1,0:T(8,128)(2,1)S(1)} %get-tuple-element.22), channel_id=1, source_target_pairs={{0,128},{34,162},{68,196},{102,230},{136,264},{170,298},{204,332},... | collective-permute-start | bytes 405512 | tf_op jit(solution)/shard_map/ppermute | solution.py:282
  15.9 1.9 %collective-permute-start = (bf16[2048,128]{1,0:T(8,128)(2,1)S(1)}, bf16[2048,128]{1,0:T(8,128)(2,1)S(1)}, u32[]{:S(2)}, u32[]{:S(2)}) collective-permute-start(bf16[2048,128]{1,0:T(8,128)(2,1)S(1)} %bitcast.8), channel_id=1, source_target_pairs={{0,30},{2,0},{4,2},{6,4},{8,6},{10,8},{12,10},{14,12},{16,14},{18,... | collective-permute-start | bytes 1572872 | tf_op jit(solution)/shard_map/ppermute | solution.py:285
  17.8 1.0 %weights.1 = (bf16[256,128]{1,0:T(8,128)(2,1)S(1)}, bf16[256,128]{1,0:T(8,128)(2,1)S(1)}, bf16[128,128]{1,0:T(8,128)(2,1)S(1)}, bf16[128,128]{1,0:T(8,128)(2,1)S(1)}) custom-call(bf16[128,128]{1,0:T(8,128)(2,1)} %refs_0_.1, bf16[128,128]{1,0:T(8,128)(2,1)} %refs_1_.1, bf16[128,128]{1,0:T(8,128)(2,1)} %refs_2_.1, bf16[128,128]{1,0:T(8,128)(2,1)} %refs_3_.1, ...), custom_call_target="tpu_custom_call" | custom-call | flops 10000000000 | bytes 1048576 | tf_op jit(solution)/shard_map/weights/pallas_call | solution.py:255
  18.9 0.7 copy-done.1
  19.6 0.1 convert_bitcast_fusion.mask_k
  19.7 0.1 fusion.2
  19.8 5.5 %collective-permute-start.5 = (bf16[272,128]{1,0:T(8,128)(2,1)S(1)}, bf16[272,128]{1,0:T(8,128)(2,1)S(1)}, u32[]{:S(2)}, u32[]{:S(2)}) collective-permute-start(bf16[272,128]{1,0:T(8,128)(2,1)S(1)} %slice_add_fusion), channel_id=1, source_target_pairs={{0,384},{64,192},{448,320},{128,256},{32,160},{480,352},{96,224},{... | collective-permute-start | bytes 208904 | tf_op jit(solution)/shard_map/ppermute | solution.py:293
  25.3 2.2 %left.1 = bf16[128,32,128]{2,1,0:T(8,128)(2,1)S(1)} custom-call(s32[32]{0:T(128)S(1)} %get-tuple-element.34.flags, bf16[32,64,128]{2,1,0:T(8,128)(2,1)S(1)} %copy-done, bf16[32,64,128]{2,1,0:T(8,128)(2,1)S(1)} %bitcast.10, f32[1,128]{1,0:T(1,128)S(1)} %convert_bitcast_fusion.mask_k, bf16[256,128]{1,0:T(8,128)(2,1)S(1)} %get-tuple-element.24.weights), custom_call_target="tpu_custom_call" | custom-call | flops 671088640 | bytes 2097152 | tf_op jit(solution)/shard_map/left/pallas_call | solution.py:60
  27.5 3.3 %collective-permute-start.7 = (bf16[128,32,128]{2,1,0:T(8,128)(2,1)S(1)}, bf16[128,32,128]{2,1,0:T(8,128)(2,1)S(1)}, u32[]{:S(2)}, u32[]{:S(2)}) collective-permute-start(bf16[128,32,128]{2,1,0:T(8,128)(2,1)S(1)} %left.1), channel_id=1, source_target_pairs={{0,1},{1,0},{2,3},{3,2},{4,5},{5,4},{6,7},{7,6},{8,9},{9,8},{10,11... | collective-permute-start | bytes 3145736 | tf_op jit(solution)/shard_map/ppermute | solution.py:303
  30.8 0.1 pad_add_fusion.place
  30.9 0.3 chunk.1
  31.2 1.9 %collective-permute-start.6 = (bf16[16,128]{1,0:T(8,128)(2,1)S(1)}, bf16[16,128]{1,0:T(8,128)(2,1)S(1)}, u32[]{:S(2)}, u32[]{:S(2)}) collective-permute-start(bf16[16,128]{1,0:T(8,128)(2,1)S(1)} %get-tuple-element.26.rest), channel_id=1, source_target_pairs={{0,32},{32,0},{64,96},{96,64},{128,160},{160,128},{192,224},{224,1... | collective-permute-start | bytes 12296 | tf_op jit(solution)/shard_map/ppermute | solution.py:306
  33.1 39.7 %all-gather.1.gathered = bf16[16,255,128]{2,1,0:T(8,128)(2,1)S(1)} all-gather(bf16[1,255,128]{2,1,0:T(8,128)(2,1)S(1)} %bitcast.9), channel_id=2, replica_groups=mesh['row'=16,'col'=16,'rep'=2] {'row'}, dimensions={0}, use_global_device_ids=true | all-gather | bytes 1109760 | tf_op jit(solution)/shard_map/all_gather | solution.py:307
  72.8 1.6 %right.1 = bf16[128,32,128]{2,1,0:T(8,128)(2,1)S(1)} custom-call(s32[2]{0:T(128)S(1)} %pad_add_fusion.place, s32[32]{0:T(128)S(1)} %get-tuple-element.33.flags, bf16[16,255,128]{2,1,0:T(8,128)(2,1)S(1)} %all-gather.1.gathered, bf16[16,128]{1,0:T(8,128)(2,1)S(1)} %get-tuple-element.26.rest, bf16[16,128]{1,0:T(8,128)(2,1)S(1)} %collective-permute-done.6.rest_other, ...), custom_call_target="tpu_custom_call" | custom-call | flops 5000000000 | bytes 4194304 | tf_op jit(solution)/shard_map/right/pallas_call | solution.py:135
  74.4 1.3 %theirs.1 = bf16[32,32,128]{2,1,0:T(8,128)(2,1)S(1)} custom-call(bf16[128,32,128]{2,1,0:T(8,128)(2,1)S(1)} %collective-permute-done.7.left, bf16[128,32,128]{2,1,0:T(8,128)(2,1)S(1)} %right.1, bf16[128,128]{1,0:T(8,128)(2,1)S(1)} %get-tuple-element.28.w_out), custom_call_target="tpu_custom_call" | custom-call | flops 134217728 | bytes 2097152 | tf_op jit(solution)/shard_map/theirs/pallas_call | solution.py:157
  75.7 2.6 %collective-permute-start.8 = (bf16[32,32,128]{2,1,0:T(8,128)(2,1)S(1)}, bf16[32,32,128]{2,1,0:T(8,128)(2,1)S(1)}, u32[]{:S(2)}, u32[]{:S(2)}) collective-permute-start(bf16[32,32,128]{2,1,0:T(8,128)(2,1)S(1)} %theirs.1), channel_id=1, source_target_pairs={{0,1},{1,0},{2,3},{3,2},{4,5},{5,4},{6,7},{7,6},{8,9},{9,8},{10,11... | collective-permute-start | bytes 786440 | tf_op jit(solution)/shard_map/ppermute | solution.py:311
  78.3 1.9 %own_tri.1 = (f32[32,32,128]{2,1,0:T(8,128)S(1)}, f32[32,64,128]{2,1,0:T(8,128)S(1)}) custom-call(bf16[32,64,128]{2,1,0:T(8,128)(2,1)S(1)} %copy-done, bf16[128,128]{1,0:T(8,128)(2,1)S(1)} %get-tuple-element.18.w_gate, bf16[128,32,128]{2,1,0:T(8,128)(2,1)S(1)} %left.1, bf16[128,32,128]{2,1,0:T(8,128)(2,1)S(1)} %right.1, ...), custom_call_target="tpu_custom_call" | custom-call | flops 268435456 | bytes 4194304 | tf_op jit(solution)/shard_map/own_tri/pallas_call | solution.py:184
  80.2 3.7 %collective-permute-done.8 = bf16[32,32,128]{2,1,0:T(8,128)(2,1)S(1)} collective-permute-done((bf16[32,32,128]{2,1,0:T(8,128)(2,1)S(1)}, bf16[32,32,128]{2,1,0:T(8,128)(2,1)S(1)}, u32[]{:S(2)}, u32[]{:S(2)}) %collective-permute-start.8) | collective-permute-done | bytes 262176 | tf_op jit(solution)/shard_map/ppermute | solution.py:311
  84.0 0.1 convert_select_fusion.1
  84.1 1.0 %fusion = bf16[32,64,128]{2,1,0:T(8,128)(2,1)} fusion(f32[32,64,128]{2,1,0:T(8,128)S(1)} %get-tuple-element.29, f32[32,32,128]{2,1,0:T(8,128)S(1)} %get-tuple-element.32, f32[32,32,128]{2,1,0:T(8,128)S(1)} %get-tuple-element.31), kind=kLoop, calls=%fused_computation.1 | loop fusion | flops 786432 | bytes 2621440 | tf_op jit(solution)/shard_map/convert_element_type | solution.py:316
  (14 shorter events, 0.1 us)
Async XLA Ops:
  0.0 15.9 %copy-start = (bf16[32,64,128]{2,1,0:T(8,128)(2,1)S(1)}, bf16[32,64,128]{2,1,0:T(8,128)(2,1)}, u32[]{:S(2)}) copy-start(bf16[32,64,128]{2,1,0:T(8,128)(2,1)} %x.3) | copy-start | bytes 1572868
  1.4 18.4 %collective-permute-start.1 = (bf16[528,128]{1,0:T(8,128)(2,1)S(1)}, bf16[528,128]{1,0:T(8,128)(2,1)S(1)}, u32[]{:S(2)}, u32[]{:S(2)}) collective-permute-start(bf16[528,128]{1,0:T(8,128)(2,1)S(1)} %get-tuple-element.19), channel_id=1, source_target_pairs={{0,0},{34,34},{68,68},{102,102},{136,136},{170,170},{204,204},{238... | collective-permute-start | bytes 405512 | tf_op jit(solution)/shard_map/ppermute | solution.py:282
  2.1 17.7 %collective-permute-start.2 = (bf16[528,128]{1,0:T(8,128)(2,1)S(1)}, bf16[528,128]{1,0:T(8,128)(2,1)S(1)}, u32[]{:S(2)}, u32[]{:S(2)}) collective-permute-start(bf16[528,128]{1,0:T(8,128)(2,1)S(1)} %get-tuple-element.20), channel_id=1, source_target_pairs={{0,64},{34,98},{68,132},{102,166},{136,200},{170,234},{204,268},{2... | collective-permute-start | bytes 405512 | tf_op jit(solution)/shard_map/ppermute | solution.py:282
  7.3 12.5 %collective-permute-start.3 = (bf16[528,128]{1,0:T(8,128)(2,1)S(1)}, bf16[528,128]{1,0:T(8,128)(2,1)S(1)}, u32[]{:S(2)}, u32[]{:S(2)}) collective-permute-start(bf16[528,128]{1,0:T(8,128)(2,1)S(1)} %get-tuple-element.21), channel_id=1, source_target_pairs={{0,448},{34,482},{68,4},{102,38},{136,72},{170,106},{204,140},{238... | collective-permute-start | bytes 405512 | tf_op jit(solution)/shard_map/ppermute | solution.py:282
  14.6 5.2 %collective-permute-start.4 = (bf16[528,128]{1,0:T(8,128)(2,1)S(1)}, bf16[528,128]{1,0:T(8,128)(2,1)S(1)}, u32[]{:S(2)}, u32[]{:S(2)}) collective-permute-start(bf16[528,128]{1,0:T(8,128)(2,1)S(1)} %get-tuple-element.22), channel_id=1, source_target_pairs={{0,128},{34,162},{68,196},{102,230},{136,264},{170,298},{204,332},... | collective-permute-start | bytes 405512 | tf_op jit(solution)/shard_map/ppermute | solution.py:282
  15.9 9.4 %collective-permute-start = (bf16[2048,128]{1,0:T(8,128)(2,1)S(1)}, bf16[2048,128]{1,0:T(8,128)(2,1)S(1)}, u32[]{:S(2)}, u32[]{:S(2)}) collective-permute-start(bf16[2048,128]{1,0:T(8,128)(2,1)S(1)} %bitcast.8), channel_id=1, source_target_pairs={{0,30},{2,0},{4,2},{6,4},{8,6},{10,8},{12,10},{14,12},{16,14},{18,... | collective-permute-start | bytes 1572872 | tf_op jit(solution)/shard_map/ppermute | solution.py:285
  18.9 0.7 copy-start.1
  18.9 0.7 slice-start
  19.8 11.1 %collective-permute-start.5 = (bf16[272,128]{1,0:T(8,128)(2,1)S(1)}, bf16[272,128]{1,0:T(8,128)(2,1)S(1)}, u32[]{:S(2)}, u32[]{:S(2)}) collective-permute-start(bf16[272,128]{1,0:T(8,128)(2,1)S(1)} %slice_add_fusion), channel_id=1, source_target_pairs={{0,384},{64,192},{448,320},{128,256},{32,160},{480,352},{96,224},{... | collective-permute-start | bytes 208904 | tf_op jit(solution)/shard_map/ppermute | solution.py:293
  27.5 46.9 %collective-permute-start.7 = (bf16[128,32,128]{2,1,0:T(8,128)(2,1)S(1)}, bf16[128,32,128]{2,1,0:T(8,128)(2,1)S(1)}, u32[]{:S(2)}, u32[]{:S(2)}) collective-permute-start(bf16[128,32,128]{2,1,0:T(8,128)(2,1)S(1)} %left.1), channel_id=1, source_target_pairs={{0,1},{1,0},{2,3},{3,2},{4,5},{5,4},{6,7},{7,6},{8,9},{9,8},{10,11... | collective-permute-start | bytes 3145736 | tf_op jit(solution)/shard_map/ppermute | solution.py:303
  31.2 41.6 %collective-permute-start.6 = (bf16[16,128]{1,0:T(8,128)(2,1)S(1)}, bf16[16,128]{1,0:T(8,128)(2,1)S(1)}, u32[]{:S(2)}, u32[]{:S(2)}) collective-permute-start(bf16[16,128]{1,0:T(8,128)(2,1)S(1)} %get-tuple-element.26.rest), channel_id=1, source_target_pairs={{0,32},{32,0},{64,96},{96,64},{128,160},{160,128},{192,224},{224,1... | collective-permute-start | bytes 12296 | tf_op jit(solution)/shard_map/ppermute | solution.py:306
  75.7 8.3 %collective-permute-start.8 = (bf16[32,32,128]{2,1,0:T(8,128)(2,1)S(1)}, bf16[32,32,128]{2,1,0:T(8,128)(2,1)S(1)}, u32[]{:S(2)}, u32[]{:S(2)}) collective-permute-start(bf16[32,32,128]{2,1,0:T(8,128)(2,1)S(1)} %theirs.1), channel_id=1, source_target_pairs={{0,1},{1,0},{2,3},{3,2},{4,5},{5,4},{6,7},{7,6},{8,9},{9,8},{10,11... | collective-permute-start | bytes 786440 | tf_op jit(solution)/shard_map/ppermute | solution.py:311

commit v8 on v7

--- a/solution.py
+++ b/solution.py
@@ -197,23 +197,27 @@
     *outs, tails, sems = refs
     chunks = 2 * len(outs)
     size = flat.shape[0] // chunks
-    copies = []
-    for s in range(chunks):
-        end = (s + 1) * size
-        copies.append(pltpu.make_async_copy(flat.at[end - REST : end], tails.at[s], sems.at[s]))
-    for s, out in enumerate(outs):
-        part = flat.at[2 * s * size : (2 * s + 2) * size]
-        copies.append(pltpu.make_async_copy(part, out.at[: 2 * size], sems.at[chunks + s]))
-    for copy in copies:
-        copy.start()
-    for copy in copies[:chunks]:
-        copy.wait()
-    rows = [tails[s].astype(F32)[REST - 1 :] for s in range(chunks)]
-    rest = jnp.concatenate(rows + [jnp.zeros((REST - chunks, flat.shape[1]), F32)]).astype(BF16)
-    for out in outs:
-        out[2 * size :] = rest
-    for copy in copies[chunks:]:
-        copy.wait()
+    ahead = lax.axis_index("col") - lax.axis_index("row") + lax.axis_size("col")
+
+    @pl.when(lax.rem(ahead, lax.axis_size("col")) < 2)
+    def _():
+        copies = []
+        for s in range(chunks):
+            end = (s + 1) * size
+            copies.append(pltpu.make_async_copy(flat.at[end - REST : end], tails.at[s], sems.at[s]))
+        for s, out in enumerate(outs):
+            part = flat.at[2 * s * size : (2 * s + 2) * size]
+            copies.append(pltpu.make_async_copy(part, out.at[: 2 * size], sems.at[chunks + s]))
+        for copy in copies:
+            copy.start()
+        for copy in copies[:chunks]:
+            copy.wait()
+        rows = [tails[s].astype(F32)[REST - 1 :] for s in range(chunks)]
+        rest = jnp.concatenate(rows + [jnp.zeros((REST - chunks, flat.shape[1]), F32)]).astype(BF16)
+        for out in outs:
+            out[2 * size :] = rest
+        for copy in copies[chunks:]:
+            copy.wait()
 
 
 def first_call(flat, chunks):
@@ -271,8 +275,8 @@
     swap = [(p, 1 - p) for p in range(reps)]
     flat = pair_rep.reshape(-1, chans)
 
-    near = ((0, 2, -2, 4), (1, -1, 3, -3))
-    far = ((-4, 6, -6, 8), (5, -5, 7, -7))
+    near = ((0, -2, 2, 4), (-3, -5, 1, 3))
+    far = ((-4, -6, 6, 8), (-1, -7, 5, 7))
     messages = first_call(flat, 8)
     chunk_rows = flat.shape[0] // 8
     got = []

time: 85.5 us -> 85.4 us (level)
  starting transfers between devices: 29.6 us -> 27.6 us
  waiting for transfers between devices: 3.77 us -> 5.15 us
    ppermute x1, waiting for transfers between devices: 0.01 us -> 1.37 us  [per_device(): lax.ppermute(flat, 'col', [(c, (c - 1) % cols) for c in range(cols)])]
    ppermute x1, starting transfers between devices: 3.26 us -> 2.36 us  [per_device(): other = lax.ppermute(left, 'rep', swap)]
  transfers between devices with their start and end apart: 9 -> 9, of which waited for: 1 -> 2; matrix products, arithmetic and copies ran while one was open for 0% -> 0% of each run, Pallas kernels for 8% -> 8%
where the time goes in v8:
time: 85.4 us; the launch traced here: 85 us
  blocking collectives  40.3 us (47%)
  starting transfers between devices  27.6 us (32%)
  Pallas kernels  9.7 us (11%)
  waiting for transfers between devices  5.15 us (6%)
  other arithmetic  1.27 us (1%)
    all_gather x1, blocking collectives, per_device(): gathered = lax.all_gather(chunk, 'row', axis=0, tiled=False)  40.3 us
    ppermute x4, starting transfers between devices, per_device(): got.append(lax.ppermute(message, ('row', 'col'), pairs))  14 us
    ppermute x1, starting transfers between devices, per_device(): passed = lax.ppermute(onward, ('row', 'col'), pairs)  4.84 us
    ppermute x1, waiting for transfers between devices, per_device(): received = lax.ppermute(theirs, 'rep', swap)  3.76 us
    ppermute x1, starting transfers between devices, per_device(): received = lax.ppermute(theirs, 'rep', swap)  2.58 us
    ppermute x1, starting transfers between devices, per_device(): other = lax.ppermute(left, 'rep', swap)  2.36 us
    pallas_call x1, Pallas kernels, left_call(): pl.pallas_call(left_kernel, out_shape=jax.ShapeDtypeStruct((hid, half, 2...  2.24 us
    ppermute x1, starting transfers between devices, per_device(): rest_other = lax.ppermute(rest, 'row', [(r, r ^ 1) for r in range(rows)])  1.92 us
  transfers between devices with their start and end apart: 9, of which 2 were waited for; matrix products, arithmetic and copies ran while one was open for 0% of the time, Pallas kernels for 8%

profile of v8, /device:TPU:8, one launch (start us, length us, event | category | flops | bytes accessed | tf_op | source)
XLA Modules:
  0.0 85.0 jit_solution(17788116463496883486)
XLA Ops:
  0.0 1.4 %first.1 = (bf16[528,128]{1,0:T(8,128)(2,1)S(1)}, bf16[528,128]{1,0:T(8,128)(2,1)S(1)}, bf16[528,128]{1,0:T(8,128)(2,1)S(1)}, bf16[528,128]{1,0:T(8,128)(2,1)S(1)}) custom-call(bf16[2048,128]{1,0:T(8,128)(2,1)} %bitcast.7), custom_call_target="tpu_custom_call" | custom-call | bytes 2097152 | tf_op jit(solution)/shard_map/first/pallas_call | solution.py:227
  1.4 0.7 collective-permute-start.1
  2.1 10.7 %collective-permute-start.2 = (bf16[528,128]{1,0:T(8,128)(2,1)S(1)}, bf16[528,128]{1,0:T(8,128)(2,1)S(1)}, u32[]{:S(2)}, u32[]{:S(2)}) collective-permute-start(bf16[528,128]{1,0:T(8,128)(2,1)S(1)} %get-tuple-element.20), channel_id=1, source_target_pairs={{0,448},{34,482},{68,4},{102,38},{136,72},{170,106},{204,140},{238... | collective-permute-start | bytes 405512 | tf_op jit(solution)/shard_map/ppermute | solution.py:286
  12.8 1.3 %collective-permute-start.3 = (bf16[528,128]{1,0:T(8,128)(2,1)S(1)}, bf16[528,128]{1,0:T(8,128)(2,1)S(1)}, u32[]{:S(2)}, u32[]{:S(2)}) collective-permute-start(bf16[528,128]{1,0:T(8,128)(2,1)S(1)} %get-tuple-element.21), channel_id=1, source_target_pairs={{0,64},{34,98},{68,132},{102,166},{136,200},{170,234},{204,268},{2... | collective-permute-start | bytes 405512 | tf_op jit(solution)/shard_map/ppermute | solution.py:286
  14.1 1.3 %collective-permute-start.4 = (bf16[528,128]{1,0:T(8,128)(2,1)S(1)}, bf16[528,128]{1,0:T(8,128)(2,1)S(1)}, u32[]{:S(2)}, u32[]{:S(2)}) collective-permute-start(bf16[528,128]{1,0:T(8,128)(2,1)S(1)} %get-tuple-element.22), channel_id=1, source_target_pairs={{0,128},{34,162},{68,196},{102,230},{136,264},{170,298},{204,332},... | collective-permute-start | bytes 405512 | tf_op jit(solution)/shard_map/ppermute | solution.py:286
  15.4 1.9 %collective-permute-start = (bf16[2048,128]{1,0:T(8,128)(2,1)S(1)}, bf16[2048,128]{1,0:T(8,128)(2,1)S(1)}, u32[]{:S(2)}, u32[]{:S(2)}) collective-permute-start(bf16[2048,128]{1,0:T(8,128)(2,1)S(1)} %bitcast.8), channel_id=1, source_target_pairs={{0,30},{2,0},{4,2},{6,4},{8,6},{10,8},{12,10},{14,12},{16,14},{18,... | collective-permute-start | bytes 1572872 | tf_op jit(solution)/shard_map/ppermute | solution.py:289
  17.3 1.0 %weights.1 = (bf16[256,128]{1,0:T(8,128)(2,1)S(1)}, bf16[256,128]{1,0:T(8,128)(2,1)S(1)}, bf16[128,128]{1,0:T(8,128)(2,1)S(1)}, bf16[128,128]{1,0:T(8,128)(2,1)S(1)}) custom-call(bf16[128,128]{1,0:T(8,128)(2,1)} %refs_0_.1, bf16[128,128]{1,0:T(8,128)(2,1)} %refs_1_.1, bf16[128,128]{1,0:T(8,128)(2,1)} %refs_2_.1, bf16[128,128]{1,0:T(8,128)(2,1)} %refs_3_.1, ...), custom_call_target="tpu_custom_call" | custom-call | flops 10000000000 | bytes 1048576 | tf_op jit(solution)/shard_map/weights/pallas_call | solution.py:259
  18.4 0.7 copy-done.1
  19.1 0.1 convert_bitcast_fusion.mask_k
  19.3 4.8 %collective-permute-start.5 = (bf16[272,128]{1,0:T(8,128)(2,1)S(1)}, bf16[272,128]{1,0:T(8,128)(2,1)S(1)}, u32[]{:S(2)}, u32[]{:S(2)}) collective-permute-start(bf16[272,128]{1,0:T(8,128)(2,1)S(1)} %slice_add_fusion), channel_id=1, source_target_pairs={{0,384},{448,320},{64,192},{128,256},{416,480},{352,288},{32,160},... | collective-permute-start | bytes 208904 | tf_op jit(solution)/shard_map/ppermute | solution.py:297
  24.1 1.4 %collective-permute-done = bf16[2048,128]{1,0:T(8,128)(2,1)S(1)} collective-permute-done((bf16[2048,128]{1,0:T(8,128)(2,1)S(1)}, bf16[2048,128]{1,0:T(8,128)(2,1)S(1)}, u32[]{:S(2)}, u32[]{:S(2)}) %collective-permute-start) | collective-permute-done | bytes 524320 | tf_op jit(solution)/shard_map/ppermute | solution.py:289
  25.5 2.2 %left.1 = bf16[128,32,128]{2,1,0:T(8,128)(2,1)S(1)} custom-call(s32[32]{0:T(128)S(1)} %get-tuple-element.34.flags, bf16[32,64,128]{2,1,0:T(8,128)(2,1)S(1)} %copy-done, bf16[32,64,128]{2,1,0:T(8,128)(2,1)S(1)} %bitcast.10, f32[1,128]{1,0:T(1,128)S(1)} %convert_bitcast_fusion.mask_k, bf16[256,128]{1,0:T(8,128)(2,1)S(1)} %get-tuple-element.24.weights), custom_call_target="tpu_custom_call" | custom-call | flops 671088640 | bytes 2097152 | tf_op jit(solution)/shard_map/left/pallas_call | solution.py:60
  27.8 2.4 %collective-permute-start.7 = (bf16[128,32,128]{2,1,0:T(8,128)(2,1)S(1)}, bf16[128,32,128]{2,1,0:T(8,128)(2,1)S(1)}, u32[]{:S(2)}, u32[]{:S(2)}) collective-permute-start(bf16[128,32,128]{2,1,0:T(8,128)(2,1)S(1)} %left.1), channel_id=1, source_target_pairs={{0,1},{1,0},{2,3},{3,2},{4,5},{5,4},{6,7},{7,6},{8,9},{9,8},{10,11... | collective-permute-start | bytes 3145736 | tf_op jit(solution)/shard_map/ppermute | solution.py:307
  30.1 0.1 pad_add_fusion.place
  30.2 0.3 chunk.1
  30.5 1.9 %collective-permute-start.6 = (bf16[16,128]{1,0:T(8,128)(2,1)S(1)}, bf16[16,128]{1,0:T(8,128)(2,1)S(1)}, u32[]{:S(2)}, u32[]{:S(2)}) collective-permute-start(bf16[16,128]{1,0:T(8,128)(2,1)S(1)} %get-tuple-element.26.rest), channel_id=1, source_target_pairs={{0,32},{32,0},{64,96},{96,64},{128,160},{160,128},{192,224},{224,1... | collective-permute-start | bytes 12296 | tf_op jit(solution)/shard_map/ppermute | solution.py:310
  32.5 40.3 %all-gather.1.gathered = bf16[16,255,128]{2,1,0:T(8,128)(2,1)S(1)} all-gather(bf16[1,255,128]{2,1,0:T(8,128)(2,1)S(1)} %bitcast.9), channel_id=2, replica_groups=mesh['row'=16,'col'=16,'rep'=2] {'row'}, dimensions={0}, use_global_device_ids=true | all-gather | bytes 1109760 | tf_op jit(solution)/shard_map/all_gather | solution.py:311
  72.7 1.6 %right.1 = bf16[128,32,128]{2,1,0:T(8,128)(2,1)S(1)} custom-call(s32[2]{0:T(128)S(1)} %pad_add_fusion.place, s32[32]{0:T(128)S(1)} %get-tuple-element.33.flags, bf16[16,255,128]{2,1,0:T(8,128)(2,1)S(1)} %all-gather.1.gathered, bf16[16,128]{1,0:T(8,128)(2,1)S(1)} %get-tuple-element.26.rest, bf16[16,128]{1,0:T(8,128)(2,1)S(1)} %collective-permute-done.6.rest_other, ...), custom_call_target="tpu_custom_call" | custom-call | flops 5000000000 | bytes 4194304 | tf_op jit(solution)/shard_map/right/pallas_call | solution.py:135
  74.3 1.3 %theirs.1 = bf16[32,32,128]{2,1,0:T(8,128)(2,1)S(1)} custom-call(bf16[128,32,128]{2,1,0:T(8,128)(2,1)S(1)} %collective-permute-done.7.left, bf16[128,32,128]{2,1,0:T(8,128)(2,1)S(1)} %right.1, bf16[128,128]{1,0:T(8,128)(2,1)S(1)} %get-tuple-element.28.w_out), custom_call_target="tpu_custom_call" | custom-call | flops 134217728 | bytes 2097152 | tf_op jit(solution)/shard_map/theirs/pallas_call | solution.py:157
  75.6 2.6 %collective-permute-start.8 = (bf16[32,32,128]{2,1,0:T(8,128)(2,1)S(1)}, bf16[32,32,128]{2,1,0:T(8,128)(2,1)S(1)}, u32[]{:S(2)}, u32[]{:S(2)}) collective-permute-start(bf16[32,32,128]{2,1,0:T(8,128)(2,1)S(1)} %theirs.1), channel_id=1, source_target_pairs={{0,1},{1,0},{2,3},{3,2},{4,5},{5,4},{6,7},{7,6},{8,9},{9,8},{10,11... | collective-permute-start | bytes 786440 | tf_op jit(solution)/shard_map/ppermute | solution.py:315
  78.2 1.9 %own_tri.1 = (f32[32,32,128]{2,1,0:T(8,128)S(1)}, f32[32,64,128]{2,1,0:T(8,128)S(1)}) custom-call(bf16[32,64,128]{2,1,0:T(8,128)(2,1)S(1)} %copy-done, bf16[128,128]{1,0:T(8,128)(2,1)S(1)} %get-tuple-element.18.w_gate, bf16[128,32,128]{2,1,0:T(8,128)(2,1)S(1)} %left.1, bf16[128,32,128]{2,1,0:T(8,128)(2,1)S(1)} %right.1, ...), custom_call_target="tpu_custom_call" | custom-call | flops 268435456 | bytes 4194304 | tf_op jit(solution)/shard_map/own_tri/pallas_call | solution.py:184
  80.1 3.8 %collective-permute-done.8 = bf16[32,32,128]{2,1,0:T(8,128)(2,1)S(1)} collective-permute-done((bf16[32,32,128]{2,1,0:T(8,128)(2,1)S(1)}, bf16[32,32,128]{2,1,0:T(8,128)(2,1)S(1)}, u32[]{:S(2)}, u32[]{:S(2)}) %collective-permute-start.8) | collective-permute-done | bytes 262176 | tf_op jit(solution)/shard_map/ppermute | solution.py:315
  83.9 0.1 convert_select_fusion.1
  84.0 1.0 %fusion = bf16[32,64,128]{2,1,0:T(8,128)(2,1)} fusion(f32[32,64,128]{2,1,0:T(8,128)S(1)} %get-tuple-element.29, f32[32,32,128]{2,1,0:T(8,128)S(1)} %get-tuple-element.32, f32[32,32,128]{2,1,0:T(8,128)S(1)} %get-tuple-element.31), kind=kLoop, calls=%fused_computation.1 | loop fusion | flops 786432 | bytes 2621440 | tf_op jit(solution)/shard_map/convert_element_type | solution.py:320
  (14 shorter events, 0.2 us)
Async XLA Ops:
  0.0 15.4 %copy-start = (bf16[32,64,128]{2,1,0:T(8,128)(2,1)S(1)}, bf16[32,64,128]{2,1,0:T(8,128)(2,1)}, u32[]{:S(2)}) copy-start(bf16[32,64,128]{2,1,0:T(8,128)(2,1)} %x.3) | copy-start | bytes 1572868
  1.4 17.9 %collective-permute-start.1 = (bf16[528,128]{1,0:T(8,128)(2,1)S(1)}, bf16[528,128]{1,0:T(8,128)(2,1)S(1)}, u32[]{:S(2)}, u32[]{:S(2)}) collective-permute-start(bf16[528,128]{1,0:T(8,128)(2,1)S(1)} %get-tuple-element.19), channel_id=1, source_target_pairs={{0,0},{34,34},{68,68},{102,102},{136,136},{170,170},{204,204},{238... | collective-permute-start | bytes 405512 | tf_op jit(solution)/shard_map/ppermute | solution.py:286
  2.1 17.2 %collective-permute-start.2 = (bf16[528,128]{1,0:T(8,128)(2,1)S(1)}, bf16[528,128]{1,0:T(8,128)(2,1)S(1)}, u32[]{:S(2)}, u32[]{:S(2)}) collective-permute-start(bf16[528,128]{1,0:T(8,128)(2,1)S(1)} %get-tuple-element.20), channel_id=1, source_target_pairs={{0,448},{34,482},{68,4},{102,38},{136,72},{170,106},{204,140},{238... | collective-permute-start | bytes 405512 | tf_op jit(solution)/shard_map/ppermute | solution.py:286
  12.8 6.5 %collective-permute-start.3 = (bf16[528,128]{1,0:T(8,128)(2,1)S(1)}, bf16[528,128]{1,0:T(8,128)(2,1)S(1)}, u32[]{:S(2)}, u32[]{:S(2)}) collective-permute-start(bf16[528,128]{1,0:T(8,128)(2,1)S(1)} %get-tuple-element.21), channel_id=1, source_target_pairs={{0,64},{34,98},{68,132},{102,166},{136,200},{170,234},{204,268},{2... | collective-permute-start | bytes 405512 | tf_op jit(solution)/shard_map/ppermute | solution.py:286
  14.1 5.2 %collective-permute-start.4 = (bf16[528,128]{1,0:T(8,128)(2,1)S(1)}, bf16[528,128]{1,0:T(8,128)(2,1)S(1)}, u32[]{:S(2)}, u32[]{:S(2)}) collective-permute-start(bf16[528,128]{1,0:T(8,128)(2,1)S(1)} %get-tuple-element.22), channel_id=1, source_target_pairs={{0,128},{34,162},{68,196},{102,230},{136,264},{170,298},{204,332},... | collective-permute-start | bytes 405512 | tf_op jit(solution)/shard_map/ppermute | solution.py:286
  15.4 10.1 %collective-permute-start = (bf16[2048,128]{1,0:T(8,128)(2,1)S(1)}, bf16[2048,128]{1,0:T(8,128)(2,1)S(1)}, u32[]{:S(2)}, u32[]{:S(2)}) collective-permute-start(bf16[2048,128]{1,0:T(8,128)(2,1)S(1)} %bitcast.8), channel_id=1, source_target_pairs={{0,30},{2,0},{4,2},{6,4},{8,6},{10,8},{12,10},{14,12},{16,14},{18,... | collective-permute-start | bytes 1572872 | tf_op jit(solution)/shard_map/ppermute | solution.py:289
  18.4 0.7 copy-start.1
  18.4 0.7 slice-start
  19.3 10.9 %collective-permute-start.5 = (bf16[272,128]{1,0:T(8,128)(2,1)S(1)}, bf16[272,128]{1,0:T(8,128)(2,1)S(1)}, u32[]{:S(2)}, u32[]{:S(2)}) collective-permute-start(bf16[272,128]{1,0:T(8,128)(2,1)S(1)} %slice_add_fusion), channel_id=1, source_target_pairs={{0,384},{448,320},{64,192},{128,256},{416,480},{352,288},{32,160},... | collective-permute-start | bytes 208904 | tf_op jit(solution)/shard_map/ppermute | solution.py:297
  27.8 46.6 %collective-permute-start.7 = (bf16[128,32,128]{2,1,0:T(8,128)(2,1)S(1)}, bf16[128,32,128]{2,1,0:T(8,128)(2,1)S(1)}, u32[]{:S(2)}, u32[]{:S(2)}) collective-permute-start(bf16[128,32,128]{2,1,0:T(8,128)(2,1)S(1)} %left.1), channel_id=1, source_target_pairs={{0,1},{1,0},{2,3},{3,2},{4,5},{5,4},{6,7},{7,6},{8,9},{9,8},{10,11... | collective-permute-start | bytes 3145736 | tf_op jit(solution)/shard_map/ppermute | solution.py:307
  30.5 42.2 %collective-permute-start.6 = (bf16[16,128]{1,0:T(8,128)(2,1)S(1)}, bf16[16,128]{1,0:T(8,128)(2,1)S(1)}, u32[]{:S(2)}, u32[]{:S(2)}) collective-permute-start(bf16[16,128]{1,0:T(8,128)(2,1)S(1)} %get-tuple-element.26.rest), channel_id=1, source_target_pairs={{0,32},{32,0},{64,96},{96,64},{128,160},{160,128},{192,224},{224,1... | collective-permute-start | bytes 12296 | tf_op jit(solution)/shard_map/ppermute | solution.py:310
  75.6 8.3 %collective-permute-start.8 = (bf16[32,32,128]{2,1,0:T(8,128)(2,1)S(1)}, bf16[32,32,128]{2,1,0:T(8,128)(2,1)S(1)}, u32[]{:S(2)}, u32[]{:S(2)}) collective-permute-start(bf16[32,32,128]{2,1,0:T(8,128)(2,1)S(1)} %theirs.1), channel_id=1, source_target_pairs={{0,1},{1,0},{2,3},{3,2},{4,5},{5,4},{6,7},{7,6},{8,9},{9,8},{10,11... | collective-permute-start | bytes 786440 | tf_op jit(solution)/shard_map/ppermute | solution.py:315

commit v9 on v8

--- a/solution.py
+++ b/solution.py
@@ -166,16 +166,19 @@
     )(left, right, w_out)
 
 
-def own_kernel(x, w_gate, left, right, w_out, out, gate, held):
+def own_kernel(x, w_gate, left, right, w_out, out, gate_other, held, gate):
     half, tile, chans = x.shape
-
-    def store(i, rows):
-        out[i] = rows
-
-    tri_projected(left, right, w_out, held, store)
     for q in range(0, half, GROUP):
         normed = normalise(x[q : q + GROUP].reshape(GROUP * tile, chans))
         gate[q : q + GROUP] = jax.nn.sigmoid(dot(normed, w_gate[...], ((1,), (0,)))).reshape(GROUP, tile, chans)
+    rep = lax.axis_index("rep")
+    mine = pl.ds(pl.multiple_of(rep * half, half), half)
+    gate_other[...] = gate[:, pl.ds(pl.multiple_of((1 - rep) * half, half), half), :]
+
+    def store(i, rows):
+        out[i, mine, :] = (rows * gate[i, mine, :]).astype(BF16)
+
+    tri_projected(left, right, w_out, held, store)
 
 
 def own_call(x, w_gate, left, right, w_out):
@@ -183,10 +186,10 @@
     hid = left.shape[0]
     return pl.pallas_call(
         own_kernel,
-        out_shape=(jax.ShapeDtypeStruct((half, half, chans), F32), jax.ShapeDtypeStruct((half, tile, chans), F32)),
+        out_shape=(jax.ShapeDtypeStruct((half, tile, chans), BF16), jax.ShapeDtypeStruct((half, half, chans), F32)),
         in_specs=[VMEM] * 5,
         out_specs=(VMEM, VMEM),
-        scratch_shapes=[pltpu.VMEM((half, hid, half), F32)],
+        scratch_shapes=[pltpu.VMEM((half, hid, half), F32), pltpu.VMEM((half, tile, chans), F32)],
         compiler_params=pltpu.CompilerParams(vmem_limit_bytes=LIMIT),
         name="own_tri",
         cost_estimate=pl.CostEstimate(flops=8 * half * tile * chans * chans, bytes_accessed=4 << 20, transcendentals=2 * half * tile * chans),
@@ -313,11 +316,9 @@
     right = right_call(offsets, place, mask_j, gathered, rest, rest_other, mask_k, wt_right)
     theirs = theirs_call(other, right, w_out)
     received = lax.ppermute(theirs, "rep", swap)
-    ours, gate = own_call(pair_rep, w_gate, left, right, w_out)
-    received = received.astype(F32)
-    low = rep == 0
-    projected = jnp.concatenate([jnp.where(low, ours, received), jnp.where(low, received, ours)], axis=1)
-    return (gate * projected).astype(BF16)
+    out, gate_other = own_call(pair_rep, w_gate, left, right, w_out)
+    theirs_gated = (gate_other * received.astype(F32)).astype(BF16)
+    return lax.dynamic_update_slice_in_dim(out, theirs_gated, (1 - rep) * half, 1)
 
 
 def solution(mesh):

time: 85.4 us -> 85 us (level)
  Pallas kernels: 9.7 us -> 10.7 us
  waiting for transfers between devices: 5.15 us -> 4.2 us
    convert_element_type x1 -> x0, other arithmetic: 0.96 us -> none  [per_device(): return (gate * projected).astype(BF16)]
    pallas_call x1, Pallas kernels: 1.9 us -> 2.86 us  [own_call(): pl.pallas_call(own_kernel, out_shape=(jax.ShapeDtypeStruct((half, tile, c...]
    ppermute x1, waiting for transfers between devices: 3.76 us -> 2.81 us  [per_device(): received = lax.ppermute(theirs, 'rep', swap)]
  transfers between devices with their start and end apart: 9 -> 9, of which waited for: 2 -> 2; matrix products, arithmetic and copies ran while one was open for 0% -> 0% of each run, Pallas kernels for 8% -> 9%
where the time goes in v9:
time: 85 us; the launch traced here: 84.6 us
  blocking collectives  40.3 us (47%)
  starting transfers between devices  27.6 us (32%)
  Pallas kernels  10.7 us (13%)
  waiting for transfers between devices  4.2 us (5%)
  other arithmetic  0.94 us (1%)
    all_gather x1, blocking collectives, per_device(): gathered = lax.all_gather(chunk, 'row', axis=0, tiled=False)  40.3 us
    ppermute x4, starting transfers between devices, per_device(): got.append(lax.ppermute(message, ('row', 'col'), pairs))  14 us
    ppermute x1, starting transfers between devices, per_device(): passed = lax.ppermute(onward, ('row', 'col'), pairs)  4.84 us
    pallas_call x1, Pallas kernels, own_call(): pl.pallas_call(own_kernel, out_shape=(jax.ShapeDtypeStruct((half, tile, c...  2.86 us
    ppermute x1, waiting for transfers between devices, per_device(): received = lax.ppermute(theirs, 'rep', swap)  2.81 us
    ppermute x1, starting transfers between devices, per_device(): received = lax.ppermute(theirs, 'rep', swap)  2.58 us
    ppermute x1, starting transfers between devices, per_device(): other = lax.ppermute(left, 'rep', swap)  2.36 us
    pallas_call x1, Pallas kernels, left_call(): pl.pallas_call(left_kernel, out_shape=jax.ShapeDtypeStruct((hid, half, 2...  2.24 us
  transfers between devices with their start and end apart: 9, of which 2 were waited for; matrix products, arithmetic and copies ran while one was open for 0% of the time, Pallas kernels for 9%

profile of v9, /device:TPU:8, one launch (start us, length us, event | category | flops | bytes accessed | tf_op | source)
XLA Modules:
  0.0 84.6 jit_solution(2861325436614676887)
XLA Ops:
  0.0 1.4 %first.1 = (bf16[528,128]{1,0:T(8,128)(2,1)S(1)}, bf16[528,128]{1,0:T(8,128)(2,1)S(1)}, bf16[528,128]{1,0:T(8,128)(2,1)S(1)}, bf16[528,128]{1,0:T(8,128)(2,1)S(1)}) custom-call(bf16[2048,128]{1,0:T(8,128)(2,1)} %bitcast.7), custom_call_target="tpu_custom_call" | custom-call | bytes 2097152 | tf_op jit(solution)/shard_map/first/pallas_call | solution.py:230
  1.4 0.7 collective-permute-start.1
  2.1 10.7 %collective-permute-start.2 = (bf16[528,128]{1,0:T(8,128)(2,1)S(1)}, bf16[528,128]{1,0:T(8,128)(2,1)S(1)}, u32[]{:S(2)}, u32[]{:S(2)}) collective-permute-start(bf16[528,128]{1,0:T(8,128)(2,1)S(1)} %get-tuple-element.20), channel_id=1, source_target_pairs={{0,448},{34,482},{68,4},{102,38},{136,72},{170,106},{204,140},{238... | collective-permute-start | bytes 405512 | tf_op jit(solution)/shard_map/ppermute | solution.py:289
  12.8 1.3 %collective-permute-start.3 = (bf16[528,128]{1,0:T(8,128)(2,1)S(1)}, bf16[528,128]{1,0:T(8,128)(2,1)S(1)}, u32[]{:S(2)}, u32[]{:S(2)}) collective-permute-start(bf16[528,128]{1,0:T(8,128)(2,1)S(1)} %get-tuple-element.21), channel_id=1, source_target_pairs={{0,64},{34,98},{68,132},{102,166},{136,200},{170,234},{204,268},{2... | collective-permute-start | bytes 405512 | tf_op jit(solution)/shard_map/ppermute | solution.py:289
  14.1 1.3 %collective-permute-start.4 = (bf16[528,128]{1,0:T(8,128)(2,1)S(1)}, bf16[528,128]{1,0:T(8,128)(2,1)S(1)}, u32[]{:S(2)}, u32[]{:S(2)}) collective-permute-start(bf16[528,128]{1,0:T(8,128)(2,1)S(1)} %get-tuple-element.22), channel_id=1, source_target_pairs={{0,128},{34,162},{68,196},{102,230},{136,264},{170,298},{204,332},... | collective-permute-start | bytes 405512 | tf_op jit(solution)/shard_map/ppermute | solution.py:289
  15.4 1.9 %collective-permute-start = (bf16[2048,128]{1,0:T(8,128)(2,1)S(1)}, bf16[2048,128]{1,0:T(8,128)(2,1)S(1)}, u32[]{:S(2)}, u32[]{:S(2)}) collective-permute-start(bf16[2048,128]{1,0:T(8,128)(2,1)S(1)} %bitcast.8), channel_id=1, source_target_pairs={{0,30},{2,0},{4,2},{6,4},{8,6},{10,8},{12,10},{14,12},{16,14},{18,... | collective-permute-start | bytes 1572872 | tf_op jit(solution)/shard_map/ppermute | solution.py:292
  17.3 1.0 %weights.1 = (bf16[256,128]{1,0:T(8,128)(2,1)S(1)}, bf16[256,128]{1,0:T(8,128)(2,1)S(1)}, bf16[128,128]{1,0:T(8,128)(2,1)S(1)}, bf16[128,128]{1,0:T(8,128)(2,1)S(1)}) custom-call(bf16[128,128]{1,0:T(8,128)(2,1)} %refs_0_.1, bf16[128,128]{1,0:T(8,128)(2,1)} %refs_1_.1, bf16[128,128]{1,0:T(8,128)(2,1)} %refs_2_.1, bf16[128,128]{1,0:T(8,128)(2,1)} %refs_3_.1, ...), custom_call_target="tpu_custom_call" | custom-call | flops 10000000000 | bytes 1048576 | tf_op jit(solution)/shard_map/weights/pallas_call | solution.py:262
  18.4 0.7 copy-done.1
  19.1 0.1 convert_bitcast_fusion.mask_k
  19.2 0.1 fusion.2
  19.3 4.8 %collective-permute-start.5 = (bf16[272,128]{1,0:T(8,128)(2,1)S(1)}, bf16[272,128]{1,0:T(8,128)(2,1)S(1)}, u32[]{:S(2)}, u32[]{:S(2)}) collective-permute-start(bf16[272,128]{1,0:T(8,128)(2,1)S(1)} %slice_add_fusion), channel_id=1, source_target_pairs={{0,384},{448,320},{64,192},{128,256},{416,480},{352,288},{32,160},... | collective-permute-start | bytes 208904 | tf_op jit(solution)/shard_map/ppermute | solution.py:300
  24.1 1.4 %collective-permute-done = bf16[2048,128]{1,0:T(8,128)(2,1)S(1)} collective-permute-done((bf16[2048,128]{1,0:T(8,128)(2,1)S(1)}, bf16[2048,128]{1,0:T(8,128)(2,1)S(1)}, u32[]{:S(2)}, u32[]{:S(2)}) %collective-permute-start) | collective-permute-done | bytes 524320 | tf_op jit(solution)/shard_map/ppermute | solution.py:292
  25.5 2.2 %left.1 = bf16[128,32,128]{2,1,0:T(8,128)(2,1)S(1)} custom-call(s32[32]{0:T(128)S(1)} %get-tuple-element.32.flags, bf16[32,64,128]{2,1,0:T(8,128)(2,1)S(1)} %copy-done, bf16[32,64,128]{2,1,0:T(8,128)(2,1)S(1)} %bitcast.10, f32[1,128]{1,0:T(1,128)S(1)} %convert_bitcast_fusion.mask_k, bf16[256,128]{1,0:T(8,128)(2,1)S(1)} %get-tuple-element.24.weights), custom_call_target="tpu_custom_call" | custom-call | flops 671088640 | bytes 2097152 | tf_op jit(solution)/shard_map/left/pallas_call | solution.py:60
  27.8 2.4 %collective-permute-start.7 = (bf16[128,32,128]{2,1,0:T(8,128)(2,1)S(1)}, bf16[128,32,128]{2,1,0:T(8,128)(2,1)S(1)}, u32[]{:S(2)}, u32[]{:S(2)}) collective-permute-start(bf16[128,32,128]{2,1,0:T(8,128)(2,1)S(1)} %left.1), channel_id=1, source_target_pairs={{0,1},{1,0},{2,3},{3,2},{4,5},{5,4},{6,7},{7,6},{8,9},{9,8},{10,11... | collective-permute-start | bytes 3145736 | tf_op jit(solution)/shard_map/ppermute | solution.py:310
  30.1 0.1 pad_add_fusion.place
  30.2 0.3 chunk.1
  30.5 1.9 %collective-permute-start.6 = (bf16[16,128]{1,0:T(8,128)(2,1)S(1)}, bf16[16,128]{1,0:T(8,128)(2,1)S(1)}, u32[]{:S(2)}, u32[]{:S(2)}) collective-permute-start(bf16[16,128]{1,0:T(8,128)(2,1)S(1)} %get-tuple-element.26.rest), channel_id=1, source_target_pairs={{0,32},{32,0},{64,96},{96,64},{128,160},{160,128},{192,224},{224,1... | collective-permute-start | bytes 12296 | tf_op jit(solution)/shard_map/ppermute | solution.py:313
  32.5 40.3 %all-gather.1.gathered = bf16[16,255,128]{2,1,0:T(8,128)(2,1)S(1)} all-gather(bf16[1,255,128]{2,1,0:T(8,128)(2,1)S(1)} %bitcast.9), channel_id=2, replica_groups=mesh['row'=16,'col'=16,'rep'=2] {'row'}, dimensions={0}, use_global_device_ids=true | all-gather | bytes 1109760 | tf_op jit(solution)/shard_map/all_gather | solution.py:314
  72.7 1.6 %right.1 = bf16[128,32,128]{2,1,0:T(8,128)(2,1)S(1)} custom-call(s32[2]{0:T(128)S(1)} %pad_add_fusion.place, s32[32]{0:T(128)S(1)} %get-tuple-element.31.flags, bf16[16,255,128]{2,1,0:T(8,128)(2,1)S(1)} %all-gather.1.gathered, bf16[16,128]{1,0:T(8,128)(2,1)S(1)} %get-tuple-element.26.rest, bf16[16,128]{1,0:T(8,128)(2,1)S(1)} %collective-permute-done.6.rest_other, ...), custom_call_target="tpu_custom_call" | custom-call | flops 5000000000 | bytes 4194304 | tf_op jit(solution)/shard_map/right/pallas_call | solution.py:135
  74.3 1.3 %theirs.1 = bf16[32,32,128]{2,1,0:T(8,128)(2,1)S(1)} custom-call(bf16[128,32,128]{2,1,0:T(8,128)(2,1)S(1)} %collective-permute-done.7.left, bf16[128,32,128]{2,1,0:T(8,128)(2,1)S(1)} %right.1, bf16[128,128]{1,0:T(8,128)(2,1)S(1)} %get-tuple-element.28.w_out), custom_call_target="tpu_custom_call" | custom-call | flops 134217728 | bytes 2097152 | tf_op jit(solution)/shard_map/theirs/pallas_call | solution.py:157
  75.6 2.6 %collective-permute-start.8 = (bf16[32,32,128]{2,1,0:T(8,128)(2,1)S(1)}, bf16[32,32,128]{2,1,0:T(8,128)(2,1)S(1)}, u32[]{:S(2)}, u32[]{:S(2)}) collective-permute-start(bf16[32,32,128]{2,1,0:T(8,128)(2,1)S(1)} %theirs.1), channel_id=1, source_target_pairs={{0,1},{1,0},{2,3},{3,2},{4,5},{5,4},{6,7},{7,6},{8,9},{9,8},{10,11... | collective-permute-start | bytes 786440 | tf_op jit(solution)/shard_map/ppermute | solution.py:318
  78.2 2.9 %own_tri.1 = (bf16[32,64,128]{2,1,0:T(8,128)(2,1)}, f32[32,32,128]{2,1,0:T(8,128)S(1)}) custom-call(bf16[32,64,128]{2,1,0:T(8,128)(2,1)S(1)} %copy-done, bf16[128,128]{1,0:T(8,128)(2,1)S(1)} %get-tuple-element.18.w_gate, bf16[128,32,128]{2,1,0:T(8,128)(2,1)S(1)} %left.1, bf16[128,32,128]{2,1,0:T(8,128)(2,1)S(1)} %right.1, ...), custom_call_target="tpu_custom_call" | custom-call | flops 268435456 | bytes 4194304 | tf_op jit(solution)/shard_map/own_tri/pallas_call | solution.py:187
  81.0 2.8 %collective-permute-done.8 = bf16[32,32,128]{2,1,0:T(8,128)(2,1)S(1)} collective-permute-done((bf16[32,32,128]{2,1,0:T(8,128)(2,1)S(1)}, bf16[32,32,128]{2,1,0:T(8,128)(2,1)S(1)}, u32[]{:S(2)}, u32[]{:S(2)}) %collective-permute-start.8) | collective-permute-done | bytes 262176 | tf_op jit(solution)/shard_map/ppermute | solution.py:318
  83.9 0.8 fusion
  (13 shorter events, 0.1 us)
Async XLA Ops:
  0.0 15.4 %copy-start = (bf16[32,64,128]{2,1,0:T(8,128)(2,1)S(1)}, bf16[32,64,128]{2,1,0:T(8,128)(2,1)}, u32[]{:S(2)}) copy-start(bf16[32,64,128]{2,1,0:T(8,128)(2,1)} %x.3) | copy-start | bytes 1572868
  1.4 17.9 %collective-permute-start.1 = (bf16[528,128]{1,0:T(8,128)(2,1)S(1)}, bf16[528,128]{1,0:T(8,128)(2,1)S(1)}, u32[]{:S(2)}, u32[]{:S(2)}) collective-permute-start(bf16[528,128]{1,0:T(8,128)(2,1)S(1)} %get-tuple-element.19), channel_id=1, source_target_pairs={{0,0},{34,34},{68,68},{102,102},{136,136},{170,170},{204,204},{238... | collective-permute-start | bytes 405512 | tf_op jit(solution)/shard_map/ppermute | solution.py:289
  2.1 17.2 %collective-permute-start.2 = (bf16[528,128]{1,0:T(8,128)(2,1)S(1)}, bf16[528,128]{1,0:T(8,128)(2,1)S(1)}, u32[]{:S(2)}, u32[]{:S(2)}) collective-permute-start(bf16[528,128]{1,0:T(8,128)(2,1)S(1)} %get-tuple-element.20), channel_id=1, source_target_pairs={{0,448},{34,482},{68,4},{102,38},{136,72},{170,106},{204,140},{238... | collective-permute-start | bytes 405512 | tf_op jit(solution)/shard_map/ppermute | solution.py:289
  12.8 6.5 %collective-permute-start.3 = (bf16[528,128]{1,0:T(8,128)(2,1)S(1)}, bf16[528,128]{1,0:T(8,128)(2,1)S(1)}, u32[]{:S(2)}, u32[]{:S(2)}) collective-permute-start(bf16[528,128]{1,0:T(8,128)(2,1)S(1)} %get-tuple-element.21), channel_id=1, source_target_pairs={{0,64},{34,98},{68,132},{102,166},{136,200},{170,234},{204,268},{2... | collective-permute-start | bytes 405512 | tf_op jit(solution)/shard_map/ppermute | solution.py:289
  14.1 5.2 %collective-permute-start.4 = (bf16[528,128]{1,0:T(8,128)(2,1)S(1)}, bf16[528,128]{1,0:T(8,128)(2,1)S(1)}, u32[]{:S(2)}, u32[]{:S(2)}) collective-permute-start(bf16[528,128]{1,0:T(8,128)(2,1)S(1)} %get-tuple-element.22), channel_id=1, source_target_pairs={{0,128},{34,162},{68,196},{102,230},{136,264},{170,298},{204,332},... | collective-permute-start | bytes 405512 | tf_op jit(solution)/shard_map/ppermute | solution.py:289
  15.4 10.1 %collective-permute-start = (bf16[2048,128]{1,0:T(8,128)(2,1)S(1)}, bf16[2048,128]{1,0:T(8,128)(2,1)S(1)}, u32[]{:S(2)}, u32[]{:S(2)}) collective-permute-start(bf16[2048,128]{1,0:T(8,128)(2,1)S(1)} %bitcast.8), channel_id=1, source_target_pairs={{0,30},{2,0},{4,2},{6,4},{8,6},{10,8},{12,10},{14,12},{16,14},{18,... | collective-permute-start | bytes 1572872 | tf_op jit(solution)/shard_map/ppermute | solution.py:292
  18.4 0.7 copy-start.1
  18.4 0.7 slice-start
  19.3 10.9 %collective-permute-start.5 = (bf16[272,128]{1,0:T(8,128)(2,1)S(1)}, bf16[272,128]{1,0:T(8,128)(2,1)S(1)}, u32[]{:S(2)}, u32[]{:S(2)}) collective-permute-start(bf16[272,128]{1,0:T(8,128)(2,1)S(1)} %slice_add_fusion), channel_id=1, source_target_pairs={{0,384},{448,320},{64,192},{128,256},{416,480},{352,288},{32,160},... | collective-permute-start | bytes 208904 | tf_op jit(solution)/shard_map/ppermute | solution.py:300
  27.8 46.6 %collective-permute-start.7 = (bf16[128,32,128]{2,1,0:T(8,128)(2,1)S(1)}, bf16[128,32,128]{2,1,0:T(8,128)(2,1)S(1)}, u32[]{:S(2)}, u32[]{:S(2)}) collective-permute-start(bf16[128,32,128]{2,1,0:T(8,128)(2,1)S(1)} %left.1), channel_id=1, source_target_pairs={{0,1},{1,0},{2,3},{3,2},{4,5},{5,4},{6,7},{7,6},{8,9},{9,8},{10,11... | collective-permute-start | bytes 3145736 | tf_op jit(solution)/shard_map/ppermute | solution.py:310
  30.5 42.2 %collective-permute-start.6 = (bf16[16,128]{1,0:T(8,128)(2,1)S(1)}, bf16[16,128]{1,0:T(8,128)(2,1)S(1)}, u32[]{:S(2)}, u32[]{:S(2)}) collective-permute-start(bf16[16,128]{1,0:T(8,128)(2,1)S(1)} %get-tuple-element.26.rest), channel_id=1, source_target_pairs={{0,32},{32,0},{64,96},{96,64},{128,160},{160,128},{192,224},{224,1... | collective-permute-start | bytes 12296 | tf_op jit(solution)/shard_map/ppermute | solution.py:313
  75.6 8.3 %collective-permute-start.8 = (bf16[32,32,128]{2,1,0:T(8,128)(2,1)S(1)}, bf16[32,32,128]{2,1,0:T(8,128)(2,1)S(1)}, u32[]{:S(2)}, u32[]{:S(2)}) collective-permute-start(bf16[32,32,128]{2,1,0:T(8,128)(2,1)S(1)} %theirs.1), channel_id=1, source_target_pairs={{0,1},{1,0},{2,3},{3,2},{4,5},{5,4},{6,7},{7,6},{8,9},{9,8},{10,11... | collective-permute-start | bytes 786440 | tf_op jit(solution)/shard_map/ppermute | solution.py:318

commit v10 on v9

--- a/solution.py
+++ b/solution.py
@@ -278,8 +278,8 @@
     swap = [(p, 1 - p) for p in range(reps)]
     flat = pair_rep.reshape(-1, chans)
 
-    near = ((0, -2, 2, 4), (-3, -5, 1, 3))
-    far = ((-4, -6, 6, 8), (-1, -7, 5, 7))
+    near = ((0, 2, 4, -2), (1, 3, -3, -5))
+    far = ((-4, 6, 8, -6), (5, 7, -1, -7))
     messages = first_call(flat, 8)
     chunk_rows = flat.shape[0] // 8
     got = []

time: 85 us -> 83.8 us (0.986)
  blocking collectives: 40.3 us -> 39.4 us
    ppermute x1, waiting for transfers between devices: 1.37 us -> 0.01 us  [per_device(): lax.ppermute(flat, 'col', [(c, (c - 1) % cols) for c in range(cols)])]
    ppermute x4, starting transfers between devices: 14 us -> 12.7 us  [per_device(): got.append(lax.ppermute(message, ('row', 'col'), pairs))]
    ppermute x4, waiting for transfers between devices: 0.01 us -> 0.97 us  [per_device(): got.append(lax.ppermute(message, ('row', 'col'), pairs))]
    ppermute x1, starting transfers between devices: 2.36 us -> 3.25 us  [per_device(): other = lax.ppermute(left, 'rep', swap)]
    all_gather x1, blocking collectives: 40.3 us -> 39.4 us  [per_device(): gathered = lax.all_gather(chunk, 'row', axis=0, tiled=False)]
  transfers between devices with their start and end apart: 9 -> 9, of which waited for: 2 -> 2; matrix products, arithmetic and copies ran while one was open for 0% -> 0% of each run, Pallas kernels for 9% -> 10%
where the time goes in v10:
time: 83.8 us; the launch traced here: 83.3 us
  blocking collectives  39.4 us (47%)
  starting transfers between devices  27.2 us (32%)
  Pallas kernels  10.7 us (13%)
  waiting for transfers between devices  4.12 us (5%)
  other arithmetic  0.94 us (1%)
    all_gather x1, blocking collectives, per_device(): gathered = lax.all_gather(chunk, 'row', axis=0, tiled=False)  39.4 us
    ppermute x4, starting transfers between devices, per_device(): got.append(lax.ppermute(message, ('row', 'col'), pairs))  12.7 us
    ppermute x1, starting transfers between devices, per_device(): passed = lax.ppermute(onward, ('row', 'col'), pairs)  5.15 us
    ppermute x1, starting transfers between devices, per_device(): other = lax.ppermute(left, 'rep', swap)  3.25 us
    ppermute x1, waiting for transfers between devices, per_device(): received = lax.ppermute(theirs, 'rep', swap)  3.15 us
    pallas_call x1, Pallas kernels, own_call(): pl.pallas_call(own_kernel, out_shape=(jax.ShapeDtypeStruct((half, tile, c...  2.87 us
    pallas_call x1, Pallas kernels, left_call(): pl.pallas_call(left_kernel, out_shape=jax.ShapeDtypeStruct((hid, half, 2...  2.25 us
    ppermute x1, starting transfers between devices, per_device(): received = lax.ppermute(theirs, 'rep', swap)  2.24 us
  transfers between devices with their start and end apart: 9, of which 2 were waited for; matrix products, arithmetic and copies ran while one was open for 0% of the time, Pallas kernels for 10%

profile of v10, /device:TPU:8, one launch (start us, length us, event | category | flops | bytes accessed | tf_op | source)
XLA Modules:
  0.0 83.3 jit_solution(2412085574158629198)
XLA Ops:
  0.0 1.4 %first.1 = (bf16[528,128]{1,0:T(8,128)(2,1)S(1)}, bf16[528,128]{1,0:T(8,128)(2,1)S(1)}, bf16[528,128]{1,0:T(8,128)(2,1)S(1)}, bf16[528,128]{1,0:T(8,128)(2,1)S(1)}) custom-call(bf16[2048,128]{1,0:T(8,128)(2,1)} %bitcast.7), custom_call_target="tpu_custom_call" | custom-call | bytes 2097152 | tf_op jit(solution)/shard_map/first/pallas_call | solution.py:230
  1.4 0.7 collective-permute-start.1
  2.1 4.0 %collective-permute-start.2 = (bf16[528,128]{1,0:T(8,128)(2,1)S(1)}, bf16[528,128]{1,0:T(8,128)(2,1)S(1)}, u32[]{:S(2)}, u32[]{:S(2)}) collective-permute-start(bf16[528,128]{1,0:T(8,128)(2,1)S(1)} %get-tuple-element.20), channel_id=1, source_target_pairs={{0,64},{34,98},{68,132},{102,166},{136,200},{170,234},{204,268},{2... | collective-permute-start | bytes 405512 | tf_op jit(solution)/shard_map/ppermute | solution.py:289
  6.1 4.6 %collective-permute-start.3 = (bf16[528,128]{1,0:T(8,128)(2,1)S(1)}, bf16[528,128]{1,0:T(8,128)(2,1)S(1)}, u32[]{:S(2)}, u32[]{:S(2)}) collective-permute-start(bf16[528,128]{1,0:T(8,128)(2,1)S(1)} %get-tuple-element.21), channel_id=1, source_target_pairs={{0,128},{34,162},{68,196},{102,230},{136,264},{170,298},{204,332},... | collective-permute-start | bytes 405512 | tf_op jit(solution)/shard_map/ppermute | solution.py:289
  10.7 3.4 %collective-permute-start.4 = (bf16[528,128]{1,0:T(8,128)(2,1)S(1)}, bf16[528,128]{1,0:T(8,128)(2,1)S(1)}, u32[]{:S(2)}, u32[]{:S(2)}) collective-permute-start(bf16[528,128]{1,0:T(8,128)(2,1)S(1)} %get-tuple-element.22), channel_id=1, source_target_pairs={{0,448},{34,482},{68,4},{102,38},{136,72},{170,106},{204,140},{238... | collective-permute-start | bytes 405512 | tf_op jit(solution)/shard_map/ppermute | solution.py:289
  14.2 1.9 %collective-permute-start = (bf16[2048,128]{1,0:T(8,128)(2,1)S(1)}, bf16[2048,128]{1,0:T(8,128)(2,1)S(1)}, u32[]{:S(2)}, u32[]{:S(2)}) collective-permute-start(bf16[2048,128]{1,0:T(8,128)(2,1)S(1)} %bitcast.8), channel_id=1, source_target_pairs={{0,30},{2,0},{4,2},{6,4},{8,6},{10,8},{12,10},{14,12},{16,14},{18,... | collective-permute-start | bytes 1572872 | tf_op jit(solution)/shard_map/ppermute | solution.py:292
  16.1 1.0 %weights.1 = (bf16[256,128]{1,0:T(8,128)(2,1)S(1)}, bf16[256,128]{1,0:T(8,128)(2,1)S(1)}, bf16[128,128]{1,0:T(8,128)(2,1)S(1)}, bf16[128,128]{1,0:T(8,128)(2,1)S(1)}) custom-call(bf16[128,128]{1,0:T(8,128)(2,1)} %refs_0_.1, bf16[128,128]{1,0:T(8,128)(2,1)} %refs_1_.1, bf16[128,128]{1,0:T(8,128)(2,1)} %refs_2_.1, bf16[128,128]{1,0:T(8,128)(2,1)} %refs_3_.1, ...), custom_call_target="tpu_custom_call" | custom-call | flops 10000000000 | bytes 1048576 | tf_op jit(solution)/shard_map/weights/pallas_call | solution.py:262
  17.1 0.7 copy-done.1
  17.8 0.1 convert_bitcast_fusion.mask_k
  17.9 0.1 fusion.2
  18.0 1.0 %collective-permute-done.4.refs_3_ = bf16[528,128]{1,0:T(8,128)(2,1)S(1)} collective-permute-done((bf16[528,128]{1,0:T(8,128)(2,1)S(1)}, bf16[528,128]{1,0:T(8,128)(2,1)S(1)}, u32[]{:S(2)}, u32[]{:S(2)}) %collective-permute-start.4) | collective-permute-done | bytes 135200 | tf_op jit(solution)/shard_map/ppermute | solution.py:289
  19.0 5.1 %collective-permute-start.5 = (bf16[272,128]{1,0:T(8,128)(2,1)S(1)}, bf16[272,128]{1,0:T(8,128)(2,1)S(1)}, u32[]{:S(2)}, u32[]{:S(2)}) collective-permute-start(bf16[272,128]{1,0:T(8,128)(2,1)S(1)} %slice_add_fusion), channel_id=1, source_target_pairs={{0,384},{64,192},{128,256},{448,320},{32,160},{96,224},{416,480},{... | collective-permute-start | bytes 208904 | tf_op jit(solution)/shard_map/ppermute | solution.py:300
  24.1 2.3 %left.1 = bf16[128,32,128]{2,1,0:T(8,128)(2,1)S(1)} custom-call(s32[32]{0:T(128)S(1)} %get-tuple-element.32.flags, bf16[32,64,128]{2,1,0:T(8,128)(2,1)S(1)} %copy-done, bf16[32,64,128]{2,1,0:T(8,128)(2,1)S(1)} %bitcast.10, f32[1,128]{1,0:T(1,128)S(1)} %convert_bitcast_fusion.mask_k, bf16[256,128]{1,0:T(8,128)(2,1)S(1)} %get-tuple-element.24.weights), custom_call_target="tpu_custom_call" | custom-call | flops 671088640 | bytes 2097152 | tf_op jit(solution)/shard_map/left/pallas_call | solution.py:60
  26.4 3.2 %collective-permute-start.7 = (bf16[128,32,128]{2,1,0:T(8,128)(2,1)S(1)}, bf16[128,32,128]{2,1,0:T(8,128)(2,1)S(1)}, u32[]{:S(2)}, u32[]{:S(2)}) collective-permute-start(bf16[128,32,128]{2,1,0:T(8,128)(2,1)S(1)} %left.1), channel_id=1, source_target_pairs={{0,1},{1,0},{2,3},{3,2},{4,5},{5,4},{6,7},{7,6},{8,9},{9,8},{10,11... | collective-permute-start | bytes 3145736 | tf_op jit(solution)/shard_map/ppermute | solution.py:310
  29.7 0.1 pad_add_fusion.place
  29.7 0.3 chunk.1
  30.1 1.9 %collective-permute-start.6 = (bf16[16,128]{1,0:T(8,128)(2,1)S(1)}, bf16[16,128]{1,0:T(8,128)(2,1)S(1)}, u32[]{:S(2)}, u32[]{:S(2)}) collective-permute-start(bf16[16,128]{1,0:T(8,128)(2,1)S(1)} %get-tuple-element.26.rest), channel_id=1, source_target_pairs={{0,32},{32,0},{64,96},{96,64},{128,160},{160,128},{192,224},{224,1... | collective-permute-start | bytes 12296 | tf_op jit(solution)/shard_map/ppermute | solution.py:313
  32.0 39.4 %all-gather.1.gathered = bf16[16,255,128]{2,1,0:T(8,128)(2,1)S(1)} all-gather(bf16[1,255,128]{2,1,0:T(8,128)(2,1)S(1)} %bitcast.9), channel_id=2, replica_groups=mesh['row'=16,'col'=16,'rep'=2] {'row'}, dimensions={0}, use_global_device_ids=true | all-gather | bytes 1109760 | tf_op jit(solution)/shard_map/all_gather | solution.py:314
  71.4 1.6 %right.1 = bf16[128,32,128]{2,1,0:T(8,128)(2,1)S(1)} custom-call(s32[2]{0:T(128)S(1)} %pad_add_fusion.place, s32[32]{0:T(128)S(1)} %get-tuple-element.31.flags, bf16[16,255,128]{2,1,0:T(8,128)(2,1)S(1)} %all-gather.1.gathered, bf16[16,128]{1,0:T(8,128)(2,1)S(1)} %get-tuple-element.26.rest, bf16[16,128]{1,0:T(8,128)(2,1)S(1)} %collective-permute-done.6.rest_other, ...), custom_call_target="tpu_custom_call" | custom-call | flops 5000000000 | bytes 4194304 | tf_op jit(solution)/shard_map/right/pallas_call | solution.py:135
  73.0 1.3 %theirs.1 = bf16[32,32,128]{2,1,0:T(8,128)(2,1)S(1)} custom-call(bf16[128,32,128]{2,1,0:T(8,128)(2,1)S(1)} %collective-permute-done.7.left, bf16[128,32,128]{2,1,0:T(8,128)(2,1)S(1)} %right.1, bf16[128,128]{1,0:T(8,128)(2,1)S(1)} %get-tuple-element.28.w_out), custom_call_target="tpu_custom_call" | custom-call | flops 134217728 | bytes 2097152 | tf_op jit(solution)/shard_map/theirs/pallas_call | solution.py:157
  74.3 2.2 %collective-permute-start.8 = (bf16[32,32,128]{2,1,0:T(8,128)(2,1)S(1)}, bf16[32,32,128]{2,1,0:T(8,128)(2,1)S(1)}, u32[]{:S(2)}, u32[]{:S(2)}) collective-permute-start(bf16[32,32,128]{2,1,0:T(8,128)(2,1)S(1)} %theirs.1), channel_id=1, source_target_pairs={{0,1},{1,0},{2,3},{3,2},{4,5},{5,4},{6,7},{7,6},{8,9},{9,8},{10,11... | collective-permute-start | bytes 786440 | tf_op jit(solution)/shard_map/ppermute | solution.py:318
  76.6 2.9 %own_tri.1 = (bf16[32,64,128]{2,1,0:T(8,128)(2,1)}, f32[32,32,128]{2,1,0:T(8,128)S(1)}) custom-call(bf16[32,64,128]{2,1,0:T(8,128)(2,1)S(1)} %copy-done, bf16[128,128]{1,0:T(8,128)(2,1)S(1)} %get-tuple-element.18.w_gate, bf16[128,32,128]{2,1,0:T(8,128)(2,1)S(1)} %left.1, bf16[128,32,128]{2,1,0:T(8,128)(2,1)S(1)} %right.1, ...), custom_call_target="tpu_custom_call" | custom-call | flops 268435456 | bytes 4194304 | tf_op jit(solution)/shard_map/own_tri/pallas_call | solution.py:187
  79.4 3.1 %collective-permute-done.8 = bf16[32,32,128]{2,1,0:T(8,128)(2,1)S(1)} collective-permute-done((bf16[32,32,128]{2,1,0:T(8,128)(2,1)S(1)}, bf16[32,32,128]{2,1,0:T(8,128)(2,1)S(1)}, u32[]{:S(2)}, u32[]{:S(2)}) %collective-permute-start.8) | collective-permute-done | bytes 262176 | tf_op jit(solution)/shard_map/ppermute | solution.py:318
  82.6 0.8 fusion
  (13 shorter events, 0.1 us)
Async XLA Ops:
  0.0 14.1 %copy-start = (bf16[32,64,128]{2,1,0:T(8,128)(2,1)S(1)}, bf16[32,64,128]{2,1,0:T(8,128)(2,1)}, u32[]{:S(2)}) copy-start(bf16[32,64,128]{2,1,0:T(8,128)(2,1)} %x.3) | copy-start | bytes 1572868
  1.4 16.6 %collective-permute-start.1 = (bf16[528,128]{1,0:T(8,128)(2,1)S(1)}, bf16[528,128]{1,0:T(8,128)(2,1)S(1)}, u32[]{:S(2)}, u32[]{:S(2)}) collective-permute-start(bf16[528,128]{1,0:T(8,128)(2,1)S(1)} %get-tuple-element.19), channel_id=1, source_target_pairs={{0,0},{34,34},{68,68},{102,102},{136,136},{170,170},{204,204},{238... | collective-permute-start | bytes 405512 | tf_op jit(solution)/shard_map/ppermute | solution.py:289
  2.1 15.9 %collective-permute-start.2 = (bf16[528,128]{1,0:T(8,128)(2,1)S(1)}, bf16[528,128]{1,0:T(8,128)(2,1)S(1)}, u32[]{:S(2)}, u32[]{:S(2)}) collective-permute-start(bf16[528,128]{1,0:T(8,128)(2,1)S(1)} %get-tuple-element.20), channel_id=1, source_target_pairs={{0,64},{34,98},{68,132},{102,166},{136,200},{170,234},{204,268},{2... | collective-permute-start | bytes 405512 | tf_op jit(solution)/shard_map/ppermute | solution.py:289
  6.1 11.9 %collective-permute-start.3 = (bf16[528,128]{1,0:T(8,128)(2,1)S(1)}, bf16[528,128]{1,0:T(8,128)(2,1)S(1)}, u32[]{:S(2)}, u32[]{:S(2)}) collective-permute-start(bf16[528,128]{1,0:T(8,128)(2,1)S(1)} %get-tuple-element.21), channel_id=1, source_target_pairs={{0,128},{34,162},{68,196},{102,230},{136,264},{170,298},{204,332},... | collective-permute-start | bytes 405512 | tf_op jit(solution)/shard_map/ppermute | solution.py:289
  10.7 8.2 %collective-permute-start.4 = (bf16[528,128]{1,0:T(8,128)(2,1)S(1)}, bf16[528,128]{1,0:T(8,128)(2,1)S(1)}, u32[]{:S(2)}, u32[]{:S(2)}) collective-permute-start(bf16[528,128]{1,0:T(8,128)(2,1)S(1)} %get-tuple-element.22), channel_id=1, source_target_pairs={{0,448},{34,482},{68,4},{102,38},{136,72},{170,106},{204,140},{238... | collective-permute-start | bytes 405512 | tf_op jit(solution)/shard_map/ppermute | solution.py:289
  14.2 10.0 %collective-permute-start = (bf16[2048,128]{1,0:T(8,128)(2,1)S(1)}, bf16[2048,128]{1,0:T(8,128)(2,1)S(1)}, u32[]{:S(2)}, u32[]{:S(2)}) collective-permute-start(bf16[2048,128]{1,0:T(8,128)(2,1)S(1)} %bitcast.8), channel_id=1, source_target_pairs={{0,30},{2,0},{4,2},{6,4},{8,6},{10,8},{12,10},{14,12},{16,14},{18,... | collective-permute-start | bytes 1572872 | tf_op jit(solution)/shard_map/ppermute | solution.py:292
  17.1 0.7 copy-start.1
  17.1 0.7 slice-start
  19.0 10.8 %collective-permute-start.5 = (bf16[272,128]{1,0:T(8,128)(2,1)S(1)}, bf16[272,128]{1,0:T(8,128)(2,1)S(1)}, u32[]{:S(2)}, u32[]{:S(2)}) collective-permute-start(bf16[272,128]{1,0:T(8,128)(2,1)S(1)} %slice_add_fusion), channel_id=1, source_target_pairs={{0,384},{64,192},{128,256},{448,320},{32,160},{96,224},{416,480},{... | collective-permute-start | bytes 208904 | tf_op jit(solution)/shard_map/ppermute | solution.py:300
  26.4 46.6 %collective-permute-start.7 = (bf16[128,32,128]{2,1,0:T(8,128)(2,1)S(1)}, bf16[128,32,128]{2,1,0:T(8,128)(2,1)S(1)}, u32[]{:S(2)}, u32[]{:S(2)}) collective-permute-start(bf16[128,32,128]{2,1,0:T(8,128)(2,1)S(1)} %left.1), channel_id=1, source_target_pairs={{0,1},{1,0},{2,3},{3,2},{4,5},{5,4},{6,7},{7,6},{8,9},{9,8},{10,11... | collective-permute-start | bytes 3145736 | tf_op jit(solution)/shard_map/ppermute | solution.py:310
  30.1 41.3 %collective-permute-start.6 = (bf16[16,128]{1,0:T(8,128)(2,1)S(1)}, bf16[16,128]{1,0:T(8,128)(2,1)S(1)}, u32[]{:S(2)}, u32[]{:S(2)}) collective-permute-start(bf16[16,128]{1,0:T(8,128)(2,1)S(1)} %get-tuple-element.26.rest), channel_id=1, source_target_pairs={{0,32},{32,0},{64,96},{96,64},{128,160},{160,128},{192,224},{224,1... | collective-permute-start | bytes 12296 | tf_op jit(solution)/shard_map/ppermute | solution.py:313
  74.3 8.3 %collective-permute-start.8 = (bf16[32,32,128]{2,1,0:T(8,128)(2,1)S(1)}, bf16[32,32,128]{2,1,0:T(8,128)(2,1)S(1)}, u32[]{:S(2)}, u32[]{:S(2)}) collective-permute-start(bf16[32,32,128]{2,1,0:T(8,128)(2,1)S(1)} %theirs.1), channel_id=1, source_target_pairs={{0,1},{1,0},{2,3},{3,2},{4,5},{5,4},{6,7},{7,6},{8,9},{9,8},{10,11... | collective-permute-start | bytes 786440 | tf_op jit(solution)/shard_map/ppermute | solution.py:318

commit v11 on v10

--- a/solution.py
+++ b/solution.py
@@ -22,16 +22,21 @@
     return lax.dot_general(a, b, (dims, ((), ())), preferred_element_type=F32)
 
 
-def normalise(block):
+def normalise(block, exact=True):
     chans = block.shape[1]
     ones = jnp.ones((chans, chans), BF16)
     centred = block.astype(F32) - dot(block, ones, ((1,), (0,))) * (1.0 / chans)
-    var = dot((centred * centred).astype(BF16), ones, ((1,), (0,))) * (1.0 / chans)
+    squares = centred * centred
+    high = squares.astype(BF16)
+    total = dot(high, ones, ((1,), (0,)))
+    if exact:
+        total = total + dot((squares - high.astype(F32)).astype(BF16), ones, ((1,), (0,)))
+    var = total * (1.0 / chans)
     return (centred * lax.rsqrt(var + EPS)).astype(BF16)
 
 
-def halved_transpose(w):
-    return (w[...].astype(F32).T * 0.5).astype(BF16)
+def transposed(w):
+    return w[...].astype(F32).T.astype(BF16)
 
 
 def gated(weights, normed, masks):
@@ -41,8 +46,7 @@
     parts = []
     for n, mask in enumerate(masks):
         at = slice(n * width, (n + 1) * width)
-        value = both[:hid, at] * mask
-        parts.append(value + value * jnp.tanh(both[hid:, at]))
+        parts.append(both[:hid, at] * mask * jax.nn.sigmoid(both[hid:, at]))
     return jnp.concatenate(parts, axis=1).reshape(hid, len(masks), width).astype(BF16)
 
 
@@ -51,7 +55,7 @@
     for q in range(0, half, GROUP):
         blocks = [part[i] for i in range(q, q + GROUP) for part in (x, x_next)]
         masks = [mask_k[...] * flags[i].astype(F32) for i in range(q, q + GROUP)]
-        out[:, q : q + GROUP, :] = gated(weights[...], normalise(jnp.concatenate(blocks)), masks)
+        out[:, q : q + GROUP, :] = gated(weights[...], normalise(jnp.concatenate(blocks), exact=False), masks)
 
 
 def left_call(flags, x, x_next, mask_k, weights):
@@ -251,8 +255,8 @@
         copy.wait()
     hid = held.shape[2]
     for i, wt in enumerate((wt_left, wt_right)):
-        wt[:hid] = halved_transpose(held.at[2 * i])
-        wt[hid:] = halved_transpose(held.at[2 * i + 1])
+        wt[:hid] = transposed(held.at[2 * i])
+        wt[hid:] = transposed(held.at[2 * i + 1])
 
 
 def weights_call(*ws):
@@ -278,8 +282,8 @@
     swap = [(p, 1 - p) for p in range(reps)]
     flat = pair_rep.reshape(-1, chans)
 
-    near = ((0, 2, 4, -2), (1, 3, -3, -5))
-    far = ((-4, 6, 8, -6), (5, 7, -1, -7))
+    near = ((0, 2, -2, 4), (1, 3, -3, -5))
+    far = ((-4, 6, -6, 8), (5, 7, -1, -7))
     messages = first_call(flat, 8)
     chunk_rows = flat.shape[0] // 8
     got = []

time: 83.8 us -> 83.8 us (level)
  waiting for transfers between devices: 4.12 us -> 2.44 us
  starting transfers between devices: 27.2 us -> 28.5 us
    ppermute x4, waiting for transfers between devices: 0.97 us -> 0.01 us  [per_device(): got.append(lax.ppermute(message, ('row', 'col'), pairs))]
  transfers between devices with their start and end apart: 9 -> 9, of which waited for: 2 -> 1; matrix products, arithmetic and copies ran while one was open for 0% -> 0% of each run, Pallas kernels for 10% -> 10%
where the time goes in v11:
time: 83.8 us; the launch traced here: 83.4 us
  blocking collectives  39.4 us (47%)
  starting transfers between devices  28.5 us (34%)
  Pallas kernels  11.1 us (13%)
  waiting for transfers between devices  2.44 us (3%)
  other arithmetic  0.94 us (1%)
    all_gather x1, blocking collectives, per_device(): gathered = lax.all_gather(chunk, 'row', axis=0, tiled=False)  39.4 us
    ppermute x4, starting transfers between devices, per_device(): got.append(lax.ppermute(message, ('row', 'col'), pairs))  13.4 us
    ppermute x1, starting transfers between devices, per_device(): passed = lax.ppermute(onward, ('row', 'col'), pairs)  5.47 us
    ppermute x1, starting transfers between devices, per_device(): other = lax.ppermute(left, 'rep', swap)  3.26 us
    pallas_call x1, Pallas kernels, own_call(): pl.pallas_call(own_kernel, out_shape=(jax.ShapeDtypeStruct((half, tile, c...  3.24 us
    ppermute x1, starting transfers between devices, per_device(): received = lax.ppermute(theirs, 'rep', swap)  2.59 us
    ppermute x1, waiting for transfers between devices, per_device(): received = lax.ppermute(theirs, 'rep', swap)  2.42 us
    pallas_call x1, Pallas kernels, left_call(): pl.pallas_call(left_kernel, out_shape=jax.ShapeDtypeStruct((hid, half, 2...  2.23 us
  transfers between devices with their start and end apart: 9, of which 1 were waited for; matrix products, arithmetic and copies ran while one was open for 0% of the time, Pallas kernels for 10%

profile of v11, /device:TPU:8, one launch (start us, length us, event | category | flops | bytes accessed | tf_op | source)
XLA Modules:
  0.0 83.4 jit_solution(7896668615475615410)
XLA Ops:
  0.0 1.4 %first.1 = (bf16[528,128]{1,0:T(8,128)(2,1)S(1)}, bf16[528,128]{1,0:T(8,128)(2,1)S(1)}, bf16[528,128]{1,0:T(8,128)(2,1)S(1)}, bf16[528,128]{1,0:T(8,128)(2,1)S(1)}) custom-call(bf16[2048,128]{1,0:T(8,128)(2,1)} %bitcast.7), custom_call_target="tpu_custom_call" | custom-call | bytes 2097152 | tf_op jit(solution)/shard_map/first/pallas_call | solution.py:234
  1.4 0.7 collective-permute-start.1
  2.1 4.0 %collective-permute-start.2 = (bf16[528,128]{1,0:T(8,128)(2,1)S(1)}, bf16[528,128]{1,0:T(8,128)(2,1)S(1)}, u32[]{:S(2)}, u32[]{:S(2)}) collective-permute-start(bf16[528,128]{1,0:T(8,128)(2,1)S(1)} %get-tuple-element.20), channel_id=1, source_target_pairs={{0,64},{34,98},{68,132},{102,166},{136,200},{170,234},{204,268},{2... | collective-permute-start | bytes 405512 | tf_op jit(solution)/shard_map/ppermute | solution.py:293
  6.1 7.3 %collective-permute-start.3 = (bf16[528,128]{1,0:T(8,128)(2,1)S(1)}, bf16[528,128]{1,0:T(8,128)(2,1)S(1)}, u32[]{:S(2)}, u32[]{:S(2)}) collective-permute-start(bf16[528,128]{1,0:T(8,128)(2,1)S(1)} %get-tuple-element.21), channel_id=1, source_target_pairs={{0,448},{34,482},{68,4},{102,38},{136,72},{170,106},{204,140},{238... | collective-permute-start | bytes 405512 | tf_op jit(solution)/shard_map/ppermute | solution.py:293
  13.5 1.3 %collective-permute-start.4 = (bf16[528,128]{1,0:T(8,128)(2,1)S(1)}, bf16[528,128]{1,0:T(8,128)(2,1)S(1)}, u32[]{:S(2)}, u32[]{:S(2)}) collective-permute-start(bf16[528,128]{1,0:T(8,128)(2,1)S(1)} %get-tuple-element.22), channel_id=1, source_target_pairs={{0,128},{34,162},{68,196},{102,230},{136,264},{170,298},{204,332},... | collective-permute-start | bytes 405512 | tf_op jit(solution)/shard_map/ppermute | solution.py:293
  14.8 1.9 %collective-permute-start = (bf16[2048,128]{1,0:T(8,128)(2,1)S(1)}, bf16[2048,128]{1,0:T(8,128)(2,1)S(1)}, u32[]{:S(2)}, u32[]{:S(2)}) collective-permute-start(bf16[2048,128]{1,0:T(8,128)(2,1)S(1)} %bitcast.8), channel_id=1, source_target_pairs={{0,30},{2,0},{4,2},{6,4},{8,6},{10,8},{12,10},{14,12},{16,14},{18,... | collective-permute-start | bytes 1572872 | tf_op jit(solution)/shard_map/ppermute | solution.py:296
  16.7 1.0 %weights.1 = (bf16[256,128]{1,0:T(8,128)(2,1)S(1)}, bf16[256,128]{1,0:T(8,128)(2,1)S(1)}, bf16[128,128]{1,0:T(8,128)(2,1)S(1)}, bf16[128,128]{1,0:T(8,128)(2,1)S(1)}) custom-call(bf16[128,128]{1,0:T(8,128)(2,1)} %refs_0_.1, bf16[128,128]{1,0:T(8,128)(2,1)} %refs_1_.1, bf16[128,128]{1,0:T(8,128)(2,1)} %refs_2_.1, bf16[128,128]{1,0:T(8,128)(2,1)} %refs_3_.1, ...), custom_call_target="tpu_custom_call" | custom-call | flops 10000000000 | bytes 1048576 | tf_op jit(solution)/shard_map/weights/pallas_call | solution.py:266
  17.7 0.7 copy-done.1
  18.4 0.0 slice-done
  18.5 0.1 convert_bitcast_fusion.mask_k
  18.5 0.1 fusion.2
  18.7 5.5 %collective-permute-start.5 = (bf16[272,128]{1,0:T(8,128)(2,1)S(1)}, bf16[272,128]{1,0:T(8,128)(2,1)S(1)}, u32[]{:S(2)}, u32[]{:S(2)}) collective-permute-start(bf16[272,128]{1,0:T(8,128)(2,1)S(1)} %slice_add_fusion), channel_id=1, source_target_pairs={{0,384},{64,192},{448,320},{128,256},{32,160},{96,224},{416,480},{... | collective-permute-start | bytes 208904 | tf_op jit(solution)/shard_map/ppermute | solution.py:304
  24.1 2.2 %left.1 = bf16[128,32,128]{2,1,0:T(8,128)(2,1)S(1)} custom-call(s32[32]{0:T(128)S(1)} %get-tuple-element.32.flags, bf16[32,64,128]{2,1,0:T(8,128)(2,1)S(1)} %copy-done, bf16[32,64,128]{2,1,0:T(8,128)(2,1)S(1)} %bitcast.10, f32[1,128]{1,0:T(1,128)S(1)} %convert_bitcast_fusion.mask_k, bf16[256,128]{1,0:T(8,128)(2,1)S(1)} %get-tuple-element.24.weights), custom_call_target="tpu_custom_call" | custom-call | flops 671088640 | bytes 2097152 | tf_op jit(solution)/shard_map/left/pallas_call | solution.py:64
  26.4 3.3 %collective-permute-start.7 = (bf16[128,32,128]{2,1,0:T(8,128)(2,1)S(1)}, bf16[128,32,128]{2,1,0:T(8,128)(2,1)S(1)}, u32[]{:S(2)}, u32[]{:S(2)}) collective-permute-start(bf16[128,32,128]{2,1,0:T(8,128)(2,1)S(1)} %left.1), channel_id=1, source_target_pairs={{0,1},{1,0},{2,3},{3,2},{4,5},{5,4},{6,7},{7,6},{8,9},{9,8},{10,11... | collective-permute-start | bytes 3145736 | tf_op jit(solution)/shard_map/ppermute | solution.py:314
  29.7 0.1 pad_add_fusion.place
  29.7 0.4 chunk.1
  30.2 1.9 %collective-permute-start.6 = (bf16[16,128]{1,0:T(8,128)(2,1)S(1)}, bf16[16,128]{1,0:T(8,128)(2,1)S(1)}, u32[]{:S(2)}, u32[]{:S(2)}) collective-permute-start(bf16[16,128]{1,0:T(8,128)(2,1)S(1)} %get-tuple-element.26.rest), channel_id=1, source_target_pairs={{0,32},{32,0},{64,96},{96,64},{128,160},{160,128},{192,224},{224,1... | collective-permute-start | bytes 12296 | tf_op jit(solution)/shard_map/ppermute | solution.py:317
  32.1 39.4 %all-gather.1.gathered = bf16[16,255,128]{2,1,0:T(8,128)(2,1)S(1)} all-gather(bf16[1,255,128]{2,1,0:T(8,128)(2,1)S(1)} %bitcast.9), channel_id=2, replica_groups=mesh['row'=16,'col'=16,'rep'=2] {'row'}, dimensions={0}, use_global_device_ids=true | all-gather | bytes 1109760 | tf_op jit(solution)/shard_map/all_gather | solution.py:318
  71.5 1.6 %right.1 = bf16[128,32,128]{2,1,0:T(8,128)(2,1)S(1)} custom-call(s32[2]{0:T(128)S(1)} %pad_add_fusion.place, s32[32]{0:T(128)S(1)} %get-tuple-element.31.flags, bf16[16,255,128]{2,1,0:T(8,128)(2,1)S(1)} %all-gather.1.gathered, bf16[16,128]{1,0:T(8,128)(2,1)S(1)} %get-tuple-element.26.rest, bf16[16,128]{1,0:T(8,128)(2,1)S(1)} %collective-permute-done.6.rest_other, ...), custom_call_target="tpu_custom_call" | custom-call | flops 5000000000 | bytes 4194304 | tf_op jit(solution)/shard_map/right/pallas_call | solution.py:139
  73.1 1.3 %theirs.1 = bf16[32,32,128]{2,1,0:T(8,128)(2,1)S(1)} custom-call(bf16[128,32,128]{2,1,0:T(8,128)(2,1)S(1)} %collective-permute-done.7.left, bf16[128,32,128]{2,1,0:T(8,128)(2,1)S(1)} %right.1, bf16[128,128]{1,0:T(8,128)(2,1)S(1)} %get-tuple-element.28.w_out), custom_call_target="tpu_custom_call" | custom-call | flops 134217728 | bytes 2097152 | tf_op jit(solution)/shard_map/theirs/pallas_call | solution.py:161
  74.4 2.6 %collective-permute-start.8 = (bf16[32,32,128]{2,1,0:T(8,128)(2,1)S(1)}, bf16[32,32,128]{2,1,0:T(8,128)(2,1)S(1)}, u32[]{:S(2)}, u32[]{:S(2)}) collective-permute-start(bf16[32,32,128]{2,1,0:T(8,128)(2,1)S(1)} %theirs.1), channel_id=1, source_target_pairs={{0,1},{1,0},{2,3},{3,2},{4,5},{5,4},{6,7},{7,6},{8,9},{9,8},{10,11... | collective-permute-start | bytes 786440 | tf_op jit(solution)/shard_map/ppermute | solution.py:322
  77.0 3.2 %own_tri.1 = (bf16[32,64,128]{2,1,0:T(8,128)(2,1)}, f32[32,32,128]{2,1,0:T(8,128)S(1)}) custom-call(bf16[32,64,128]{2,1,0:T(8,128)(2,1)S(1)} %copy-done, bf16[128,128]{1,0:T(8,128)(2,1)S(1)} %get-tuple-element.18.w_gate, bf16[128,32,128]{2,1,0:T(8,128)(2,1)S(1)} %left.1, bf16[128,32,128]{2,1,0:T(8,128)(2,1)S(1)} %right.1, ...), custom_call_target="tpu_custom_call" | custom-call | flops 268435456 | bytes 4194304 | tf_op jit(solution)/shard_map/own_tri/pallas_call | solution.py:191
  80.2 2.4 %collective-permute-done.8 = bf16[32,32,128]{2,1,0:T(8,128)(2,1)S(1)} collective-permute-done((bf16[32,32,128]{2,1,0:T(8,128)(2,1)S(1)}, bf16[32,32,128]{2,1,0:T(8,128)(2,1)S(1)}, u32[]{:S(2)}, u32[]{:S(2)}) %collective-permute-start.8) | collective-permute-done | bytes 262176 | tf_op jit(solution)/shard_map/ppermute | solution.py:322
  82.6 0.8 fusion
  (13 shorter events, 0.1 us)
Async XLA Ops:
  0.0 14.8 %copy-start = (bf16[32,64,128]{2,1,0:T(8,128)(2,1)S(1)}, bf16[32,64,128]{2,1,0:T(8,128)(2,1)}, u32[]{:S(2)}) copy-start(bf16[32,64,128]{2,1,0:T(8,128)(2,1)} %x.3) | copy-start | bytes 1572868
  1.4 17.2 %collective-permute-start.1 = (bf16[528,128]{1,0:T(8,128)(2,1)S(1)}, bf16[528,128]{1,0:T(8,128)(2,1)S(1)}, u32[]{:S(2)}, u32[]{:S(2)}) collective-permute-start(bf16[528,128]{1,0:T(8,128)(2,1)S(1)} %get-tuple-element.19), channel_id=1, source_target_pairs={{0,0},{34,34},{68,68},{102,102},{136,136},{170,170},{204,204},{238... | collective-permute-start | bytes 405512 | tf_op jit(solution)/shard_map/ppermute | solution.py:293
  2.1 16.6 %collective-permute-start.2 = (bf16[528,128]{1,0:T(8,128)(2,1)S(1)}, bf16[528,128]{1,0:T(8,128)(2,1)S(1)}, u32[]{:S(2)}, u32[]{:S(2)}) collective-permute-start(bf16[528,128]{1,0:T(8,128)(2,1)S(1)} %get-tuple-element.20), channel_id=1, source_target_pairs={{0,64},{34,98},{68,132},{102,166},{136,200},{170,234},{204,268},{2... | collective-permute-start | bytes 405512 | tf_op jit(solution)/shard_map/ppermute | solution.py:293
  6.1 12.5 %collective-permute-start.3 = (bf16[528,128]{1,0:T(8,128)(2,1)S(1)}, bf16[528,128]{1,0:T(8,128)(2,1)S(1)}, u32[]{:S(2)}, u32[]{:S(2)}) collective-permute-start(bf16[528,128]{1,0:T(8,128)(2,1)S(1)} %get-tuple-element.21), channel_id=1, source_target_pairs={{0,448},{34,482},{68,4},{102,38},{136,72},{170,106},{204,140},{238... | collective-permute-start | bytes 405512 | tf_op jit(solution)/shard_map/ppermute | solution.py:293
  13.5 5.2 %collective-permute-start.4 = (bf16[528,128]{1,0:T(8,128)(2,1)S(1)}, bf16[528,128]{1,0:T(8,128)(2,1)S(1)}, u32[]{:S(2)}, u32[]{:S(2)}) collective-permute-start(bf16[528,128]{1,0:T(8,128)(2,1)S(1)} %get-tuple-element.22), channel_id=1, source_target_pairs={{0,128},{34,162},{68,196},{102,230},{136,264},{170,298},{204,332},... | collective-permute-start | bytes 405512 | tf_op jit(solution)/shard_map/ppermute | solution.py:293
  14.8 9.4 %collective-permute-start = (bf16[2048,128]{1,0:T(8,128)(2,1)S(1)}, bf16[2048,128]{1,0:T(8,128)(2,1)S(1)}, u32[]{:S(2)}, u32[]{:S(2)}) collective-permute-start(bf16[2048,128]{1,0:T(8,128)(2,1)S(1)} %bitcast.8), channel_id=1, source_target_pairs={{0,30},{2,0},{4,2},{6,4},{8,6},{10,8},{12,10},{14,12},{16,14},{18,... | collective-permute-start | bytes 1572872 | tf_op jit(solution)/shard_map/ppermute | solution.py:296
  17.7 0.7 copy-start.1
  17.7 0.7 slice-start
  18.7 11.1 %collective-permute-start.5 = (bf16[272,128]{1,0:T(8,128)(2,1)S(1)}, bf16[272,128]{1,0:T(8,128)(2,1)S(1)}, u32[]{:S(2)}, u32[]{:S(2)}) collective-permute-start(bf16[272,128]{1,0:T(8,128)(2,1)S(1)} %slice_add_fusion), channel_id=1, source_target_pairs={{0,384},{64,192},{448,320},{128,256},{32,160},{96,224},{416,480},{... | collective-permute-start | bytes 208904 | tf_op jit(solution)/shard_map/ppermute | solution.py:304
  26.4 46.7 %collective-permute-start.7 = (bf16[128,32,128]{2,1,0:T(8,128)(2,1)S(1)}, bf16[128,32,128]{2,1,0:T(8,128)(2,1)S(1)}, u32[]{:S(2)}, u32[]{:S(2)}) collective-permute-start(bf16[128,32,128]{2,1,0:T(8,128)(2,1)S(1)} %left.1), channel_id=1, source_target_pairs={{0,1},{1,0},{2,3},{3,2},{4,5},{5,4},{6,7},{7,6},{8,9},{9,8},{10,11... | collective-permute-start | bytes 3145736 | tf_op jit(solution)/shard_map/ppermute | solution.py:314
  30.2 41.4 %collective-permute-start.6 = (bf16[16,128]{1,0:T(8,128)(2,1)S(1)}, bf16[16,128]{1,0:T(8,128)(2,1)S(1)}, u32[]{:S(2)}, u32[]{:S(2)}) collective-permute-start(bf16[16,128]{1,0:T(8,128)(2,1)S(1)} %get-tuple-element.26.rest), channel_id=1, source_target_pairs={{0,32},{32,0},{64,96},{96,64},{128,160},{160,128},{192,224},{224,1... | collective-permute-start | bytes 12296 | tf_op jit(solution)/shard_map/ppermute | solution.py:317
  74.4 8.3 %collective-permute-start.8 = (bf16[32,32,128]{2,1,0:T(8,128)(2,1)S(1)}, bf16[32,32,128]{2,1,0:T(8,128)(2,1)S(1)}, u32[]{:S(2)}, u32[]{:S(2)}) collective-permute-start(bf16[32,32,128]{2,1,0:T(8,128)(2,1)S(1)} %theirs.1), channel_id=1, source_target_pairs={{0,1},{1,0},{2,3},{3,2},{4,5},{5,4},{6,7},{7,6},{8,9},{9,8},{10,11... | collective-permute-start | bytes 786440 | tf_op jit(solution)/shard_map/ppermute | solution.py:322

commit v12 on v11

--- a/solution.py
+++ b/solution.py
@@ -295,6 +295,7 @@
     flat, messages = lax.optimization_barrier((flat, messages))
     x_next = lax.ppermute(flat, "col", [(c, (c - 1) % cols) for c in range(cols)])
     onward = sum((g[chunk_rows:] for g in got[1:]), got[0][chunk_rows:])
+    token_mask, onward = lax.optimization_barrier((token_mask, onward))
     pairs = [
         ((c + n) % rows * cols + c, (c + f) % rows * cols + c)
         for c in range(cols)

time: 83.8 us -> 83.9 us (level)
  transfers between devices with their start and end apart: 9 -> 9, of which waited for: 1 -> 2; matrix products, arithmetic and copies ran while one was open for 0% -> 0% of each run, Pallas kernels for 10% -> 10%
where the time goes in v12:
time: 83.9 us; the launch traced here: 83.5 us
  blocking collectives  40.2 us (48%)
  starting transfers between devices  28 us (33%)
  Pallas kernels  11.1 us (13%)
  waiting for transfers between devices  2.99 us (4%)
  other arithmetic  0.95 us (1%)
    all_gather x1, blocking collectives, per_device(): gathered = lax.all_gather(chunk, 'row', axis=0, tiled=False)  40.2 us
    ppermute x4, starting transfers between devices, per_device(): got.append(lax.ppermute(message, ('row', 'col'), pairs))  13.4 us
    ppermute x1, starting transfers between devices, per_device(): passed = lax.ppermute(onward, ('row', 'col'), pairs)  5.07 us
    ppermute x1, starting transfers between devices, per_device(): other = lax.ppermute(left, 'rep', swap)  3.26 us
    pallas_call x1, Pallas kernels, own_call(): pl.pallas_call(own_kernel, out_shape=(jax.ShapeDtypeStruct((half, tile, c...  3.24 us
    ppermute x1, waiting for transfers between devices, per_device(): received = lax.ppermute(theirs, 'rep', swap)  2.56 us
    ppermute x1, starting transfers between devices, per_device(): received = lax.ppermute(theirs, 'rep', swap)  2.46 us
    pallas_call x1, Pallas kernels, left_call(): pl.pallas_call(left_kernel, out_shape=jax.ShapeDtypeStruct((hid, half, 2...  2.24 us
  transfers between devices with their start and end apart: 9, of which 2 were waited for; matrix products, arithmetic and copies ran while one was open for 0% of the time, Pallas kernels for 10%

profile of v12, /device:TPU:8, one launch (start us, length us, event | category | flops | bytes accessed | tf_op | source)
XLA Modules:
  0.0 83.5 jit_solution(14663978467811783078)
XLA Ops:
  0.0 1.4 %first.1 = (bf16[528,128]{1,0:T(8,128)(2,1)S(1)}, bf16[528,128]{1,0:T(8,128)(2,1)S(1)}, bf16[528,128]{1,0:T(8,128)(2,1)S(1)}, bf16[528,128]{1,0:T(8,128)(2,1)S(1)}) custom-call(bf16[2048,128]{1,0:T(8,128)(2,1)} %bitcast.7), custom_call_target="tpu_custom_call" | custom-call | bytes 2097152 | tf_op jit(solution)/shard_map/first/pallas_call | solution.py:234
  1.4 0.7 collective-permute-start
  2.1 4.0 %collective-permute-start.1 = (bf16[528,128]{1,0:T(8,128)(2,1)S(1)}, bf16[528,128]{1,0:T(8,128)(2,1)S(1)}, u32[]{:S(2)}, u32[]{:S(2)}) collective-permute-start(bf16[528,128]{1,0:T(8,128)(2,1)S(1)} %get-tuple-element.22), channel_id=1, source_target_pairs={{0,64},{34,98},{68,132},{102,166},{136,200},{170,234},{204,268},{2... | collective-permute-start | bytes 405512 | tf_op jit(solution)/shard_map/ppermute | solution.py:293
  6.1 7.3 %collective-permute-start.2 = (bf16[528,128]{1,0:T(8,128)(2,1)S(1)}, bf16[528,128]{1,0:T(8,128)(2,1)S(1)}, u32[]{:S(2)}, u32[]{:S(2)}) collective-permute-start(bf16[528,128]{1,0:T(8,128)(2,1)S(1)} %get-tuple-element.23), channel_id=1, source_target_pairs={{0,448},{34,482},{68,4},{102,38},{136,72},{170,106},{204,140},{238... | collective-permute-start | bytes 405512 | tf_op jit(solution)/shard_map/ppermute | solution.py:293
  13.5 1.3 %collective-permute-start.3 = (bf16[528,128]{1,0:T(8,128)(2,1)S(1)}, bf16[528,128]{1,0:T(8,128)(2,1)S(1)}, u32[]{:S(2)}, u32[]{:S(2)}) collective-permute-start(bf16[528,128]{1,0:T(8,128)(2,1)S(1)} %get-tuple-element.24), channel_id=1, source_target_pairs={{0,128},{34,162},{68,196},{102,230},{136,264},{170,298},{204,332},... | collective-permute-start | bytes 405512 | tf_op jit(solution)/shard_map/ppermute | solution.py:293
  14.8 1.9 %collective-permute-start.4 = (bf16[2048,128]{1,0:T(8,128)(2,1)S(1)}, bf16[2048,128]{1,0:T(8,128)(2,1)S(1)}, u32[]{:S(2)}, u32[]{:S(2)}) collective-permute-start(bf16[2048,128]{1,0:T(8,128)(2,1)S(1)} %bitcast.8), channel_id=1, source_target_pairs={{0,30},{2,0},{4,2},{6,4},{8,6},{10,8},{12,10},{14,12},{16,14},{18,... | collective-permute-start | bytes 1572872 | tf_op jit(solution)/shard_map/ppermute | solution.py:296
  16.7 1.0 %weights.1 = (bf16[256,128]{1,0:T(8,128)(2,1)S(1)}, bf16[256,128]{1,0:T(8,128)(2,1)S(1)}, bf16[128,128]{1,0:T(8,128)(2,1)S(1)}, bf16[128,128]{1,0:T(8,128)(2,1)S(1)}) custom-call(bf16[128,128]{1,0:T(8,128)(2,1)} %refs_0_.1, bf16[128,128]{1,0:T(8,128)(2,1)} %refs_1_.1, bf16[128,128]{1,0:T(8,128)(2,1)} %refs_2_.1, bf16[128,128]{1,0:T(8,128)(2,1)} %refs_3_.1, ...), custom_call_target="tpu_custom_call" | custom-call | flops 10000000000 | bytes 1048576 | tf_op jit(solution)/shard_map/weights/pallas_call | solution.py:266
  17.7 0.0 copy-start.1
  17.8 0.4 collective-permute-done.2.refs_2_
  18.2 5.1 %collective-permute-start.5 = (bf16[272,128]{1,0:T(8,128)(2,1)S(1)}, bf16[272,128]{1,0:T(8,128)(2,1)S(1)}, u32[]{:S(2)}, u32[]{:S(2)}) collective-permute-start(bf16[272,128]{1,0:T(8,128)(2,1)S(1)} %slice_add_fusion), channel_id=1, source_target_pairs={{0,384},{64,192},{448,320},{128,256},{32,160},{96,224},{416,480},{... | collective-permute-start | bytes 208904 | tf_op jit(solution)/shard_map/ppermute | solution.py:305
  23.3 0.1 convert_bitcast_fusion.mask_k
  23.4 0.1 fusion.2
  23.5 2.2 %left.1 = bf16[128,32,128]{2,1,0:T(8,128)(2,1)S(1)} custom-call(s32[32]{0:T(128)S(1)} %get-tuple-element.36.flags, bf16[32,64,128]{2,1,0:T(8,128)(2,1)S(1)} %copy-done, bf16[32,64,128]{2,1,0:T(8,128)(2,1)S(1)} %bitcast.10, f32[1,128]{1,0:T(1,128)S(1)} %convert_bitcast_fusion.mask_k, bf16[256,128]{1,0:T(8,128)(2,1)S(1)} %get-tuple-element.27.weights), custom_call_target="tpu_custom_call" | custom-call | flops 671088640 | bytes 2097152 | tf_op jit(solution)/shard_map/left/pallas_call | solution.py:64
  25.7 3.3 %collective-permute-start.7 = (bf16[128,32,128]{2,1,0:T(8,128)(2,1)S(1)}, bf16[128,32,128]{2,1,0:T(8,128)(2,1)S(1)}, u32[]{:S(2)}, u32[]{:S(2)}) collective-permute-start(bf16[128,32,128]{2,1,0:T(8,128)(2,1)S(1)} %left.1), channel_id=1, source_target_pairs={{0,1},{1,0},{2,3},{3,2},{4,5},{5,4},{6,7},{7,6},{8,9},{9,8},{10,11... | collective-permute-start | bytes 3145736 | tf_op jit(solution)/shard_map/ppermute | solution.py:315
  29.0 0.1 pad_add_fusion.place
  29.1 0.4 chunk.1
  29.5 1.9 %collective-permute-start.6 = (bf16[16,128]{1,0:T(8,128)(2,1)S(1)}, bf16[16,128]{1,0:T(8,128)(2,1)S(1)}, u32[]{:S(2)}, u32[]{:S(2)}) collective-permute-start(bf16[16,128]{1,0:T(8,128)(2,1)S(1)} %get-tuple-element.30.rest), channel_id=1, source_target_pairs={{0,32},{32,0},{64,96},{96,64},{128,160},{160,128},{192,224},{224,1... | collective-permute-start | bytes 12296 | tf_op jit(solution)/shard_map/ppermute | solution.py:318
  31.4 40.2 %all-gather.1.gathered = bf16[16,255,128]{2,1,0:T(8,128)(2,1)S(1)} all-gather(bf16[1,255,128]{2,1,0:T(8,128)(2,1)S(1)} %bitcast.9), channel_id=2, replica_groups=mesh['row'=16,'col'=16,'rep'=2] {'row'}, dimensions={0}, use_global_device_ids=true | all-gather | bytes 1109760 | tf_op jit(solution)/shard_map/all_gather | solution.py:319
  71.6 1.6 %right.1 = bf16[128,32,128]{2,1,0:T(8,128)(2,1)S(1)} custom-call(s32[2]{0:T(128)S(1)} %pad_add_fusion.place, s32[32]{0:T(128)S(1)} %get-tuple-element.35.flags, bf16[16,255,128]{2,1,0:T(8,128)(2,1)S(1)} %all-gather.1.gathered, bf16[16,128]{1,0:T(8,128)(2,1)S(1)} %get-tuple-element.30.rest, bf16[16,128]{1,0:T(8,128)(2,1)S(1)} %collective-permute-done.6.rest_other, ...), custom_call_target="tpu_custom_call" | custom-call | flops 5000000000 | bytes 4194304 | tf_op jit(solution)/shard_map/right/pallas_call | solution.py:139
  73.2 1.3 %theirs.1 = bf16[32,32,128]{2,1,0:T(8,128)(2,1)S(1)} custom-call(bf16[128,32,128]{2,1,0:T(8,128)(2,1)S(1)} %collective-permute-done.7.left, bf16[128,32,128]{2,1,0:T(8,128)(2,1)S(1)} %right.1, bf16[128,128]{1,0:T(8,128)(2,1)S(1)} %get-tuple-element.32.w_out), custom_call_target="tpu_custom_call" | custom-call | flops 134217728 | bytes 2097152 | tf_op jit(solution)/shard_map/theirs/pallas_call | solution.py:161
  74.5 2.5 %collective-permute-start.8 = (bf16[32,32,128]{2,1,0:T(8,128)(2,1)S(1)}, bf16[32,32,128]{2,1,0:T(8,128)(2,1)S(1)}, u32[]{:S(2)}, u32[]{:S(2)}) collective-permute-start(bf16[32,32,128]{2,1,0:T(8,128)(2,1)S(1)} %theirs.1), channel_id=1, source_target_pairs={{0,1},{1,0},{2,3},{3,2},{4,5},{5,4},{6,7},{7,6},{8,9},{9,8},{10,11... | collective-permute-start | bytes 786440 | tf_op jit(solution)/shard_map/ppermute | solution.py:323
  76.9 3.2 %own_tri.1 = (bf16[32,64,128]{2,1,0:T(8,128)(2,1)}, f32[32,32,128]{2,1,0:T(8,128)S(1)}) custom-call(bf16[32,64,128]{2,1,0:T(8,128)(2,1)S(1)} %copy-done, bf16[128,128]{1,0:T(8,128)(2,1)S(1)} %get-tuple-element.20.w_gate, bf16[128,32,128]{2,1,0:T(8,128)(2,1)S(1)} %left.1, bf16[128,32,128]{2,1,0:T(8,128)(2,1)S(1)} %right.1, ...), custom_call_target="tpu_custom_call" | custom-call | flops 268435456 | bytes 4194304 | tf_op jit(solution)/shard_map/own_tri/pallas_call | solution.py:191
  80.2 2.6 %collective-permute-done.8 = bf16[32,32,128]{2,1,0:T(8,128)(2,1)S(1)} collective-permute-done((bf16[32,32,128]{2,1,0:T(8,128)(2,1)S(1)}, bf16[32,32,128]{2,1,0:T(8,128)(2,1)S(1)}, u32[]{:S(2)}, u32[]{:S(2)}) %collective-permute-start.8) | collective-permute-done | bytes 262176 | tf_op jit(solution)/shard_map/ppermute | solution.py:323
  82.7 0.8 fusion
  (13 shorter events, 0.1 us)
Async XLA Ops:
  0.0 14.8 %copy-start = (bf16[32,64,128]{2,1,0:T(8,128)(2,1)S(1)}, bf16[32,64,128]{2,1,0:T(8,128)(2,1)}, u32[]{:S(2)}) copy-start(bf16[32,64,128]{2,1,0:T(8,128)(2,1)} %x.3) | copy-start | bytes 1572868
  1.4 16.4 %collective-permute-start = (bf16[528,128]{1,0:T(8,128)(2,1)S(1)}, bf16[528,128]{1,0:T(8,128)(2,1)S(1)}, u32[]{:S(2)}, u32[]{:S(2)}) collective-permute-start(bf16[528,128]{1,0:T(8,128)(2,1)S(1)} %get-tuple-element.21), channel_id=1, source_target_pairs={{0,0},{34,34},{68,68},{102,102},{136,136},{170,170},{204,204},{238... | collective-permute-start | bytes 405512 | tf_op jit(solution)/shard_map/ppermute | solution.py:293
  2.1 15.7 %collective-permute-start.1 = (bf16[528,128]{1,0:T(8,128)(2,1)S(1)}, bf16[528,128]{1,0:T(8,128)(2,1)S(1)}, u32[]{:S(2)}, u32[]{:S(2)}) collective-permute-start(bf16[528,128]{1,0:T(8,128)(2,1)S(1)} %get-tuple-element.22), channel_id=1, source_target_pairs={{0,64},{34,98},{68,132},{102,166},{136,200},{170,234},{204,268},{2... | collective-permute-start | bytes 405512 | tf_op jit(solution)/shard_map/ppermute | solution.py:293
  6.1 12.1 %collective-permute-start.2 = (bf16[528,128]{1,0:T(8,128)(2,1)S(1)}, bf16[528,128]{1,0:T(8,128)(2,1)S(1)}, u32[]{:S(2)}, u32[]{:S(2)}) collective-permute-start(bf16[528,128]{1,0:T(8,128)(2,1)S(1)} %get-tuple-element.23), channel_id=1, source_target_pairs={{0,448},{34,482},{68,4},{102,38},{136,72},{170,106},{204,140},{238... | collective-permute-start | bytes 405512 | tf_op jit(solution)/shard_map/ppermute | solution.py:293
  13.5 4.7 %collective-permute-start.3 = (bf16[528,128]{1,0:T(8,128)(2,1)S(1)}, bf16[528,128]{1,0:T(8,128)(2,1)S(1)}, u32[]{:S(2)}, u32[]{:S(2)}) collective-permute-start(bf16[528,128]{1,0:T(8,128)(2,1)S(1)} %get-tuple-element.24), channel_id=1, source_target_pairs={{0,128},{34,162},{68,196},{102,230},{136,264},{170,298},{204,332},... | collective-permute-start | bytes 405512 | tf_op jit(solution)/shard_map/ppermute | solution.py:293
  14.8 8.7 %collective-permute-start.4 = (bf16[2048,128]{1,0:T(8,128)(2,1)S(1)}, bf16[2048,128]{1,0:T(8,128)(2,1)S(1)}, u32[]{:S(2)}, u32[]{:S(2)}) collective-permute-start(bf16[2048,128]{1,0:T(8,128)(2,1)S(1)} %bitcast.8), channel_id=1, source_target_pairs={{0,30},{2,0},{4,2},{6,4},{8,6},{10,8},{12,10},{14,12},{16,14},{18,... | collective-permute-start | bytes 1572872 | tf_op jit(solution)/shard_map/ppermute | solution.py:296
  17.7 5.6 %copy-start.1 = (s32[1024]{0:T(1024)S(1)}, s32[1024]{0:T(1024)}, u32[]{:S(2)}) copy-start(s32[1024]{0:T(1024)} %param.9) | copy-start | bytes 12292
  18.2 5.1 %slice-start = ((s32[1024]{0:T(1024)}), s32[64]{0:T(128)S(1)}, s32[]{:S(2)}) async-start(s32[1024]{0:T(1024)} %param.9), calls=%async_computation | async-start | bytes 1024 | tf_op jit(solution)/shard_map/slice | solution.py:309
  18.2 10.9 %collective-permute-start.5 = (bf16[272,128]{1,0:T(8,128)(2,1)S(1)}, bf16[272,128]{1,0:T(8,128)(2,1)S(1)}, u32[]{:S(2)}, u32[]{:S(2)}) collective-permute-start(bf16[272,128]{1,0:T(8,128)(2,1)S(1)} %slice_add_fusion), channel_id=1, source_target_pairs={{0,384},{64,192},{448,320},{128,256},{32,160},{96,224},{416,480},{... | collective-permute-start | bytes 208904 | tf_op jit(solution)/shard_map/ppermute | solution.py:305
  25.7 47.5 %collective-permute-start.7 = (bf16[128,32,128]{2,1,0:T(8,128)(2,1)S(1)}, bf16[128,32,128]{2,1,0:T(8,128)(2,1)S(1)}, u32[]{:S(2)}, u32[]{:S(2)}) collective-permute-start(bf16[128,32,128]{2,1,0:T(8,128)(2,1)S(1)} %left.1), channel_id=1, source_target_pairs={{0,1},{1,0},{2,3},{3,2},{4,5},{5,4},{6,7},{7,6},{8,9},{9,8},{10,11... | collective-permute-start | bytes 3145736 | tf_op jit(solution)/shard_map/ppermute | solution.py:315
  29.5 42.1 %collective-permute-start.6 = (bf16[16,128]{1,0:T(8,128)(2,1)S(1)}, bf16[16,128]{1,0:T(8,128)(2,1)S(1)}, u32[]{:S(2)}, u32[]{:S(2)}) collective-permute-start(bf16[16,128]{1,0:T(8,128)(2,1)S(1)} %get-tuple-element.30.rest), channel_id=1, source_target_pairs={{0,32},{32,0},{64,96},{96,64},{128,160},{160,128},{192,224},{224,1... | collective-permute-start | bytes 12296 | tf_op jit(solution)/shard_map/ppermute | solution.py:318
  74.5 8.3 %collective-permute-start.8 = (bf16[32,32,128]{2,1,0:T(8,128)(2,1)S(1)}, bf16[32,32,128]{2,1,0:T(8,128)(2,1)S(1)}, u32[]{:S(2)}, u32[]{:S(2)}) collective-permute-start(bf16[32,32,128]{2,1,0:T(8,128)(2,1)S(1)} %theirs.1), channel_id=1, source_target_pairs={{0,1},{1,0},{2,3},{3,2},{4,5},{5,4},{6,7},{7,6},{8,9},{9,8},{10,11... | collective-permute-start | bytes 786440 | tf_op jit(solution)/shard_map/ppermute | solution.py:323
